TPU v7x, 256 devices: a whole 4x4x8 slice. The times are simulated.
256 devices in a mesh: dp: 32 (over z, y), slab: 8 (over x, core).
Axes of the slice: x: 4, y: 4, z: 8, core: 2. Of those that a mesh axis runs over, the one named last changes fastest.
Arguments:
- volume: bfloat16 [256, 16, 8, 128], P('dp', 'slab'), may hold values from -13 to 13, as said below
- flux_target: bfloat16 [256, 3, 8, 4, 64], P('dp', None, 'slab'), may hold values from -6 to 6
- tensor_target: bfloat16 [256, 6], P('dp'), may hold values from -6 to 6
- dest: int32 [256], P('dp'), may hold values from -1 to 255, as said below
- first_weight: bfloat16 [16, 1, 3, 3, 3], replicated, may hold values from -1.25 to 1.25
- first_bias: float32 [16], replicated, may hold values from -3 to 3
- second_weight: bfloat16 [32, 16, 3, 3, 3], replicated, may hold values from -0.3125 to 0.3125
- second_bias: float32 [32], replicated, may hold values from -3 to 3
- short_weight: bfloat16 [32, 16], replicated, may hold values from -1.5 to 1.5
- flux_weight: bfloat16 [3, 32], replicated, may hold values from -1 to 1
- flux_bias: float32 [3], replicated, may hold values from -3 to 3
- tensor_weight: bfloat16 [6, 32], replicated, may hold values from -1 to 1
- tensor_bias: float32 [6], replicated, may hold values from -3 to 3
Outputs:
- flux_pred: bfloat16 [256, 3, 8, 4, 64], P('dp', None, 'slab')
- tensor_pred: bfloat16 [256, 6], P('dp')
- grad_first: float32 [16, 1, 3, 3, 3], replicated
- grad_first_bias: float32 [16], replicated
- grad_second: float32 [32, 16, 3, 3, 3], replicated
- grad_second_bias: float32 [32], replicated
- grad_short: float32 [32, 16], replicated
- grad_flux: float32 [3, 32], replicated
- grad_flux_bias: float32 [3], replicated
- grad_tensor: float32 [6, 32], replicated
- grad_tensor_bias: float32 [6], replicated
Inputs may be any that keep to these rules, and one draw needn't show every extreme that they name: `volume`: values are drawn independently per record and z plane; records are fully formed in every slot. `dest`: each entry is -1 (an empty archive slot) or g * 8 + s, sending that record to slot s of trainer group g; no trainer slot is named twice. At most 2 records of one owner go to one trainer group, and some owner sends exactly 2 to some group; some trainer group has all 8 slots filled.
All inputs are finite; a program needn't handle non-finite values.
Results may differ from a plain program's by a relative error of at most 0.0043.
The roundings to bfloat16 on the way count: a program that leaves them out, or rounds other values in their place, can miss the bound.
Values may be sent and summed in bfloat16 or wider, within the bound.
No kernel may reach another device: no remote copies, remote signals or barrier semaphores. Data moves between devices by JAX's collectives and lax.ppermute only.
A program may use at most 128 MiB of HBM per device.

v0:
```python
import jax
import jax.numpy as jnp
from jax import lax
from jax.sharding import PartitionSpec as P


def padded_2(cells, sides, width):
    for axis, dim in sides:
        count = lax.axis_size(axis)
        ends = count - 1
        head = lax.slice_in_dim(cells, 0, width, axis=dim)
        tail = lax.slice_in_dim(cells, cells.shape[dim] - width, cells.shape[dim], axis=dim)
        cells = jnp.concatenate(
            [
                lax.ppermute(tail, axis, [(i, (i + 1) % count) for i in range(ends)]),
                cells,
                lax.ppermute(head, axis, [((i + 1) % count, i) for i in range(ends)]),
            ],
            axis=dim,
        )
    return cells


def passed_along(block, axis, distance):
    devices = range(lax.axis_size(axis))
    route = [(i - distance, i) for i in devices if i - distance in devices]
    return lax.ppermute(block, axis, route)


def conv_forward(inputs, kernel, stride, padding):
    return lax.conv_general_dilated(
        inputs,
        kernel,
        (stride, stride, stride),
        padding,
        dimension_numbers=("NCDHW", "OIDHW", "NCDHW"),
        preferred_element_type=jnp.float32,
    )


def kernel_grad(inputs, cotangent, stride, padding):
    pad_spans = []
    for spatial in range(3):
        low_pad = padding[spatial][0]
        pad_spans.append(
            (
                low_pad,
                3
                + stride * (cotangent.shape[2 + spatial] - 1)
                - inputs.shape[2 + spatial]
                - low_pad,
            )
        )
    result = lax.conv_general_dilated(
        inputs,
        cotangent,
        (1, 1, 1),
        pad_spans,
        rhs_dilation=(stride, stride, stride),
        dimension_numbers=("CNDHW", "IODHW", "NCDHW"),
        preferred_element_type=jnp.float32,
    )
    return jnp.transpose(result, (1, 0, 2, 3, 4))


def input_grad(cotangent, kernel, stride, padding, lengths):
    pad_spans = []
    for spatial in range(3):
        low_pad = padding[spatial][0]
        pad_spans.append(
            (
                2 - low_pad,
                lengths[spatial] - 1 - stride * (cotangent.shape[2 + spatial] - 1) + low_pad,
            )
        )
    flipped = kernel[:, :, ::-1, ::-1, ::-1]
    return lax.conv_general_dilated(
        cotangent,
        flipped,
        (1, 1, 1),
        pad_spans,
        lhs_dilation=(stride, stride, stride),
        dimension_numbers=("NCDHW", "IODHW", "NCDHW"),
        preferred_element_type=jnp.float32,
    )


def send_plan(dest, peers, width, slots):
    count = dest.shape[0]
    owners_group = jnp.where(dest >= 0, dest // slots, -1)
    positions = jnp.arange(count)
    earlier = positions[None, :] < positions[:, None]
    same_group = owners_group[None, :] == owners_group[:, None]
    rank_in = jnp.sum(jnp.where(earlier & same_group, 1, 0), axis=1)
    wanted = jnp.arange(peers * width)
    matches = (owners_group[None, :] == (wanted // width)[:, None]) & (
        rank_in[None, :] == (wanted % width)[:, None]
    )
    source_index = jnp.sum(jnp.where(matches, positions[None, :], 0), axis=1)
    filled = jnp.any(matches, axis=1)
    sent_slot = jnp.where(filled, dest[source_index] % slots, -1)
    return (source_index, filled, sent_slot)


def receive_plan(incoming_slot, slots):
    matches = incoming_slot[None, :] == jnp.arange(slots)[:, None]
    positions = jnp.arange(incoming_slot.shape[0])
    source_index = jnp.sum(jnp.where(matches, positions[None, :], 0), axis=1)
    return (source_index, jnp.any(matches, axis=1))


def pick_rows(values, source_index, filled):
    taken = jnp.take(values, source_index, axis=0)
    shape_mask = filled.reshape(filled.shape + (1,) * (values.ndim - 1))
    return jnp.where(shape_mask, taken, jnp.zeros((), values.dtype))


def train(records, flux_goal, tensor_goal, mask, weights, flux_count, tensor_count):
    w_first, b_first, w_second, b_second, w_short, w_flux, b_flux, w_tensor, b_tensor = weights
    slab_count = lax.axis_size("slab")
    pad_first = ((0, 0), (1, 1), (1, 1))
    padded = padded_2(records, (("slab", 1),), 1)
    inputs = padded[:, None]
    z_first = conv_forward(inputs, w_first, 1, pad_first) + b_first[None, :, None, None, None]
    a_first = jnp.maximum(z_first, 0.0).astype(jnp.bfloat16)
    plane_below = passed_along(a_first[:, :, -1:], "slab", 1)
    a_joined = jnp.concatenate([plane_below, a_first], axis=2)
    pad_second = ((0, 0), (1, 0), (1, 0))
    even_cells = a_first[:, :, ::2, ::2, ::2]
    z_second = conv_forward(a_joined, w_second, 2, pad_second) + b_second[None, :, None, None, None]
    z_second = z_second + jnp.einsum(
        "oc,rczyx->rozyx", w_short, even_cells, preferred_element_type=jnp.float32
    )
    a_second = jnp.maximum(z_second, 0.0).astype(jnp.bfloat16)
    flux_full = (
        jnp.einsum("fo,rozyx->rfzyx", w_flux, a_second, preferred_element_type=jnp.float32)
        + b_flux[None, :, None, None, None]
    )
    cell_count = a_second.shape[2] * slab_count * a_second.shape[3] * a_second.shape[4]
    pooled = lax.psum(jnp.sum(a_second, axis=(2, 3, 4), dtype=jnp.float32), "slab") / cell_count
    tensor_full = (
        jnp.dot(pooled, w_tensor.astype(jnp.float32).T, precision=lax.Precision.HIGHEST)
        + b_tensor[None, :]
    )
    weight_mask = mask.astype(jnp.float32)
    flux_out = (flux_full * weight_mask[:, None, None, None, None]).astype(jnp.bfloat16)
    tensor_out = (tensor_full * weight_mask[:, None]).astype(jnp.bfloat16)
    d_flux = (
        2.0
        / flux_count
        * (flux_full - flux_goal.astype(jnp.float32))
        * weight_mask[:, None, None, None, None]
    ).astype(jnp.bfloat16)
    d_tensor = (
        2.0 / tensor_count * (tensor_full - tensor_goal.astype(jnp.float32)) * weight_mask[:, None]
    )
    leading = lax.axis_index("slab") == 0
    g_flux = jnp.einsum("rfzyx,rozyx->fo", d_flux, a_second, preferred_element_type=jnp.float32)
    g_flux_bias = jnp.sum(d_flux, axis=(0, 2, 3, 4), dtype=jnp.float32)
    g_tensor = jnp.where(leading, jnp.dot(d_tensor.T, pooled, precision=lax.Precision.HIGHEST), 0.0)
    g_tensor_bias = jnp.where(leading, jnp.sum(d_tensor, axis=0), 0.0)
    d_pooled = jnp.dot(d_tensor, w_tensor.astype(jnp.float32), precision=lax.Precision.HIGHEST)
    da_second = (
        jnp.einsum("fo,rfzyx->rozyx", w_flux, d_flux, preferred_element_type=jnp.float32)
        + (d_pooled / cell_count)[:, :, None, None, None]
    )
    dz_second = jnp.where(a_second > 0, da_second, 0.0).astype(jnp.bfloat16)
    g_second = kernel_grad(a_joined, dz_second, 2, pad_second)
    g_second_bias = jnp.sum(dz_second, axis=(0, 2, 3, 4), dtype=jnp.float32)
    g_short = jnp.einsum(
        "rozyx,rczyx->oc", dz_second, even_cells, preferred_element_type=jnp.float32
    )
    da_joined = input_grad(dz_second, w_second, 2, pad_second, a_joined.shape[2:])
    from_above = passed_along(da_joined[:, :, :1].astype(jnp.bfloat16), "slab", -1).astype(
        jnp.float32
    )
    da_first = da_joined[:, :, 1:]
    da_first = da_first.at[:, :, -1:].add(from_above)
    shortcut = jnp.einsum("oc,rozyx->rczyx", w_short, dz_second, preferred_element_type=jnp.float32)
    da_first = da_first.at[:, :, ::2, ::2, ::2].add(shortcut)
    dz_first = jnp.where(a_first > 0, da_first, 0.0).astype(jnp.bfloat16)
    g_first = kernel_grad(inputs, dz_first, 1, pad_first)
    g_first_bias = jnp.sum(dz_first, axis=(0, 2, 3, 4), dtype=jnp.float32)
    grads = lax.psum(
        (
            g_first,
            g_first_bias,
            g_second,
            g_second_bias,
            g_short,
            g_flux,
            g_flux_bias,
            g_tensor,
            g_tensor_bias,
        ),
        ("dp", "slab"),
    )
    return (flux_out, tensor_out, grads)


def on_device(
    volume,
    flux_target,
    tensor_target,
    dest,
    first_weight,
    first_bias,
    second_weight,
    second_bias,
    short_weight,
    flux_weight,
    flux_bias,
    tensor_weight,
    tensor_bias,
):
    weights = (
        first_weight,
        first_bias,
        second_weight,
        second_bias,
        short_weight,
        flux_weight,
        flux_bias,
        tensor_weight,
        tensor_bias,
    )
    peers = lax.axis_size("dp")
    slots = dest.shape[0]
    width = max(2, slots // peers)
    cells_half = (
        flux_target.shape[2] * lax.axis_size("slab") * flux_target.shape[3] * flux_target.shape[4]
    )
    flux_count = slots * peers * flux_target.shape[1] * cells_half
    tensor_count = slots * peers * tensor_target.shape[1]
    source_index, filled, sent_slot = send_plan(dest, peers, width, slots)
    shipped = (
        pick_rows(volume, source_index, filled),
        pick_rows(flux_target, source_index, filled),
        pick_rows(tensor_target, source_index, filled),
        sent_slot,
    )
    got_volume, got_flux, got_tensor, got_slot = (
        lax.all_to_all(shipped[0], "dp", split_axis=0, concat_axis=0, tiled=True),
        lax.all_to_all(shipped[1], "dp", split_axis=0, concat_axis=0, tiled=True),
        lax.all_to_all(shipped[2], "dp", split_axis=0, concat_axis=0, tiled=True),
        lax.all_to_all(shipped[3], "dp", split_axis=0, concat_axis=0, tiled=True),
    )
    pick_index, alive = receive_plan(got_slot, slots)
    records = pick_rows(got_volume, pick_index, alive)
    flux_goal = pick_rows(got_flux, pick_index, alive)
    tensor_goal = pick_rows(got_tensor, pick_index, alive)
    flux_pred, tensor_pred, grads = train(
        records, flux_goal, tensor_goal, alive, weights, flux_count, tensor_count
    )
    return (
        flux_pred,
        tensor_pred,
        grads[0],
        grads[1],
        grads[2],
        grads[3],
        grads[4],
        grads[5],
        grads[6],
        grads[7],
        grads[8],
    )


def solution(mesh):
    placed = (
        P("dp", "slab", None, None),
        P("dp", None, "slab", None, None),
        P("dp", None),
        P("dp"),
        P(),
        P(),
        P(),
        P(),
        P(),
        P(),
        P(),
        P(),
        P(),
    )
    return jax.shard_map(
        on_device,
        mesh=mesh,
        in_specs=placed,
        out_specs=(
            P("dp", None, "slab", None, None),
            P("dp", None),
            P(),
            P(),
            P(),
            P(),
            P(),
            P(),
            P(),
            P(),
            P(),
        ),
        check_vma=False,
    )
```

profile of v0, /device:TPU:1, one launch (start us, length us, event | category | flops | bytes accessed | tf_op | source)
XLA Modules:
  0.0 291.1 jit_solution(13452625156906637542)
XLA Ops:
  1.7 1.6 fusion.48
  3.4 5.2 %compare_select_fusion.5 = s32[64]{0:T(128)S(1)} fusion(s32[]{:T(128)} %bitcast.2, s32[]{:T(128)} %bitcast.3, s32[]{:T(128)} %bitcast.4, s32[]{:T(128)} %bitcast.5, s32[]{:T(128)} %bitcast.6, s32[]{:T(128)} %bitcast.7, s32[]{:T(128)} %bitcast.8, s32[]{:T(128)} %bitcast.9, s32[64]{0:T(128)S(1)} %select_reduce_fusion.1), kind=kLoop, calls=%fused_computation.101 | loop fusion | flops 1088 | bytes 544 | tf_op jit(solution)/shard_map/gather | solution.py:101
  9.3 12.0 %all-to-all-start = ((s32[32,2,1]{1,2,0:T(1,128)}), s32[32,2,1]{1,2,0:T(1,128)S(1)}, u32[]{:S(2)}, u32[]{:S(2)}) async-start(s32[32,2,1]{1,2,0:T(1,128)} %bitcast.10), calls=%async_computation | async-start | bytes 32768 | tf_op jit(solution)/shard_map/all_to_all | solution.py:246
  23.0 1.5 gather_fusion.2
  29.9 8.1 %all-to-all-start.3 = ((bf16[32,2,6]{2,1,0:T(2,128)(2,1)}), bf16[32,2,6]{2,1,0:T(2,128)(2,1)S(1)}, u32[]{:S(2)}, u32[]{:S(2)}) async-start(bf16[32,2,6]{2,1,0:T(2,128)(2,1)} %broadcast_select_fusion.1), calls=%async_computation.3 | async-start | bytes 32768 | tf_op jit(solution)/shard_map/all_to_all | solution.py:245
  39.6 7.0 %all-to-all-done.3 = bf16[32,2,6]{2,1,0:T(2,128)(2,1)S(1)} async-done(((bf16[32,2,6]{2,1,0:T(2,128)(2,1)}), bf16[32,2,6]{2,1,0:T(2,128)(2,1)S(1)}, u32[]{:S(2)}, u32[]{:S(2)}) %all-to-all-start.3) | async-done | bytes 800 | tf_op jit(solution)/shard_map/all_to_all | solution.py:245
  46.6 3.9 %all-to-all-start.2 = ((bf16[32,2,768]{2,1,0:T(2,128)(2,1)}), bf16[32,2,768]{2,1,0:T(2,128)(2,1)S(1)}, u32[]{:S(2)}, u32[]{:S(2)}) async-start(bf16[32,2,768]{2,1,0:T(2,128)(2,1)} %reshape.379), calls=%async_computation.2 | async-start | bytes 196608 | tf_op jit(solution)/shard_map/all_to_all | solution.py:244
  50.5 9.1 %all-to-all-done.2 = bf16[32,2,768]{2,1,0:T(2,128)(2,1)S(1)} async-done(((bf16[32,2,768]{2,1,0:T(2,128)(2,1)}), bf16[32,2,768]{2,1,0:T(2,128)(2,1)S(1)}, u32[]{:S(2)}, u32[]{:S(2)}) %all-to-all-start.2) | async-done | bytes 98336 | tf_op jit(solution)/shard_map/all_to_all | solution.py:244
  59.6 3.9 %all-to-all-start.1 = ((bf16[64,2,8,128]{3,2,1,0:T(8,128)(2,1)}), bf16[64,2,8,128]{3,2,1,0:T(8,128)(2,1)S(1)}, u32[]{:S(2)}, u32[]{:S(2)}) async-start(bf16[64,2,8,128]{3,2,1,0:T(8,128)(2,1)} %select_select_fusion), calls=%async_computation.1 | async-start | bytes 524288 | tf_op jit(solution)/shard_map/all_to_all | solution.py:243
  64.8 9.3 %all-to-all-done.1 = bf16[64,2,8,128]{3,2,1,0:T(8,128)(2,1)S(1)} async-done(((bf16[64,2,8,128]{3,2,1,0:T(8,128)(2,1)}), bf16[64,2,8,128]{3,2,1,0:T(8,128)(2,1)S(1)}, u32[]{:S(2)}, u32[]{:S(2)}) %all-to-all-start.1) | async-done | bytes 262176 | tf_op jit(solution)/shard_map/all_to_all | solution.py:243
  74.7 7.9 %collective-permute-start = (bf16[8,1,8,128]{3,2,1,0:T(8,128)(2,1)S(1)}, bf16[8,1,8,128]{3,2,1,0:T(8,128)(2,1)S(1)}, u32[]{:S(2)}, u32[]{:S(2)}) collective-permute-start(bf16[8,1,8,128]{3,2,1,0:T(8,128)(2,1)S(1)} %get-tuple-element.83), channel_id=1, source_target_pairs={{0,1},{1,2},{2,3},{3,4},{4,5},{5,6},{6,7},{8,9},{9,10},{10,11},{11... | collective-permute-start | bytes 49160 | tf_op jit(solution)/shard_map/ppermute | solution.py:15
  82.6 2.2 collective-permute-start.1
  85.5 2.2 collective-permute-done.1
  88.9 14.6 %fusion.3 = (u8[8,16,2,128]{1,0,3,2:T(8,128)(4,1)S(1)}, bf16[8,16,2,8,128]{1,0,4,3,2:T(8,128)(2,1)S(1)}) fusion(f32[16]{0:T(128)S(1)} %copy-done.16, bf16[8,1,4,8,128]{0,1,4,3,2:T(2,128)(2,1)S(1)} %copy.72, bf16[16,1,3,3,3]{0,4,3,2,1:T(4,128)(2,1)S(1)} %copy-done.15), kind=kOutput, calls=%fused_computation.18 | convolution fusion | flops 15497216 | bytes 623520 | tf_op jit(solution)/shard_map/conv_general_dilated | solution.py:31
  103.5 1.9 copy-done.6
  105.6 1.5 copy.97
  107.1 2.5 collective-permute-start.2
  113.8 6.7 %convert_reduce_fusion.2 = (f32[8,32]{1,0:T(8,128)S(1)}, bf16[8,32,1,4,64]{1,0,4,3,2:T(8,128)(2,1)S(1)}) fusion(f32[8,4,64,32]{3,0,2,1:T(8,128)} %copy.77, f32[32]{0:T(128)S(1)} %copy-done.17, bf16[32,16,3,3,3]{0,1,4,3,2:T(8,128)(2,1)S(1)} %copy-done, bf16[8,16,2,8,128]{1,0,4,3,2:T(8,128)(2,1)} %copy-done.6, bf16[8,16,1,8,128]{1,0,4,3,2:T(8,128)(2,1)S(1)} %copy.75), kind=kOutput, calls=%fused_computation.39 | convolution fusion | flops 53600000 | bytes 1208448 | tf_op jit(solution)/shard_map/conv_general_dilated | solution.py:31
  120.5 12.9 %psum.70 = f32[8,32]{1,0:T(8,128)S(1)} all-reduce(f32[8,32]{1,0:T(8,128)S(1)} %get-tuple-element.96), channel_id=1, replica_groups=mesh['dp'=32,'slab'=8] {'slab'}, use_global_device_ids=true, to_apply=%region_6.7 | all-reduce | flops 256 | bytes 2048 | tf_op jit(solution)/shard_map/psum | solution.py:140
  135.7 1.5 convert_reduce_fusion.3
  138.8 7.1 %fusion.1 = f32[32,16,3,3,3]{0,1,4,3,2:T(8,128)} fusion(bf16[8,32,1,4,64]{1,0,4,3,2:T(8,128)(2,1)S(1)} %get-tuple-element.81, bf16[8,16,2,8,128]{1,0,4,3,2:T(8,128)(2,1)} %copy-done.6, bf16[8,16,1,8,128]{1,0,4,3,2:T(8,128)(2,1)} %copy-done.3), kind=kOutput, calls=%fused_computation.16 | convolution fusion | flops 53207040 | bytes 972800 | tf_op jit(solution)/shard_map/transpose | solution.py:63
  146.7 6.2 %fusion.50 = f32[8,16,3,8,128]{1,0,4,3,2:T(8,128)S(1)} fusion(bf16[8,32,1,4,64]{1,0,4,3,2:T(8,128)(2,1)S(1)} %get-tuple-element.81, bf16[32,16,3,3,3]{0,1,4,3,2:T(8,128)(2,1)S(1)} %copy-done), kind=kOutput, calls=%fused_computation.140 | convolution fusion | flops 51634176 | bytes 1731584 | tf_op jit(solution)/shard_map/conv_general_dilated | solution.py:77
  152.9 4.6 %copy-done.1 = f32[8,16,3,8,128]{1,0,4,3,2:T(8,128)} copy-done((f32[8,16,3,8,128]{1,0,4,3,2:T(8,128)}, f32[8,16,3,8,128]{1,0,4,3,2:T(8,128)S(1)}, u32[]{:S(2)}) %copy-start.1) | copy-done | bytes 1572888
  157.8 1.7 copy.98
  159.5 2.1 collective-permute-start.3
  161.8 7.4 %slice.89 = f32[8,16,2,8,128]{1,0,4,3,2:T(8,128)} slice(f32[8,16,3,8,128]{1,0,4,3,2:T(8,128)} %copy-done.1), slice={[0:8], [0:16], [1:3], [0:8], [0:128]} | slice | bytes 2097152 | tf_op jit(solution)/shard_map/slice | solution.py:177
  170.5 2.7 copy.82
  173.2 5.9 %fusion = f32[8,16,2,8,128]{1,0,4,3,2:T(8,128)} fusion(f32[8,16,2,8,128]{1,0,4,3,2:T(8,128)} %slice.89, f32[8,16,1,8,128]{1,0,4,3,2:T(8,128)} %copy.82, f32[8,16,3,8,128]{1,0,4,3,2:T(8,128)} %copy-done.1), kind=kLoop, calls=%fused_computation.15 | loop fusion | flops 131072 | bytes 12582912 | tf_op jit(solution)/shard_map/scatter-add | solution.py:178
  179.1 25.6 %scatter_fusion = f32[8,16,2,8,128]{1,0,4,3,2:T(8,128)} fusion(f32[8,16,2,8,128]{1,0,4,3,2:T(8,128)} %fusion, s32[256]{0:T(256)S(1)} %reshape.359, f32[256,8,16]{2,1,0:T(8,128)S(1)} %bitcast.134), kind=kCustom, calls=%fused_computation.6 | custom fusion | flops 32768 | bytes 396288 | tf_op jit(solution)/shard_map/scatter-add | solution.py:180
  204.7 9.2 %convolution_bitcast_fusion.2 = f32[16,1,3,3,3]{0,1,4,3,2:T(1,128)S(1)} fusion(bf16[8,1,4,8,128]{0,1,4,3,2:T(2,128)(2,1)S(1)} %copy-done.5, f32[8,16,2,8,128]{1,0,4,3,2:T(8,128)} %scatter_fusion, u8[8,16,2,128]{1,0,3,2:T(8,128)(4,1)S(1)} %get-tuple-element.98), kind=kOutput, calls=%fused_computation.27 | convolution fusion | flops 14219264 | bytes 1148608 | tf_op jit(solution)/shard_map/conv_general_dilated | solution.py:54
  214.0 2.2 convert_reduce_fusion
  216.2 74.7 %all-reduce = (f32[16,1,3,3,3]{0,1,4,3,2:T(1,128)}, f32[16]{0:T(128)}, f32[32,16,3,3,3]{0,1,4,3,2:T(8,128)}, f32[32]{0:T(128)}, f32[32,16]{0,1:T(8,128)}, /*inde...) all-reduce(f32[16,1,3,3,3]{0,1,4,3,2:T(1,128)S(1)} %convolution_bit, ...), channel_id=1, replica_groups=mesh['dp'=32,'slab'=8] {'dp','slab'}, use_global_device_ids=true, to_apply=%region_8.9 | all-reduce | flops 15113 | bytes 120904 | tf_op jit(solution)/shard_map/psum | solution.py:184
  (113 shorter events, 24.7 us)
Async XLA Ops:
  0.6 113.1 %copy-start = (bf16[32,16,3,3,3]{0,1,4,3,2:T(8,128)(2,1)S(1)}, bf16[32,16,3,3,3]{0,1,4,3,2:T(8,128)(2,1)}, u32[]{:S(2)}) copy-start(bf16[32,16,3,3,3]{0,1,4,3,2:T(8,128)(2,1)} %param.21) | copy-start | bytes 82948
  0.7 88.2 %copy-start.16 = (f32[16]{0:T(128)S(1)}, f32[16]{0:T(128)}, u32[]{:S(2)}) copy-start(f32[16]{0:T(128)} %param.20) | copy-start | bytes 196
  0.7 88.2 %copy-start.15 = (bf16[16,1,3,3,3]{0,4,3,2,1:T(4,128)(2,1)S(1)}, bf16[16,1,3,3,3]{0,4,3,2,1:T(4,128)(2,1)}, u32[]{:S(2)}) copy-start(bf16[16,1,3,3,3]{0,4,3,2,1:T(4,128)(2,1)} %param.19) | copy-start | bytes 2596
  9.3 20.6 %all-to-all-start = ((s32[32,2,1]{1,2,0:T(1,128)}), s32[32,2,1]{1,2,0:T(1,128)S(1)}, u32[]{:S(2)}, u32[]{:S(2)}) async-start(s32[32,2,1]{1,2,0:T(1,128)} %bitcast.10), calls=%async_computation | async-start | bytes 32768 | tf_op jit(solution)/shard_map/all_to_all | solution.py:246
  29.9 16.7 %all-to-all-start.3 = ((bf16[32,2,6]{2,1,0:T(2,128)(2,1)}), bf16[32,2,6]{2,1,0:T(2,128)(2,1)S(1)}, u32[]{:S(2)}, u32[]{:S(2)}) async-start(bf16[32,2,6]{2,1,0:T(2,128)(2,1)} %broadcast_select_fusion.1), calls=%async_computation.3 | async-start | bytes 32768 | tf_op jit(solution)/shard_map/all_to_all | solution.py:245
  39.6 93.9 %copy-start.12 = (pred[8]{0:T(512)(128)(4,1)}, pred[8]{0:T(512)(128)(4,1)S(1)}, u32[]{:S(2)}) copy-start(pred[8]{0:T(512)(128)(4,1)S(1)} %fusion.23) | copy-start | bytes 28
  39.6 93.8 %copy-start.20 = (f32[8]{0:T(128)}, f32[8]{0:T(128)S(1)}, u32[]{:S(2)}) copy-start(f32[8]{0:T(128)S(1)} %convert_element_type.66) | copy-start | bytes 100
  46.6 13.0 %all-to-all-start.2 = ((bf16[32,2,768]{2,1,0:T(2,128)(2,1)}), bf16[32,2,768]{2,1,0:T(2,128)(2,1)S(1)}, u32[]{:S(2)}, u32[]{:S(2)}) async-start(bf16[32,2,768]{2,1,0:T(2,128)(2,1)} %reshape.379), calls=%async_computation.2 | async-start | bytes 196608 | tf_op jit(solution)/shard_map/all_to_all | solution.py:244
  59.6 14.5 %all-to-all-start.1 = ((bf16[64,2,8,128]{3,2,1,0:T(8,128)(2,1)}), bf16[64,2,8,128]{3,2,1,0:T(8,128)(2,1)S(1)}, u32[]{:S(2)}, u32[]{:S(2)}) async-start(bf16[64,2,8,128]{3,2,1,0:T(8,128)(2,1)} %select_select_fusion), calls=%async_computation.1 | async-start | bytes 524288 | tf_op jit(solution)/shard_map/all_to_all | solution.py:243
  63.5 69.9 %copy-start.13 = (pred[8]{0:T(512)(128)(4,1)}, pred[8]{0:T(512)(128)(4,1)S(1)}, u32[]{:S(2)}) copy-start(pred[8]{0:T(512)(128)(4,1)S(1)} %compare_and_fusion.3) | copy-start | bytes 28
  74.7 10.8 %collective-permute-start = (bf16[8,1,8,128]{3,2,1,0:T(8,128)(2,1)S(1)}, bf16[8,1,8,128]{3,2,1,0:T(8,128)(2,1)S(1)}, u32[]{:S(2)}, u32[]{:S(2)}) collective-permute-start(bf16[8,1,8,128]{3,2,1,0:T(8,128)(2,1)S(1)} %get-tuple-element.83), channel_id=1, source_target_pairs={{0,1},{1,2},{2,3},{3,4},{4,5},{5,6},{6,7},{8,9},{9,10},{10,11},{11... | collective-permute-start | bytes 49160 | tf_op jit(solution)/shard_map/ppermute | solution.py:15
  82.6 5.1 %collective-permute-start.1 = (bf16[8,1,8,128]{3,2,1,0:T(8,128)(2,1)S(1)}, bf16[8,1,8,128]{3,2,1,0:T(8,128)(2,1)S(1)}, u32[]{:S(2)}, u32[]{:S(2)}) collective-permute-start(bf16[8,1,8,128]{3,2,1,0:T(8,128)(2,1)S(1)} %get-tuple-element.84), channel_id=1, source_target_pairs={{1,0},{2,1},{3,2},{4,3},{5,4},{6,5},{7,6},{9,8},{10,9},{11,10},{12... | collective-permute-start | bytes 49160 | tf_op jit(solution)/shard_map/ppermute | solution.py:17
  88.9 14.6 %copy-start.4 = (bf16[8,1,4,8,128]{0,1,4,3,2:T(2,128)(2,1)}, bf16[8,1,4,8,128]{0,1,4,3,2:T(2,128)(2,1)S(1)}, u32[]{:S(2)}) copy-start(bf16[8,1,4,8,128]{0,1,4,3,2:T(2,128)(2,1)S(1)} %copy.72) | copy-start | bytes 196612
  103.5 1.9 copy-start.6
  103.5 7.5 %copy-start.8 = (bf16[32,16]{0,1:T(8,128)(2,1)S(1)}, bf16[32,16]{0,1:T(8,128)(2,1)}, u32[]{:S(2)}) copy-start(bf16[32,16]{0,1:T(8,128)(2,1)} %param.23) | copy-start | bytes 3076
  105.4 8.3 %copy-start.17 = (f32[32]{0:T(128)S(1)}, f32[32]{0:T(128)}, u32[]{:S(2)}) copy-start(f32[32]{0:T(128)} %param.22) | copy-start | bytes 388
  107.1 5.6 %collective-permute-start.2 = (bf16[8,16,1,8,128]{4,3,2,1,0:T(8,128)(2,1)S(1)}, bf16[8,16,1,8,128]{4,3,2,1,0:T(8,128)(2,1)S(1)}, u32[]{:S(2)}, u32[]{:S(2)}) collective-permute-start(bf16[8,16,1,8,128]{4,3,2,1,0:T(8,128)(2,1)S(1)} %copy.97), channel_id=1, source_target_pairs={{0,1},{1,2},{2,3},{3,4},{4,5},{5,6},{6,7},{8,9},{9,10},{10,11},{11... | collective-permute-start | bytes 786440 | tf_op jit(solution)/shard_map/ppermute | solution.py:27
  113.7 6.8 %copy-start.3 = (bf16[8,16,1,8,128]{1,0,4,3,2:T(8,128)(2,1)}, bf16[8,16,1,8,128]{1,0,4,3,2:T(8,128)(2,1)S(1)}, u32[]{:S(2)}) copy-start(bf16[8,16,1,8,128]{1,0,4,3,2:T(8,128)(2,1)S(1)} %copy.75) | copy-start | bytes 786436
  113.8 19.7 %copy-start.11 = (bf16[6,32]{1,0:T(8,128)(2,1)S(1)}, bf16[6,32]{1,0:T(8,128)(2,1)}, u32[]{:S(2)}) copy-start(bf16[6,32]{1,0:T(8,128)(2,1)} %param.26) | copy-start | bytes 1156
  113.8 19.7 %copy-start.18 = (f32[6]{0:T(128)S(1)}, f32[6]{0:T(128)}, u32[]{:S(2)}) copy-start(f32[6]{0:T(128)} %param.27) | copy-start | bytes 76
  134.7 0.6 copy-start.9
  152.9 4.6 %copy-start.1 = (f32[8,16,3,8,128]{1,0,4,3,2:T(8,128)}, f32[8,16,3,8,128]{1,0,4,3,2:T(8,128)S(1)}, u32[]{:S(2)}) copy-start(f32[8,16,3,8,128]{1,0,4,3,2:T(8,128)S(1)} %fusion.50) | copy-start | bytes 4718596
  157.5 4.2 %copy-start.19 = (f32[6]{0:T(128)S(1)}, f32[6]{0:T(128)}, u32[]{:S(2)}) copy-start(f32[6]{0:T(128)} %get-tuple-element.76) | copy-start | bytes 76
  159.5 10.9 %collective-permute-start.3 = (bf16[8,16,1,8,128]{4,3,2,1,0:T(8,128)(2,1)S(1)}, bf16[8,16,1,8,128]{4,3,2,1,0:T(8,128)(2,1)S(1)}, u32[]{:S(2)}, u32[]{:S(2)}) collective-permute-start(bf16[8,16,1,8,128]{4,3,2,1,0:T(8,128)(2,1)S(1)} %copy.98), channel_id=1, source_target_pairs={{1,0},{2,1},{3,2},{4,3},{5,4},{6,5},{7,6},{9,8},{10,9},{11,10},{12... | collective-permute-start | bytes 786440 | tf_op jit(solution)/shard_map/ppermute | solution.py:27
  161.8 8.4 %copy-start.10 = (f32[8,6]{1,0:T(8,128)S(1)}, f32[8,6]{1,0:T(8,128)}, u32[]{:S(2)}) copy-start(f32[8,6]{1,0:T(8,128)} %copy-done.9) | copy-start | bytes 580
  173.2 31.5 %copy-start.5 = (bf16[8,1,4,8,128]{0,1,4,3,2:T(2,128)(2,1)S(1)}, bf16[8,1,4,8,128]{0,1,4,3,2:T(2,128)(2,1)}, u32[]{:S(2)}) copy-start(bf16[8,1,4,8,128]{0,1,4,3,2:T(2,128)(2,1)} %copy-done.4) | copy-start | bytes 196612
  204.7 9.2 %copy-start.2 = (f32[8,16,2,8,128]{1,0,4,3,2:T(8,128)S(1)}, f32[8,16,2,8,128]{1,0,4,3,2:T(8,128)}, u32[]{:S(2)}) copy-start(f32[8,16,2,8,128]{1,0,4,3,2:T(8,128)} %scatter_fusion) | copy-start | bytes 3145732
  213.9 2.2 copy-start.7
  213.9 2.2 copy-start.14
where the time goes:
time: 296 us; the launch traced here: 291 us
  blocking collectives  87.6 us (30%)
  matrix products  48.6 us (16%)
  other arithmetic  44.6 us (15%)
  starting transfers between devices  42.5 us (14%)
  local copies, waits for them, and re-layouts  37.5 us (13%)
  waiting for transfers between devices  28.7 us (10%)
    psum x1, blocking collectives, train(): lax.psum((g_first, g_first_bias, g_second, g_second_bias, g_short, g_flux...  74.7 us
    scatter-add x1, other arithmetic, train(): da_first = da_first.at[:, :, ::2, ::2, ::2].add(shortcut)  25.6 us
    conv_general_dilated x2, matrix products, conv_forward(): lax.conv_general_dilated(inputs, kernel, (stride, stride, stride), paddin...  21.3 us
    psum x1, blocking collectives, train(): lax.psum(jnp.sum(a_second, axis=(2, 3, 4), dtype=jnp.float32), 'slab')  12.9 us
    all_to_all x1, starting transfers between devices, on_device(): lax.all_to_all(shipped[3], 'dp', split_axis=0, concat_axis=0, tiled=True)  12 us
    unnamed x47, local copies, waits for them, and re-layouts  11.6 us
    all_to_all x1, waiting for transfers between devices, on_device(): lax.all_to_all(shipped[0], 'dp', split_axis=0, concat_axis=0, tiled=True)  9.28 us
    conv_general_dilated x1, matrix products, kernel_grad(): lax.conv_general_dilated(inputs, cotangent, (1, 1, 1), pad_spans, rhs_dil...  9.22 us
  transfers between devices with their start and end apart: 8, of which 5 were waited for; matrix products, arithmetic and copies ran while one was open for 8% of the time, Pallas kernels for 0%

commit v1 on v0

v1 whole, which is shorter than its diff:
```python
import functools

import jax
import jax.numpy as jnp
from jax import lax
from jax.experimental import pallas as pl
from jax.experimental.pallas import tpu as pltpu
from jax.sharding import PartitionSpec as P

F32 = jnp.float32
BF16 = jnp.bfloat16
NN = (((1,), (0,)), ((), ()))
NT = (((1,), (1,)), ((), ()))
TN = (((0,), (0,)), ((), ()))

BLOCK = 144
CELLS = 512
TAPS = 144
CHUNK = 18
SENT = 25
ROUTED = 32


def mxu(a, b, dims=NN):
    return lax.dot_general(a, b, dims, preferred_element_type=F32)


def lanes(shape):
    return lax.broadcasted_iota(jnp.int32, shape, len(shape) - 1)


def rows(shape):
    return lax.broadcasted_iota(jnp.int32, shape, len(shape) - 2)


def pack(place_ref, vol_ref, ft_ref, out_ref):
    odd = place_ref[0] % 2 == 1
    for z in range(2):
        out_ref[:, z * 8 : z * 8 + 8, :] = vol_ref[:, z]
    goal = ft_ref[...].astype(F32)
    none = jnp.zeros_like(goal)
    low = jnp.concatenate([goal, none], axis=3)
    high = jnp.concatenate([none, goal], axis=3)
    both = jnp.where(odd, high, low)
    both = jnp.concatenate([both, jnp.zeros_like(both)], axis=2)
    out_ref[:, 16:40, :] = both.reshape(8, 24, 128).astype(BF16)


def prepare(
    w1_ref, w2_ref, ws_ref, wf_ref, wt_ref, b1_ref, b2_ref, bt_ref,
    t1_ref, w2a_ref, wb_ref, wsb_ref, fw_ref, fwt_ref, cols_ref, wtt_ref,
    base, order,
):
    base[...] = jnp.zeros_like(base)
    for kz in range(3):
        for ky in range(3):
            for kx in range(3):
                at = kz * 32 + kx * 8 + ky
                base[at : at + 1, 0:16] = w1_ref[kz, ky, kx : kx + 1, :].astype(F32)
    taps = base[0:88]
    placed = jnp.zeros((128, 128), F32)
    for px in range(2):
        for z in range(2):
            down, right = z * 32 + px * 8, px * 32 + z * 16
            parts = [pltpu.roll(taps, right, 1) if right else taps]
            if down < 40:
                parts = parts + [jnp.zeros((40 - down, 128), F32)]
            if down:
                parts = [jnp.zeros((down, 128), F32)] + parts
            placed = placed + jnp.concatenate(parts, axis=0)
    across = jnp.transpose(placed)[0:64]
    place = lanes((64, 128)) % 8
    for y in range(8):
        own = across
        if y == 0:
            own = jnp.where(place == 0, 0.0, own)
        if y == 7:
            own = jnp.where(place == 2, 0.0, own)
        if y != 1:
            own = pltpu.roll(own, (y - 1) % 128, 1)
        t1_ref[y * 64 : y * 64 + 64, :] = own.astype(BF16)
    order[...] = jnp.zeros_like(order)
    w2 = w2_ref[...].astype(F32)
    for ky in range(3):
        for s, kx in enumerate((1, 2, 0)):
            for zo, kz in enumerate((1, 2, 0)):
                to, at = ky * 144 + s * 48 + zo * 16, ((kz * 3 + ky) * 3 + kx) * 16
                order[to : to + 16, 0:32] = w2[at : at + 16]
    order[432:448, 0:32] = ws_ref[...].astype(F32)
    w2t = order[...]
    w2a_ref[...] = jnp.transpose(w2t)[0:32].astype(BF16)
    wsb_ref[...] = w2t[432:448].astype(BF16)
    own, near = ((1, 0),), ((2, 0), (0, 1))
    for sub in range(2):
        for px in range(2):
            for z in range(2):
                sides = [jnp.zeros((16, 128), F32), jnp.zeros((16, 128), F32)]
                for ky, sy in near if sub else own:
                    for kx, sx in near if px else own:
                        for kz, sz in near if z else own:
                            at = ky * 144 + (1, 2, 0).index(kx) * 48 + (1, 2, 0).index(kz) * 16
                            to = sz * 64 + sx * 32
                            part = w2t[at : at + 16]
                            sides[sy] = sides[sy] + (pltpu.roll(part, to, 1) if to else part)
                to = sub * 64 + px * 32 + z * 16
                wb_ref[to : to + 16, :] = jnp.concatenate(sides, axis=1).astype(BF16)
    base[...] = jnp.zeros_like(base)
    base[0:3, 0:32] = wf_ref[...].astype(F32)
    wide = base[0:8, :]
    wide = wide + pltpu.roll(wide, 32, 1)
    wide = wide + pltpu.roll(wide, 64, 1)
    head = jnp.concatenate(
        [jnp.broadcast_to(wide[f : f + 1], (8, 128)) for f in range(3)]
        + [jnp.zeros((104, 128), F32)],
        axis=0,
    )
    mine = (lanes((128, 128)) // 32 == rows((128, 128)) % 8) & (rows((128, 128)) < 24)
    head = jnp.where(mine, head, 0.0)
    fw_ref[...] = head[0:32].astype(BF16)
    fwt_ref[...] = jnp.transpose(head).astype(BF16)
    base[...] = jnp.zeros_like(base)
    base[0:1, 0:16] = b1_ref[...]
    base[1:2, 0:32] = b2_ref[...]
    base[8:14, 0:32] = wt_ref[...].astype(F32)
    pad = jnp.zeros((120, 128), F32)
    cols_ref[...] = jnp.transpose(jnp.concatenate([base[0:8, :], pad], axis=0))
    wtt_ref[0:32] = jnp.transpose(jnp.concatenate([base[8:16, :], pad], axis=0))[0:32]
    wtt_ref[32:40] = jnp.zeros((8, 128), F32)
    wtt_ref[32:33, 0:6] = bt_ref[...]


def step(
    flux_scale, tensor_scale, cell_count,
    place_ref, dest_ref, bf_ref, got_ref, kt_ref,
    t1_ref, w2a_ref, wb_ref, wsb_ref, fw_ref, fwt_ref, cols_ref, wtt_ref,
    out_ref,
    a_ref, a2_ref, d_ref, goal, g1, total,
):
    place = place_ref[0]
    live = jnp.where(dest_ref[place] >= 0, 1.0, 0.0)
    empty = jnp.zeros((8, 128), F32)

    def plane(z):
        if z < 0 or z > 15:
            return empty
        at = (z % 2) * 8
        return got_ref[z // 2, at : at + 8, :].astype(F32)

    low = jnp.concatenate([plane(4 * q - 1 + zi) for zi in range(4) for q in range(4)], axis=0)
    high = jnp.concatenate([plane(4 * q + 1 + zi) for zi in range(4) for q in range(4)], axis=0)
    cells = jnp.concatenate([low, high], axis=1).astype(BF16)
    r, c = rows((256, CELLS)), lanes((256, CELLS))
    x = 2 * (c % 64) - 1 + c // 128
    pick = (r % 128 == x) & (r // 128 == (c % 128) // 64)
    apart = mxu(cells, jnp.where(pick, 1.0, 0.0).astype(BF16))
    lines = []
    for zi in range(4):
        for xt in range(4):
            lines.append(
                jnp.concatenate(
                    [
                        apart[zi * 32 + q * 8 : zi * 32 + q * 8 + 8, xt * 128 : xt * 128 + 128]
                        for q in range(4)
                    ],
                    axis=1,
                )
            )
    lines.append(jnp.where(rows((16, CELLS)) == 0, 1.0, 0.0))
    xcol = jnp.concatenate(lines, axis=0).astype(BF16)
    b1 = jnp.concatenate([cols_ref[0:16, 0:1]] * 4, axis=0)
    first_z = lanes((16, CELLS)) < 64
    first_x = lanes((48, CELLS)) % 64 == 0
    a_ref[0:BLOCK] = jnp.zeros((BLOCK, CELLS), BF16)
    for y in range(8):
        z1 = mxu(t1_ref[y * 64 : y * 64 + 64], xcol[0:128]) + b1
        act = jnp.maximum(z1, 0.0).astype(BF16)
        wide = act.astype(F32)
        at = (y + 1) * BLOCK
        for px in range(2):
            moved = pltpu.roll(wide[px * 32 + 16 : px * 32 + 32], 64, 1)
            moved = jnp.where(first_z, 0.0, moved)
            a_ref[at + px * 48 : at + px * 48 + 32] = act[px * 32 : px * 32 + 32]
            a_ref[at + px * 48 + 32 : at + px * 48 + 48] = moved.astype(BF16)
        late = jnp.concatenate([wide[32:64], moved], axis=0)
        late = jnp.where(first_x, 0.0, pltpu.roll(late, 1, 1))
        a_ref[at + 96 : at + BLOCK] = late.astype(BF16)
    b2 = cols_ref[0:32, 1:2]
    pooled = jnp.zeros((32, 1), F32)
    for y in range(4):
        at = 2 * y * BLOCK
        z2 = mxu(w2a_ref[:, 0:432], a_ref[at : at + 432])
        short = mxu(w2a_ref[:, 432:448], a_ref[at + BLOCK : at + BLOCK + 16])
        z2 = (z2 + b2) + short
        act = jnp.maximum(z2, 0.0).astype(BF16)
        a2_ref[y * 32 : y * 32 + 32] = act
        pooled = pooled + jnp.sum(act.astype(F32), axis=1, keepdims=True)
    pooled = pooled / cell_count
    a2 = a2_ref[...]
    head = wtt_ref[0:32]
    tensor = jnp.sum(head * pooled, axis=0, keepdims=True) + wtt_ref[32:33]
    goal[0:8] = jnp.zeros((8, 128), F32)
    goal[0:8, 0:6] = kt_ref[...].astype(F32)
    wanted = jnp.sum(jnp.where(rows((8, 128)) == place, goal[0:8], 0.0), axis=0, keepdims=True)
    dt = tensor_scale * (tensor - wanted) * live
    spread = jnp.sum(head * dt, axis=1, keepdims=True) / cell_count
    row = rows((24, 1))
    bias = jnp.where(row < 8, bf_ref[0], jnp.where(row < 16, bf_ref[1], bf_ref[2]))
    full = mxu(fw_ref[0:24], a2) + bias
    wanted = jnp.concatenate(
        [
            got_ref[2 * q, 16:40, :].astype(F32) + got_ref[2 * q + 1, 16:40, :].astype(F32)
            for q in range(4)
        ],
        axis=1,
    )
    diff = flux_scale * (full - wanted) * live
    df = jnp.where(row % 8 < 4, diff, 0.0)
    df = jnp.concatenate([df, jnp.zeros((8, CELLS), F32)], axis=0).astype(BF16)
    member = lanes((8, CELLS)) // 64 == rows((8, CELLS))
    shares = []
    for f in range(3):
        for y in range(4):
            line = jnp.where(member, full[f * 8 + y : f * 8 + y + 1], 0.0)
            line = (line[:, 0:128] + line[:, 128:256]) + (line[:, 256:384] + line[:, 384:512])
            shares.append(line + pltpu.roll(line, 64, 1))
    left = lanes((8, 128)) < 64
    for k in range(6):
        both = jnp.where(left, shares[2 * k], shares[2 * k + 1])
        out_ref[:, CHUNK + k, :] = both.astype(BF16).astype(F32)
    tensor = tensor.astype(BF16).astype(F32)
    out_ref[:, CHUNK + 6, :] = jnp.broadcast_to(tensor, (8, 128))
    last_x = lanes((32, CELLS)) % 64 == 63
    last_z = lanes((32, CELLS)) >= 448
    bias2 = jnp.zeros((32, 1), F32)
    dz2 = []
    for y in range(4):
        da2 = mxu(fwt_ref[y * 32 : y * 32 + 32, 0:32], df) + spread
        d = jnp.where(a2_ref[y * 32 : y * 32 + 32] > 0, da2, 0.0).astype(BF16)
        wide = d.astype(F32)
        bias2 = bias2 + jnp.sum(wide, axis=1, keepdims=True)
        next_x = jnp.where(last_x, 0.0, pltpu.roll(wide, CELLS - 1, 1))
        next_z = jnp.where(last_z, 0.0, pltpu.roll(wide, CELLS - 64, 1))
        both = jnp.where(last_z, 0.0, pltpu.roll(next_x, CELLS - 64, 1))
        d_ref[y * 128 : y * 128 + 32] = d
        d_ref[y * 128 + 32 : y * 128 + 64] = next_x.astype(BF16)
        d_ref[y * 128 + 64 : y * 128 + 96] = next_z.astype(BF16)
        d_ref[y * 128 + 96 : y * 128 + 128] = both.astype(BF16)
        dz2.append(d)
    d_ref[512:640] = jnp.zeros((128, CELLS), BF16)
    none = jnp.zeros((32, CELLS), BF16)
    second = jnp.zeros((BLOCK, 128), F32)
    fold = jnp.zeros((128, 64), F32)
    tail = jnp.zeros((1, 64), F32)
    place8 = rows((128, 64)) % 8
    for y in range(4):
        at = (2 * y + 1) * BLOCK
        da1 = mxu(wb_ref[...], d_ref[y * 128 : y * 128 + 256])
        short = mxu(wsb_ref[:, 0:32], dz2[y])
        da1 = jnp.concatenate([da1[0:16] + short, da1[16:128]], axis=0)
        for sub in range(2):
            act = a_ref[at + sub * BLOCK : at + sub * BLOCK + BLOCK]
            if sub == 0:
                sides = [none, dz2[y], none, none]
            else:
                sides = [dz2[y + 1] if y < 3 else none, none, dz2[y], none]
            second = second + mxu(act, jnp.concatenate(sides, axis=0), NT)
            on = jnp.concatenate([act[0:32], act[48:80]], axis=0) > 0
            dz1 = jnp.where(on, da1[sub * 64 : sub * 64 + 64], 0.0).astype(BF16)
            part = mxu(xcol, dz1, NT)
            tail = tail + part[128:129]
            part = part[0:128]
            shift = 2 * y + sub - 1
            if shift == -1:
                part = jnp.where(place8 == 7, 0.0, part)
            if shift == 6:
                part = jnp.where(place8 == 0, 0.0, part)
            if shift:
                part = pltpu.roll(part, (-shift) % 128, 0)
            fold = fold + part
    g1[...] = jnp.zeros_like(g1)
    g1[0:128, 0:64] = fold
    g1[128:129, 0:64] = tail
    first = jnp.zeros((88, 128), F32)
    first_bias = jnp.zeros((1, 128), F32)
    for px in range(2):
        for z in range(2):
            down, right = z * 32 + px * 8, px * 32 + z * 16
            to = (96 - right) % 128
            first = first + pltpu.roll(g1[down : down + 88, :], to, 1)
            first_bias = first_bias + pltpu.roll(g1[128:129, :], to, 1)
    cross = mxu(df, a2, NT)
    same = lanes((32, 128)) // 32 == rows((32, 128)) % 8
    cross = jnp.where(same, cross, 0.0)
    cross = cross + pltpu.roll(cross, 64, 1)
    cross = cross + pltpu.roll(cross, 32, 1)
    flux_sum = jnp.sum(df.astype(F32), axis=1, keepdims=True)
    lane = lanes((1, 128))
    total[...] = second
    total[0:88] = second[0:88] + jnp.where((lane >= 96) & (lane < 112), first, 0.0)
    total[96:128] = second[96:128] + jnp.where(lane >= 96, pltpu.roll(pooled * dt, 96, 1), 0.0)
    kept = lane >= 96
    bias_row = jnp.zeros((1, 128), F32)
    for f in range(3):
        line = jnp.sum(cross[f * 8 : f * 8 + 8], axis=0, keepdims=True)
        total[128 + f : 129 + f] = second[128 + f : 129 + f] + jnp.where(kept, line, 0.0)
        sums = jnp.sum(flux_sum[f * 8 : f * 8 + 8], axis=0, keepdims=True)
        bias_row = jnp.where(lane == 96 + f, sums, bias_row)
    total[131:132] = second[131:132] + bias_row
    total[132:133] = second[132:133] + jnp.where(kept, pltpu.roll(dt, 96, 1), 0.0)
    total[133:134] = second[133:134] + jnp.where(kept & (lane < 112), first_bias, 0.0)
    column = jnp.concatenate([jnp.zeros((96, 1), F32), bias2], axis=0)
    column = jnp.transpose(jnp.broadcast_to(column, (128, 128)))[0:1]
    total[134:135] = second[134:135] + column
    for p in range(8):
        out_ref[p, 0:CHUNK] = total[p * CHUNK : p * CHUNK + CHUNK]


def route(dest_ref, got_ref, out_ref):
    chunk = got_ref[0, 0:CHUNK]
    for s in range(1, 8):
        chunk = chunk + got_ref[s, 0:CHUNK]
    groups = out_ref.shape[0]
    out_ref[:, 0:CHUNK, :] = jnp.broadcast_to(chunk[None], (groups, CHUNK, 128))
    lane = lanes((7, 128))
    marked = (lane == 127) & (rows((7, 128)) == 6)
    blank = jnp.where(marked, -1.0, 0.0)
    for w in range(2):
        at = CHUNK + 7 * w
        out_ref[:, at : at + 7, :] = jnp.broadcast_to(blank[None], (groups, 7, 128))
    for r in range(8):
        dest = dest_ref[r]
        group = dest // 8
        earlier = jnp.int32(0)
        for e in range(r):
            twin = (dest_ref[e] >= 0) & (dest_ref[e] // 8 == group)
            earlier = earlier + jnp.where(twin, 1, 0)
        slot = (dest % 8).astype(F32)
        piece = jnp.where(marked, slot, got_ref[r, CHUNK : CHUNK + 7])

        @pl.when((dest >= 0) & (earlier == 0))
        def _():
            out_ref[group, CHUNK : CHUNK + 7, :] = piece

        @pl.when((dest >= 0) & (earlier > 0))
        def _():
            out_ref[group, CHUNK + 7 : CHUNK + 14, :] = piece


def spread(got_ref, out_ref):
    chunk = jnp.sum(got_ref[:, 0:CHUNK, :], axis=0)
    out_ref[...] = jnp.broadcast_to(chunk[None], out_ref.shape)


def place_records(got_ref, fp_ref, tp_ref):
    count = got_ref.shape[0]

    def candidates(k):
        return jnp.concatenate(
            [got_ref[:, CHUNK + k, :], got_ref[:, CHUNK + 7 + k, :]], axis=0
        )

    last = candidates(6)
    lane = lanes((2 * count, 128))
    slot = jnp.sum(jnp.where(lane == 127, last, 0.0), axis=1, keepdims=True)
    hit = jnp.where((slot == lane.astype(F32)) & (lane < 8), 1.0, 0.0)
    hit = jnp.concatenate([hit, jnp.zeros((128 - 2 * count, 128), F32)], axis=0)
    choose = jnp.transpose(hit)[0:8, 0 : 2 * count].astype(BF16)
    for k in range(6):
        got = mxu(choose, candidates(k).astype(BF16)).astype(BF16)
        f, y = (2 * k) // 4, (2 * k) % 4
        fp_ref[:, f, y, :] = got[:, 0:64]
        fp_ref[:, f, y + 1, :] = got[:, 64:128]
    tp_ref[...] = mxu(choose, last.astype(BF16))[:, 0:6].astype(BF16)


def finish(
    got_ref,
    g1_ref, b1_ref, g2_ref, b2_ref, gs_ref, gf_ref, bf_ref, gt_ref, bt_ref,
    total,
):
    for p in range(8):
        total[p * CHUNK : p * CHUNK + CHUNK] = got_ref[p]
    for kz in range(3):
        for ky in range(3):
            for kx in range(3):
                at = kz * 32 + kx * 8 + ky
                g1_ref[(kz * 3 + ky) * 3 + kx] = total[at : at + 1, 96:112]
    for ky in range(3):
        block = total[0:144, ky * 32 : ky * 32 + 32]
        for s, kx in enumerate((1, 2, 0)):
            for zo, kz in enumerate((1, 2, 0)):
                to = ((kz * 3 + ky) * 3 + kx) * 16
                part = block[s * 48 + zo * 16 : s * 48 + zo * 16 + 16]
                g2_ref[to : to + 16] = part
                if ky == 1 and kx == 1 and kz == 1:
                    gs_ref[...] = part
    heads = jnp.concatenate([total[96:128, :], jnp.zeros((96, 128), F32)], axis=0)
    gt_ref[...] = jnp.transpose(heads)[96:102, 0:32]
    gf_ref[...] = total[128:131, 96:128]
    bf_ref[...] = total[131:132, 96:99]
    bt_ref[...] = total[132:133, 96:102]
    b1_ref[...] = total[133:134, 96:112]
    b2_ref[...] = total[134:135, 96:128]


SMEM = pl.BlockSpec(memory_space=pltpu.SMEM)
VMEM = pl.BlockSpec(memory_space=pltpu.VMEM)
LIMIT = 48 * 1024 * 1024


def run(kernel, name, scalars, arrays, outs, scratch=()):
    return pl.pallas_call(
        kernel,
        out_shape=tuple(jax.ShapeDtypeStruct(s, t) for s, t in outs),
        in_specs=[SMEM] * len(scalars) + [VMEM] * len(arrays),
        out_specs=(VMEM,) * len(outs),
        scratch_shapes=[pltpu.VMEM(s, t) for s, t in scratch],
        compiler_params=pltpu.CompilerParams(vmem_limit_bytes=LIMIT),
        name=name,
    )(*scalars, *arrays)


def exchange(block, axis):
    return lax.all_to_all(block, axis, 0, 0, tiled=True)


def on_device(
    volume, flux_target, tensor_target, dest,
    first_weight, first_bias, second_weight, second_bias, short_weight,
    flux_weight, flux_bias, tensor_weight, tensor_bias,
):
    groups, slabs = lax.axis_size("dp"), lax.axis_size("slab")
    records = 8 * groups
    flux_count = records * 3 * slabs * 4 * 64
    tensor_count = records * 6
    cell_count = slabs * 4 * 64
    place = lax.axis_index("slab").astype(jnp.int32).reshape(1)
    (mine,) = run(
        pack, "pack", [place], [volume, flux_target[:, :, 0]], [((8, 40, 128), BF16)]
    )
    record = exchange(mine, "slab")
    weights = run(
        prepare, "prepare", [],
        [
            jnp.transpose(first_weight[:, 0], (1, 2, 3, 0)),
            jnp.transpose(second_weight, (2, 3, 4, 1, 0)).reshape(432, 32),
            jnp.transpose(short_weight),
            flux_weight, tensor_weight,
            first_bias.reshape(1, 16), second_bias.reshape(1, 32), tensor_bias.reshape(1, 6),
        ],
        [
            ((512, 128), BF16), ((32, 512), BF16), ((128, 256), BF16), ((16, 128), BF16),
            ((32, 128), BF16), ((128, 128), BF16), ((128, 128), F32), ((40, 128), F32),
        ],
        [((96, 128), F32), ((512, 128), F32)],
    )
    (terms,) = run(
        functools.partial(step, 2.0 / flux_count, 2.0 / tensor_count, float(cell_count)),
        "step", [place, dest, flux_bias], [record, tensor_target, *weights],
        [((8, SENT, 128), F32)],
        [
            ((9 * BLOCK, CELLS), BF16), ((128, CELLS), BF16), ((640, CELLS), BF16),
            ((8, 128), F32), ((136, 128), F32), ((BLOCK, 128), F32),
        ],
    )
    terms = exchange(terms, "slab")
    (routed,) = run(route, "route", [dest], [terms], [((groups, ROUTED, 128), F32)])
    routed = exchange(routed, "dp")
    (chunk,) = run(spread, "spread", [], [routed], [((slabs, CHUNK, 128), F32)])
    total = exchange(chunk, "slab")
    fp, tp = run(
        place_records, "place", [], [routed], [((8, 3, 4, 64), BF16), ((8, 6), BF16)]
    )
    g1, b1, g2, b2, gs, gf, bf, gt, bt = run(
        finish, "finish", [], [total],
        [
            ((27, 1, 16), F32), ((1, 16), F32), ((432, 32), F32), ((1, 32), F32),
            ((16, 32), F32), ((3, 32), F32), ((1, 3), F32), ((6, 32), F32), ((1, 6), F32),
        ],
        [((BLOCK, 128), F32)],
    )
    return (
        fp[:, :, None],
        tp,
        jnp.transpose(g1.reshape(3, 3, 3, 1, 16), (4, 3, 0, 1, 2)),
        b1.reshape(16),
        jnp.transpose(g2.reshape(3, 3, 3, 16, 32), (4, 3, 0, 1, 2)),
        b2.reshape(32),
        jnp.transpose(gs),
        gf,
        bf.reshape(3),
        gt,
        bt.reshape(6),
    )


def solution(mesh):
    cells = P("dp", "slab", None, None)
    fields = P("dp", None, "slab", None, None)
    return jax.shard_map(
        on_device,
        mesh=mesh,
        in_specs=(cells, fields, P("dp", None), P("dp")) + (P(),) * 9,
        out_specs=(fields, P("dp", None)) + (P(),) * 9,
        check_vma=False,
    )
```

time: 296 us -> 67.6 us (0.23); the launches traced: 291 us -> 67.1 us
  blocking collectives: 87.6 us -> 34.2 us
  matrix products: 48.6 us -> 0 us
  other arithmetic: 44.6 us -> 0 us
  local copies, waits for them, and re-layouts: 37.5 us -> 2.86 us
  starting transfers between devices: 42.5 us -> 13.2 us
  waiting for transfers between devices: 28.7 us -> 7.75 us
  Pallas kernels: 0 us -> 8.29 us
    psum x2 -> x0, blocking collectives: 87.6 us -> none  [the longest x1 74.7 us: train(): lax.psum((g_first, g_first_bias, g_second, g_second_bias, g_short, g_flux...]
    conv_general_dilated x4 -> x0, matrix products: 36.8 us -> none  [the longest x2 21.3 us: conv_forward(): lax.conv_general_dilated(inputs, kernel, (stride, stride, stride), paddin...]
    all_to_all x0 -> x2, blocking collectives: none -> 34.2 us  [exchange(): return lax.all_to_all(block, axis, 0, 0, tiled=True)]
    scatter-add x2 -> x0, other arithmetic: 31.5 us -> none  [the longest x1 25.6 us: train(): da_first = da_first.at[:, :, ::2, ::2, ::2].add(shortcut)]
    all_to_all x4 -> x2, waiting for transfers between devices: 26.5 us -> 7.75 us  [exchange(): return lax.all_to_all(block, axis, 0, 0, tiled=True)]
    all_to_all x4 -> x2, starting transfers between devices: 27.9 us -> 13.2 us  [exchange(): return lax.all_to_all(block, axis, 0, 0, tiled=True)]
    ppermute x4 -> x0, starting transfers between devices: 14.6 us -> none  [the longest x1 7.88 us: padded_2(): lax.ppermute(tail, axis, [(i, (i + 1) % count) for i in range(ends)])]
    unnamed x47 -> x26, local copies, waits for them, and re-layouts: 11.6 us -> 2.86 us
  transfers between devices with their start and end apart: 8 -> 2, of which waited for: 5 -> 2; matrix products, arithmetic and copies ran while one was open for 8% -> 0% of each run, Pallas kernels for 0% -> 2%
where the time goes in v1:
time: 67.6 us; the launch traced here: 67.1 us
  blocking collectives  34.2 us (51%)
  starting transfers between devices  13.2 us (20%)
  Pallas kernels  8.29 us (12%)
  waiting for transfers between devices  7.75 us (11%)
  local copies, waits for them, and re-layouts  2.86 us (4%)
  between operations  0.74 us (1%)
    all_to_all x2, blocking collectives, exchange(): return lax.all_to_all(block, axis, 0, 0, tiled=True)  34.2 us
    all_to_all x2, starting transfers between devices, exchange(): return lax.all_to_all(block, axis, 0, 0, tiled=True)  13.2 us
    pallas_call x7, Pallas kernels, run(): pl.pallas_call(kernel, out_shape=tuple((jax.ShapeDtypeStruct(s, t) for s,...  8.29 us
    all_to_all x2, waiting for transfers between devices, exchange(): return lax.all_to_all(block, axis, 0, 0, tiled=True)  7.75 us
    unnamed x26, local copies, waits for them, and re-layouts  2.86 us
  transfers between devices with their start and end apart: 2, of which 2 were waited for; matrix products, arithmetic and copies ran while one was open for 0% of the time, Pallas kernels for 2%

profile of v1, /device:TPU:1, one launch (start us, length us, event | category | flops | bytes accessed | tf_op | source)
XLA Modules:
  0.0 67.1 jit_solution(17979944491274566733)
XLA Ops:
  0.6 0.0 copy-start.1
  0.7 0.7 %copy-done.1 = bf16[8,2,8,128]{3,2,1,0:T(8,128)(2,1)S(1)} copy-done((bf16[8,2,8,128]{3,2,1,0:T(8,128)(2,1)S(1)}, bf16[8,2,8,128]{3,2,1,0:T(8,128)(2,1)}, u32[]{:S(2)}) %copy-start.1) | copy-done | bytes 32792
  1.4 0.0 copy-start.2
  1.4 0.7 %copy-done.2 = bf16[8,3,1,4,64]{4,3,2,1,0:T(4,128)(2,1)S(1)} copy-done((bf16[8,3,1,4,64]{4,3,2,1,0:T(4,128)(2,1)S(1)}, bf16[8,3,1,4,64]{4,3,2,1,0:T(4,128)(2,1)}, u32[]{:S(2)}) %copy-start.2) | copy-done | bytes 12312
  2.1 0.7 %pack.1 = bf16[8,40,128]{2,1,0:T(8,128)(2,1)} custom-call(s32[1]{0:T(128)} %bitcast.place_ref, bf16[8,2,8,128]{3,2,1,0:T(8,128)(2,1)S(1)} %copy-done.1, bf16[8,3,4,64]{3,2,1,0:T(4,128)(2,1)S(1)} %bitcast.27), custom_call_target="tpu_custom_call" | custom-call | tf_op jit(solution)/shard_map/pack/pallas_call | solution.py:412
  2.9 0.0 copy-start
  2.9 0.0 copy-start.4
  2.9 0.0 copy-start.10
  2.9 0.0 copy-start.11
  2.9 6.6 %all-to-all-start = ((bf16[8,40,128]{2,1,0:T(8,128)(2,1)}), bf16[8,40,128]{2,1,0:T(8,128)(2,1)S(1)}, u32[]{:S(2)}, u32[]{:S(2)}) async-start(bf16[8,40,128]{2,1,0:T(8,128)(2,1)} %pack.1), calls=%async_computation | async-start | bytes 163840 | tf_op jit(solution)/shard_map/all_to_all | solution.py:424
  9.5 0.0 copy-done
  9.6 0.0 copy-done.4
  9.6 0.0 copy-done.8
  9.6 0.0 copy-done.9
  9.6 0.0 copy-done.10
  9.6 0.0 copy-done.11
  9.6 0.6 copy-done.3
  10.2 0.0 copy-done.5
  10.3 0.4 prepare.1
  10.7 3.8 %all-to-all-done.got_ref = bf16[8,40,128]{2,1,0:T(8,128)(2,1)S(1)} async-done(((bf16[8,40,128]{2,1,0:T(8,128)(2,1)}), bf16[8,40,128]{2,1,0:T(8,128)(2,1)S(1)}, u32[]{:S(2)}, u32[]{:S(2)}) %all-to-all-start) | async-done | bytes 81952 | tf_op jit(solution)/shard_map/all_to_all | solution.py:424
  14.5 0.7 %copy-done.6 = bf16[8,6]{1,0:T(8,128)(2,1)S(1)} copy-done((bf16[8,6]{1,0:T(8,128)(2,1)S(1)}, bf16[8,6]{1,0:T(8,128)(2,1)}, u32[]{:S(2)}) %copy-start.6) | copy-done | bytes 120
  15.2 0.0 copy-done.7
  15.2 0.0 copy-done.12
  15.2 3.7 %step.1 = f32[8,25,128]{2,1,0:T(8,128)S(1)} custom-call(s32[1]{0:T(128)} %bitcast.place_ref, s32[8]{0:T(128)S(1)} %copy-done.7, f32[3]{0:T(128)S(1)} %copy-done.12, bf16[8,40,128]{2,1,0:T(8,128)(2,1)S(1)} %all-to-all-done.got_ref, bf16[8,6]{1,0:T(8,128)(2,1)S(1)} %copy-done.6, bf16[512,128]{1,0:T(8,128)(2,1)S(1)} %get-tuple-element.30.t1_ref, ...), custom_call_target="tpu_custom_call" | custom-call | tf_op jit(solution)/shard_map/step/pallas_call | solution.py:412
  18.8 8.5 %all_to_all.20.got_ref = f32[8,25,128]{2,1,0:T(8,128)S(1)} all-to-all(f32[8,25,128]{2,1,0:T(8,128)S(1)} %step.1), channel_id=1, replica_groups=mesh['dp'=32,'slab'=8] {'slab'}, dimensions={0} | all-to-all | bytes 204800 | tf_op jit(solution)/shard_map/all_to_all | solution.py:424
  27.3 0.9 %route.1 = f32[32,32,128]{2,1,0:T(8,128)S(1)} custom-call(s32[8]{0:T(128)S(1)} %copy-done.7, f32[8,25,128]{2,1,0:T(8,128)S(1)} %all_to_all.20.got_ref), custom_call_target="tpu_custom_call" | custom-call | tf_op jit(solution)/shard_map/route/pallas_call | solution.py:412
  28.2 25.8 %all_to_all.21.got_ref = f32[32,32,128]{2,1,0:T(8,128)S(1)} all-to-all(f32[32,32,128]{2,1,0:T(8,128)S(1)} %route.1), channel_id=1, replica_groups=mesh['dp'=32,'slab'=8] {'dp'}, dimensions={0} | all-to-all | bytes 1048576 | tf_op jit(solution)/shard_map/all_to_all | solution.py:424
  54.0 0.7 %spread.1 = f32[8,18,128]{2,1,0:T(8,128)} custom-call(f32[32,32,128]{2,1,0:T(8,128)S(1)} %all_to_all.21.got_ref), custom_call_target="tpu_custom_call" | custom-call | tf_op jit(solution)/shard_map/spread/pallas_call | solution.py:412
  54.6 6.6 %all-to-all-start.3 = ((f32[8,18,128]{2,1,0:T(8,128)}), f32[8,18,128]{2,1,0:T(8,128)S(1)}, u32[]{:S(2)}, u32[]{:S(2)}) async-start(f32[8,18,128]{2,1,0:T(8,128)} %spread.1), calls=%async_computation.3 | async-start | bytes 196608 | tf_op jit(solution)/shard_map/all_to_all | solution.py:424
  61.2 1.0 %place.1 = (bf16[8,3,4,64]{3,2,1,0:T(4,128)(2,1)}, bf16[8,6]{1,0:T(8,128)(2,1)}) custom-call(f32[32,32,128]{2,1,0:T(8,128)S(1)} %all_to_all.21.got_ref), custom_call_target="tpu_custom_call" | custom-call | tf_op jit(solution)/shard_map/place/pallas_call | solution.py:412
  62.2 4.0 %all-to-all-done.3.got_ref = f32[8,18,128]{2,1,0:T(8,128)S(1)} async-done(((f32[8,18,128]{2,1,0:T(8,128)}), f32[8,18,128]{2,1,0:T(8,128)S(1)}, u32[]{:S(2)}, u32[]{:S(2)}) %all-to-all-start.3) | async-done | bytes 73760 | tf_op jit(solution)/shard_map/all_to_all | solution.py:424
  66.2 0.8 %finish.1 = (f32[27,1,16]{2,1,0:T(1,128)}, f32[1,16]{1,0:T(1,128)}, f32[432,32]{1,0:T(8,128)}, f32[1,32]{1,0:T(1,128)}, f32[16,32]{1,0:T(8,128)}, /*index=5*/f32...) custom-call(f32[8,18,128]{2,1,0:T(8,128)S(1)} %all-to-all-done.3.got_ref), custom_call_target="tpu_custom_call" | custom-call | tf_op jit(solution)/shard_map/finish/pallas_call | solution.py:412
  (7 shorter events, 0.0 us)
Async XLA Ops:
  0.6 0.8 %copy-start.1 = (bf16[8,2,8,128]{3,2,1,0:T(8,128)(2,1)S(1)}, bf16[8,2,8,128]{3,2,1,0:T(8,128)(2,1)}, u32[]{:S(2)}) copy-start(bf16[8,2,8,128]{3,2,1,0:T(8,128)(2,1)} %vol_ref.1) | copy-start | bytes 98308
  1.4 0.7 %copy-start.2 = (bf16[8,3,1,4,64]{4,3,2,1,0:T(4,128)(2,1)S(1)}, bf16[8,3,1,4,64]{4,3,2,1,0:T(4,128)(2,1)}, u32[]{:S(2)}) copy-start(bf16[8,3,1,4,64]{4,3,2,1,0:T(4,128)(2,1)} %param.14) | copy-start | bytes 36868
  2.9 6.7 %copy-start = (bf16[32,16,3,3,3]{0,1,4,3,2:T(8,128)(2,1)S(1)}, bf16[32,16,3,3,3]{0,1,4,3,2:T(8,128)(2,1)}, u32[]{:S(2)}) copy-start(bf16[32,16,3,3,3]{0,1,4,3,2:T(8,128)(2,1)} %param.19) | copy-start | bytes 82948
  2.9 6.7 %copy-start.4 = (bf16[32,16]{0,1:T(8,128)(2,1)S(1)}, bf16[32,16]{0,1:T(8,128)(2,1)}, u32[]{:S(2)}) copy-start(bf16[32,16]{0,1:T(8,128)(2,1)} %param.21) | copy-start | bytes 3076
  2.9 6.7 %copy-start.8 = (bf16[3,32]{1,0:T(4,128)(2,1)S(1)}, bf16[3,32]{1,0:T(4,128)(2,1)}, u32[]{:S(2)}) copy-start(bf16[3,32]{1,0:T(4,128)(2,1)} %wf_ref.1) | copy-start | bytes 580
  2.9 6.7 %copy-start.9 = (f32[16]{0:T(128)S(1)}, f32[16]{0:T(128)}, u32[]{:S(2)}) copy-start(f32[16]{0:T(128)} %param.18) | copy-start | bytes 196
  2.9 6.7 %copy-start.10 = (f32[32]{0:T(128)S(1)}, f32[32]{0:T(128)}, u32[]{:S(2)}) copy-start(f32[32]{0:T(128)} %param.20) | copy-start | bytes 388
  2.9 6.7 %copy-start.11 = (f32[6]{0:T(128)S(1)}, f32[6]{0:T(128)}, u32[]{:S(2)}) copy-start(f32[6]{0:T(128)} %param.25) | copy-start | bytes 76
  2.9 11.6 %all-to-all-start = ((bf16[8,40,128]{2,1,0:T(8,128)(2,1)}), bf16[8,40,128]{2,1,0:T(8,128)(2,1)S(1)}, u32[]{:S(2)}, u32[]{:S(2)}) async-start(bf16[8,40,128]{2,1,0:T(8,128)(2,1)} %pack.1), calls=%async_computation | async-start | bytes 163840 | tf_op jit(solution)/shard_map/all_to_all | solution.py:424
  9.5 0.7 %copy-start.3 = (bf16[16,1,3,3,3]{0,4,3,2,1:T(4,128)(2,1)S(1)}, bf16[16,1,3,3,3]{0,4,3,2,1:T(4,128)(2,1)}, u32[]{:S(2)}) copy-start(bf16[16,1,3,3,3]{0,4,3,2,1:T(4,128)(2,1)} %param.17) | copy-start | bytes 2596
  9.5 0.7 %copy-start.5 = (bf16[6,32]{1,0:T(8,128)(2,1)S(1)}, bf16[6,32]{1,0:T(8,128)(2,1)}, u32[]{:S(2)}) copy-start(bf16[6,32]{1,0:T(8,128)(2,1)} %wt_ref.1) | copy-start | bytes 1156
  14.5 0.7 %copy-start.6 = (bf16[8,6]{1,0:T(8,128)(2,1)S(1)}, bf16[8,6]{1,0:T(8,128)(2,1)}, u32[]{:S(2)}) copy-start(bf16[8,6]{1,0:T(8,128)(2,1)} %kt_ref.1) | copy-start | bytes 292
  14.5 0.7 %copy-start.7 = (s32[8]{0:T(128)S(1)}, s32[8]{0:T(128)}, u32[]{:S(2)}) copy-start(s32[8]{0:T(128)} %dest_ref.3) | copy-start | bytes 100
  14.5 0.7 %copy-start.12 = (f32[3]{0:T(128)S(1)}, f32[3]{0:T(128)}, u32[]{:S(2)}) copy-start(f32[3]{0:T(128)} %bf_ref.1) | copy-start | bytes 40
  54.6 11.6 %all-to-all-start.3 = ((f32[8,18,128]{2,1,0:T(8,128)}), f32[8,18,128]{2,1,0:T(8,128)S(1)}, u32[]{:S(2)}, u32[]{:S(2)}) async-start(f32[8,18,128]{2,1,0:T(8,128)} %spread.1), calls=%async_computation.3 | async-start | bytes 196608 | tf_op jit(solution)/shard_map/all_to_all | solution.py:424

commit v2 on v1

v2 whole, which is shorter than its diff:
```python
import functools

import jax
import jax.numpy as jnp
from jax import lax
from jax.experimental import pallas as pl
from jax.experimental.pallas import tpu as pltpu
from jax.sharding import PartitionSpec as P

F32 = jnp.float32
BF16 = jnp.bfloat16
NN = (((1,), (0,)), ((), ()))
NT = (((1,), (1,)), ((), ()))
TN = (((0,), (0,)), ((), ()))

BLOCK = 144
CELLS = 512
TAPS = 144
ROWS = 128
LAYERS = 64


def mxu(a, b, dims=NN):
    return lax.dot_general(a, b, dims, preferred_element_type=F32)


def lanes(shape):
    return lax.broadcasted_iota(jnp.int32, shape, len(shape) - 1)


def rows(shape):
    return lax.broadcasted_iota(jnp.int32, shape, len(shape) - 2)


def pack(place_ref, vol_hbm, ft_hbm, out_ref, vol_ref, ft_ref, done):
    copies = [
        pltpu.make_async_copy(vol_hbm, vol_ref, done.at[0]),
        pltpu.make_async_copy(ft_hbm, ft_ref, done.at[1]),
    ]
    for copy in copies:
        copy.start()
    odd = place_ref[0] % 2 == 1
    copies[0].wait()
    for z in range(2):
        out_ref[:, z * 8 : z * 8 + 8, :] = vol_ref[:, z]
    copies[1].wait()
    goal = ft_ref[...].astype(F32)
    none = jnp.zeros_like(goal)
    low = jnp.concatenate([goal, none], axis=3)
    high = jnp.concatenate([none, goal], axis=3)
    both = jnp.where(odd, high, low)
    both = jnp.concatenate([both, jnp.zeros_like(both)], axis=2)
    out_ref[:, 16:40, :] = both.reshape(8, 24, 128).astype(BF16)


def prepare(
    place_ref, dest_ref, bf_ref,
    w1_ref, w2_ref, ws_ref, wf_ref, wt_ref, b1_ref, b2_ref, bt_ref, kt_ref,
    t1_ref, w2a_ref, wb_ref, wsb_ref, fw_ref, fwt_ref, cols_ref, wtt_ref, pick_ref,
    base, order,
    *, breadth,
):
    r, c = rows((256, CELLS)), lanes((256, CELLS))
    x = 2 * (c % 64) - 1 + c // 128
    pick = (r % 128 == x) & (r // 128 == (c % 128) // 64)
    pick_ref[...] = jnp.where(pick, 1.0, 0.0).astype(BF16)
    base[...] = jnp.zeros_like(base)
    for kz in range(3):
        for ky in range(3):
            for kx in range(3):
                at = kz * 32 + kx * 8 + ky
                base[at : at + 1, 0:16] = w1_ref[kz, ky, kx : kx + 1, :].astype(F32)
    taps = base[0:88]
    placed = jnp.zeros((128, 128), F32)
    for px in range(2):
        for z in range(2):
            down, right = z * 32 + px * 8, px * 32 + z * 16
            parts = [pltpu.roll(taps, right, 1) if right else taps]
            if down < 40:
                parts = parts + [jnp.zeros((40 - down, 128), F32)]
            if down:
                parts = [jnp.zeros((down, 128), F32)] + parts
            placed = placed + jnp.concatenate(parts, axis=0)
    across = jnp.transpose(placed)[0:64]
    place = lanes((64, 128)) % 8
    for y in range(8):
        own = across
        if y == 0:
            own = jnp.where(place == 0, 0.0, own)
        if y == 7:
            own = jnp.where(place == 2, 0.0, own)
        if y != 1:
            own = pltpu.roll(own, (y - 1) % 128, 1)
        t1_ref[y * 64 : y * 64 + 64, :] = own.astype(BF16)
    order[...] = jnp.zeros_like(order)
    w2 = w2_ref[...].astype(F32)
    for ky in range(3):
        for s, kx in enumerate((1, 2, 0)):
            for zo, kz in enumerate((1, 2, 0)):
                to, at = ky * 144 + s * 48 + zo * 16, ((kz * 3 + ky) * 3 + kx) * 16
                order[to : to + 16, 0:32] = w2[at : at + 16]
    order[432:448, 0:32] = ws_ref[...].astype(F32)
    w2t = order[...]
    w2a_ref[...] = jnp.transpose(w2t)[0:32].astype(BF16)
    wsb_ref[...] = w2t[432:448].astype(BF16)
    own, near = ((1, 0),), ((2, 0), (0, 1))
    for sub in range(2):
        for px in range(2):
            for z in range(2):
                sides = [jnp.zeros((16, 128), F32), jnp.zeros((16, 128), F32)]
                for ky, sy in near if sub else own:
                    for kx, sx in near if px else own:
                        for kz, sz in near if z else own:
                            at = ky * 144 + (1, 2, 0).index(kx) * 48 + (1, 2, 0).index(kz) * 16
                            to = sz * 64 + sx * 32
                            part = w2t[at : at + 16]
                            sides[sy] = sides[sy] + (pltpu.roll(part, to, 1) if to else part)
                to = sub * 64 + px * 32 + z * 16
                wb_ref[to : to + 16, :] = jnp.concatenate(sides, axis=1).astype(BF16)
    base[...] = jnp.zeros_like(base)
    base[0:3, 0:32] = wf_ref[...].astype(F32)
    wide = base[0:8, :]
    wide = wide + pltpu.roll(wide, 32, 1)
    wide = wide + pltpu.roll(wide, 64, 1)
    head = jnp.concatenate(
        [jnp.broadcast_to(wide[f : f + 1], (8, 128)) for f in range(3)]
        + [jnp.zeros((104, 128), F32)],
        axis=0,
    )
    mine = (lanes((128, 128)) // 32 == rows((128, 128)) % 8) & (rows((128, 128)) < 24)
    head = jnp.where(mine, head, 0.0)
    fw_ref[...] = head[0:32].astype(BF16)
    fwt_ref[...] = jnp.transpose(head).astype(BF16)
    base[...] = jnp.zeros_like(base)
    base[0:1, 0:16] = b1_ref[...]
    base[1:2, 0:32] = b2_ref[...]
    base[8:14, 0:32] = wt_ref[...].astype(F32)
    pad = jnp.zeros((120, 128), F32)
    cols_ref[...] = jnp.transpose(jnp.concatenate([base[0:8, :], pad], axis=0))
    wtt_ref[0:32] = jnp.transpose(jnp.concatenate([base[8:16, :], pad], axis=0))[0:32]
    base[16:24, 0:6] = kt_ref[...].astype(F32)
    wtt_ref[32:40] = jnp.zeros((8, 128), F32)
    wtt_ref[32:33, 0:6] = bt_ref[...]
    mine = rows((8, 128)) == place_ref[0]
    wtt_ref[33:34] = jnp.sum(jnp.where(mine, base[16:24], 0.0), axis=0, keepdims=True)
    dest = dest_ref[place_ref[0]]
    live = jnp.where(dest >= 0, 1.0, 0.0)
    wtt_ref[34:35] = jnp.broadcast_to(live, (1, 128))
    wtt_ref[35:36] = jnp.broadcast_to(dest.astype(F32), (1, 128))
    across = (jnp.maximum(dest, 0) // 8) % breadth
    for y in range(breadth):
        here = jnp.where((dest >= 0) & (across == y), 1.0, 0.0)
        wtt_ref[36 + y : 37 + y] = jnp.broadcast_to(here, (1, 128))
    row = rows((128, 1))
    bias = jnp.where(row < 8, bf_ref[0], jnp.where(row < 16, bf_ref[1], bf_ref[2]))
    cols_ref[:, 2:3] = bias


def step(
    flux_scale, tensor_scale, cell_count,
    got_ref,
    t1_ref, w2a_ref, wb_ref, wsb_ref, fw_ref, fwt_ref, cols_ref, wtt_ref, pick_ref,
    out_ref,
    a_ref, a2_ref, d_ref, dz1_ref, total, sent,
    *, breadth,
):
    live = wtt_ref[34:35, 0:1]
    empty = jnp.zeros((8, 128), F32)

    def plane(z):
        if z < 0 or z > 15:
            return empty
        at = (z % 2) * 8
        return got_ref[z // 2, at : at + 8, :].astype(F32)

    low = jnp.concatenate([plane(4 * q - 1 + zi) for zi in range(4) for q in range(4)], axis=0)
    high = jnp.concatenate([plane(4 * q + 1 + zi) for zi in range(4) for q in range(4)], axis=0)
    cells = jnp.concatenate([low, high], axis=1).astype(BF16)
    apart = mxu(cells, pick_ref[...])
    lines = []
    for zi in range(4):
        for xt in range(4):
            lines.append(
                jnp.concatenate(
                    [
                        apart[zi * 32 + q * 8 : zi * 32 + q * 8 + 8, xt * 128 : xt * 128 + 128]
                        for q in range(4)
                    ],
                    axis=1,
                )
            )
    lines.append(jnp.where(rows((16, CELLS)) == 0, 1.0, 0.0))
    xcol = jnp.concatenate(lines, axis=0).astype(BF16)
    b1 = jnp.concatenate([cols_ref[0:16, 0:1]] * 4, axis=0)
    first_z = lanes((16, CELLS)) < 64
    first_x = lanes((48, CELLS)) % 64 == 0
    a_ref[0:BLOCK] = jnp.zeros((BLOCK, CELLS), BF16)
    for y in range(8):
        z1 = mxu(t1_ref[y * 64 : y * 64 + 64], xcol[0:128]) + b1
        act = jnp.maximum(z1, 0.0).astype(BF16)
        wide = act.astype(F32)
        at = (y + 1) * BLOCK
        for px in range(2):
            moved = pltpu.roll(wide[px * 32 + 16 : px * 32 + 32], 64, 1)
            moved = jnp.where(first_z, 0.0, moved)
            a_ref[at + px * 48 : at + px * 48 + 32] = act[px * 32 : px * 32 + 32]
            a_ref[at + px * 48 + 32 : at + px * 48 + 48] = moved.astype(BF16)
        late = jnp.concatenate([wide[32:64], moved], axis=0)
        late = jnp.where(first_x, 0.0, pltpu.roll(late, 1, 1))
        a_ref[at + 96 : at + BLOCK] = late.astype(BF16)
    b2 = cols_ref[0:32, 1:2]
    pooled = jnp.zeros((32, 1), F32)
    for y in range(4):
        at = 2 * y * BLOCK
        z2 = mxu(w2a_ref[:, 0:432], a_ref[at : at + 432])
        short = mxu(w2a_ref[:, 432:448], a_ref[at + BLOCK : at + BLOCK + 16])
        z2 = (z2 + b2) + short
        act = jnp.maximum(z2, 0.0).astype(BF16)
        a2_ref[y * 32 : y * 32 + 32] = act
        pooled = pooled + jnp.sum(act.astype(F32), axis=1, keepdims=True)
    pooled = pooled / cell_count
    a2 = a2_ref[...]
    head = wtt_ref[0:32]
    tensor = jnp.sum(head * pooled, axis=0, keepdims=True) + wtt_ref[32:33]
    dt = tensor_scale * (tensor - wtt_ref[33:34]) * live
    spread = jnp.sum(head * dt, axis=1, keepdims=True) / cell_count
    row = rows((24, 1))
    full = mxu(fw_ref[0:24], a2) + cols_ref[0:24, 2:3]
    wanted = jnp.concatenate(
        [
            got_ref[2 * q, 16:40, :].astype(F32) + got_ref[2 * q + 1, 16:40, :].astype(F32)
            for q in range(4)
        ],
        axis=1,
    )
    diff = flux_scale * (full - wanted) * live
    df = jnp.where(row % 8 < 4, diff, 0.0)
    df = jnp.concatenate([df, jnp.zeros((8, CELLS), F32)], axis=0).astype(BF16)
    member = lanes((8, CELLS)) // 64 == rows((8, CELLS))
    shares = []
    for f in range(3):
        for y in range(4):
            line = jnp.where(member, full[f * 8 + y : f * 8 + y + 1], 0.0)
            line = (line[:, 0:128] + line[:, 128:256]) + (line[:, 256:384] + line[:, 384:512])
            shares.append(line + pltpu.roll(line, 64, 1))
    left = lanes((8, 128)) < 64
    marked = lanes((8, 128)) == 6
    for y in range(breadth):
        here = wtt_ref[36 + y : 37 + y] > 0
        for k in range(6):
            both = jnp.where(left, shares[2 * k], shares[2 * k + 1])
            sent[y * 8 : y * 8 + 8, 8 + k, :] = jnp.where(here, both, 0.0)
        last = jnp.where(marked, wtt_ref[35:36], jnp.broadcast_to(tensor, (8, 128)))
        none = jnp.where(marked, -1.0, 0.0)
        sent[y * 8 : y * 8 + 8, 14, :] = jnp.where(here, last, none)
        sent[y * 8 : y * 8 + 8, 15, :] = jnp.zeros((8, 128), F32)
    last_x = lanes((32, CELLS)) % 64 == 63
    last_z = lanes((32, CELLS)) >= 448
    bias2 = jnp.zeros((32, 1), F32)
    dz2 = []
    for y in range(4):
        da2 = mxu(fwt_ref[y * 32 : y * 32 + 32, 0:32], df) + spread
        d = jnp.where(a2_ref[y * 32 : y * 32 + 32] > 0, da2, 0.0).astype(BF16)
        wide = d.astype(F32)
        bias2 = bias2 + jnp.sum(wide, axis=1, keepdims=True)
        next_x = jnp.where(last_x, 0.0, pltpu.roll(wide, CELLS - 1, 1))
        next_z = jnp.where(last_z, 0.0, pltpu.roll(wide, CELLS - 64, 1))
        both = jnp.where(last_z, 0.0, pltpu.roll(next_x, CELLS - 64, 1))
        d_ref[y * 128 : y * 128 + 32] = d
        d_ref[y * 128 + 32 : y * 128 + 64] = next_x.astype(BF16)
        d_ref[y * 128 + 64 : y * 128 + 96] = next_z.astype(BF16)
        d_ref[y * 128 + 96 : y * 128 + 128] = both.astype(BF16)
        dz2.append(d)
    d_ref[512:640] = jnp.zeros((128, CELLS), BF16)
    none = jnp.zeros((32, CELLS), BF16)
    second = jnp.zeros((BLOCK, 128), F32)
    for y in range(4):
        at = (2 * y + 1) * BLOCK
        da1 = mxu(wb_ref[...], d_ref[y * 128 : y * 128 + 256])
        short = mxu(wsb_ref[:, 0:32], dz2[y])
        da1 = jnp.concatenate([da1[0:16] + short, da1[16:128]], axis=0)
        for sub in range(2):
            act = a_ref[at + sub * BLOCK : at + sub * BLOCK + BLOCK]
            if sub == 0:
                sides = [none, dz2[y], none, none]
            else:
                sides = [dz2[y + 1] if y < 3 else none, none, dz2[y], none]
            second = second + mxu(act, jnp.concatenate(sides, axis=0), NT)
            on = jnp.concatenate([act[0:32], act[48:80]], axis=0) > 0
            dz1 = jnp.where(on, da1[sub * 64 : sub * 64 + 64], 0.0).astype(BF16)
            dz1_ref[(2 * y + sub) * 64 : (2 * y + sub) * 64 + 64] = dz1
    parts = mxu(dz1_ref[...], xcol, NT)
    place8 = lanes((64, 128)) % 8
    fold = jnp.zeros((64, 128), F32)
    tail = jnp.zeros((64, 1), F32)
    for y in range(8):
        part = parts[y * 64 : y * 64 + 64, 0:128]
        tail = tail + parts[y * 64 : y * 64 + 64, 128:129]
        if y == 0:
            part = jnp.where(place8 == 7, 0.0, part)
        if y == 7:
            part = jnp.where(place8 == 0, 0.0, part)
        if y != 1:
            part = pltpu.roll(part, (1 - y) % 128, 1)
        fold = fold + part
    first = jnp.zeros((16, 128), F32)
    first_bias = jnp.zeros((16, 1), F32)
    for px in range(2):
        for z in range(2):
            at, left = px * 32 + z * 16, z * 32 + px * 8
            part = fold[at : at + 16]
            first = first + (pltpu.roll(part, 128 - left, 1) if left else part)
            first_bias = first_bias + tail[at : at + 16]
    lane = lanes((1, 128))
    bias2 = jnp.where(lanes((32, 128)) == 0, bias2, pooled * pltpu.roll(dt, 1, 1))
    upright = jnp.concatenate(
        [
            jnp.where(lanes((16, 128)) == 127, first_bias, first),
            jnp.zeros((16, 128), F32),
            bias2,
            jnp.zeros((64, 128), F32),
        ],
        axis=0,
    )
    upright = jnp.transpose(upright)
    cross = mxu(df, a2, NT)
    same = lanes((32, 128)) // 32 == rows((32, 128)) % 8
    cross = jnp.where(same, cross, 0.0)
    cross = cross + pltpu.roll(cross, 64, 1)
    cross = cross + pltpu.roll(cross, 32, 1)
    flux_sum = jnp.sum(df.astype(F32), axis=1, keepdims=True)
    total[0:108] = second[0:108]
    for ky in range(3):
        total[ky * 36 : ky * 36 + 36, 96:128] = second[108:144, ky * 32 : ky * 32 + 32]
    low = lanes((8, 128)) < 16
    small = jnp.zeros((8, 128), F32)
    for g in range(8):
        at = (g // 3) * 32 + (g % 3) * 8
        part = jnp.where(low, upright[at : at + 8], 0.0)
        small = small + (pltpu.roll(part, 16 * g, 1) if g else part)
    total[108:111] = small[0:3]
    lines = jnp.concatenate(
        [
            jnp.sum(cross[f * 8 : f * 8 + 8], axis=0, keepdims=True) for f in range(3)
        ]
        + [jnp.zeros((5, 128), F32)],
        axis=0,
    )
    lane8, row8 = lanes((8, 128)), rows((8, 128))
    last = jnp.where(low, upright[80:88], 0.0)
    last = jnp.where((lane8 >= 32) & (lane8 < 64), lines, last)
    first_bias = pltpu.roll(jnp.where(lane < 16, upright[127:128], 0.0), 64, 1)
    second_bias = pltpu.roll(jnp.where((lane >= 32) & (lane < 64), upright[0:1], 0.0), 32, 1)
    bias_row = jnp.zeros((1, 128), F32)
    for f in range(3):
        sums = jnp.sum(flux_sum[f * 8 : f * 8 + 8], axis=0, keepdims=True)
        bias_row = jnp.where(lane == 96 + f, sums, bias_row)
    tensor_bias = pltpu.roll(jnp.where(lane < 32, dt, 0.0), 64, 1)
    last = last + jnp.where(row8 == 0, second_bias + bias_row, 0.0)
    last = last + jnp.where(row8 == 1, first_bias, 0.0)
    last = last + jnp.where(row8 == 2, tensor_bias, 0.0)
    total[111:114] = last[0:3]
    total[114:120] = upright[1:7]
    total[120:128] = jnp.zeros((8, 128), F32)
    upper = rows((8, 128)) < 4
    for t in range(0, ROWS, 8):
        block = total[t : t + 8]
        high = block.astype(BF16).astype(F32)
        low = block - high
        sent[t // 4, 0:8, :] = jnp.where(upper, high, pltpu.roll(low, 4, 0))
        sent[t // 4 + 1, 0:8, :] = jnp.where(upper, pltpu.roll(high, 4, 0), low)
    out_ref[...] = sent[...].astype(BF16)


def route(got_ref, out_ref, recs, *, breadth):
    recs[...] = got_ref[...].astype(F32)
    count = got_ref.shape[0]
    depth = out_ref.shape[0]
    parts = recs[0, 0:8, :]
    for p in range(1, count):
        parts = parts + recs[p, 0:8, :]
    upper = rows((8, 128)) < 4
    full = parts + pltpu.roll(parts, 4, 0)
    high = full.astype(BF16).astype(F32)
    share = jnp.where(upper, high, full - high)
    lane = lanes((count, 128))
    last = recs[:, 14, :]
    dest = jnp.sum(jnp.where(lane == 6, last, 0.0), axis=1, keepdims=True)
    mine = lax.axis_index("y")
    slot = (lane // 8 * breadth + mine) * 8 + lane % 8
    hit = jnp.where((dest == slot.astype(F32)) & (lane < 8 * depth), 1.0, 0.0)
    if count < 128:
        hit = jnp.concatenate([hit, jnp.zeros((128 - count, 128), F32)], axis=0)
    choose = jnp.transpose(hit)[0 : 8 * depth, 0:count].astype(BF16)
    layers = [mxu(choose, recs[:, 8 + k, :].astype(BF16)) for k in range(7)]
    for z in range(depth):
        tall = [share] + [layer[z * 8 : z * 8 + 8] for layer in layers]
        out_ref[z] = jnp.concatenate(tall, axis=0).astype(BF16)


def spread(got_ref, out_ref):
    parts = jnp.sum(got_ref[...].astype(F32)[:, 0:8, :], axis=0)
    share = parts[0:4] + parts[4:8]
    out_ref[...] = jnp.broadcast_to(share[None], out_ref.shape)


def place_records(got_ref, fp_ref, tp_ref):
    layers = got_ref[0].astype(F32)
    for z in range(1, got_ref.shape[0]):
        layers = layers + got_ref[z].astype(F32)
    for k in range(6):
        got = layers[8 + 8 * k : 16 + 8 * k].astype(BF16)
        f, y = (2 * k) // 4, (2 * k) % 4
        fp_ref[:, f, y, :] = got[:, 0:64]
        fp_ref[:, f, y + 1, :] = got[:, 64:128]
    tp_ref[...] = layers[56:64, 0:6].astype(BF16)


def finish(
    got_ref,
    g1_ref, b1_ref, g2_ref, b2_ref, gs_ref, gf_ref, bf_ref, gt_ref, bt_ref,
    total, second,
):
    for p in range(got_ref.shape[0]):
        total[p * 4 : p * 4 + 4] = got_ref[p]
    for kz in range(3):
        for ky in range(3):
            for kx in range(3):
                g = kz * 3 + kx
                at, to = (108 + ky, 16 * g) if g < 8 else (111 + ky, 0)
                g1_ref[(kz * 3 + ky) * 3 + kx] = total[at : at + 1, to : to + 16]
    for ky in range(3):
        second[0:108] = total[0:108, ky * 32 : ky * 32 + 32]
        second[108:144] = total[ky * 36 : ky * 36 + 36, 96:128]
        for s, kx in enumerate((1, 2, 0)):
            for zo, kz in enumerate((1, 2, 0)):
                to = ((kz * 3 + ky) * 3 + kx) * 16
                part = second[s * 48 + zo * 16 : s * 48 + zo * 16 + 16]
                g2_ref[to : to + 16] = part
                if ky == 1 and kx == 1 and kz == 1:
                    gs_ref[...] = part
    gf_ref[...] = total[111:114, 32:64]
    b2_ref[...] = total[111:112, 64:96]
    bf_ref[...] = total[111:112, 96:99]
    b1_ref[...] = total[112:113, 64:80]
    bt_ref[...] = total[113:114, 64:70]
    gt_ref[...] = total[114:120, 32:64]


SMEM = pl.BlockSpec(memory_space=pltpu.SMEM)
VMEM = pl.BlockSpec(memory_space=pltpu.VMEM)
MIB = 1024 * 1024


def run(kernel, name, scalars, arrays, outs, scratch=(), held=None, limit=16):
    return pl.pallas_call(
        kernel,
        out_shape=tuple(jax.ShapeDtypeStruct(*o[0:2]) for o in outs),
        in_specs=[SMEM] * len(scalars) + [held or VMEM] * len(arrays),
        out_specs=tuple(o[2] if len(o) > 2 else VMEM for o in outs),
        scratch_shapes=[pltpu.VMEM(*s) if isinstance(s, tuple) else s for s in scratch],
        compiler_params=pltpu.CompilerParams(vmem_limit_bytes=limit * MIB),
        name=name,
    )(*scalars, *arrays)


def exchange(block, axis):
    return lax.all_to_all(block, axis, 0, 0, tiled=True)


def on_device(
    volume, flux_target, tensor_target, dest,
    first_weight, first_bias, second_weight, second_bias, short_weight,
    flux_weight, flux_bias, tensor_weight, tensor_bias,
):
    depth, breadth, slabs = (lax.axis_size(a) for a in ("z", "y", "slab"))
    count = breadth * slabs
    records = 8 * depth * breadth
    flux_count = records * 3 * slabs * 4 * 64
    tensor_count = records * 6
    cell_count = slabs * 4 * 64
    place = lax.axis_index("slab").astype(jnp.int32).reshape(1)
    (mine,) = run(
        pack, "pack", [place], [volume, flux_target[:, :, 0]], [((8, 40, 128), BF16)],
        [((8, 2, 8, 128), BF16), ((8, 3, 4, 64), BF16), pltpu.SemaphoreType.DMA((2,))],
        pl.BlockSpec(memory_space=pl.ANY), 60,
    )
    record = exchange(mine, "slab")
    weights = run(
        functools.partial(prepare, breadth=breadth), "prepare", [place, dest, flux_bias],
        [
            jnp.transpose(first_weight[:, 0], (1, 2, 3, 0)),
            jnp.transpose(second_weight, (2, 3, 4, 1, 0)).reshape(432, 32),
            jnp.transpose(short_weight),
            flux_weight, tensor_weight,
            first_bias.reshape(1, 16), second_bias.reshape(1, 32), tensor_bias.reshape(1, 6),
            tensor_target,
        ],
        [
            ((512, 128), BF16), ((32, 512), BF16), ((128, 256), BF16), ((16, 128), BF16),
            ((32, 128), BF16), ((128, 128), BF16), ((128, 128), F32), ((40, 128), F32),
            ((256, CELLS), BF16),
        ],
        [((96, 128), F32), ((512, 128), F32)],
    )
    (terms,) = run(
        functools.partial(
            step, 2.0 / flux_count, 2.0 / tensor_count, float(cell_count), breadth=breadth
        ),
        "step", [], [record, *weights],
        [((count, 16, 128), BF16)],
        [
            ((9 * BLOCK, CELLS), BF16), ((128, CELLS), BF16), ((640, CELLS), BF16),
            ((CELLS, CELLS), BF16), ((ROWS, 128), F32), ((count, 16, 128), F32),
        ],
    )
    terms = exchange(terms, ("y", "slab"))
    (routed,) = run(
        functools.partial(route, breadth=breadth), "route", [], [terms],
        [((depth, LAYERS, 128), BF16)], [((count, 16, 128), F32)],
    )
    routed = exchange(routed, "z")
    (share,) = run(spread, "spread", [], [routed], [((count, 4, 128), F32)])
    total = exchange(share, ("y", "slab"))
    fp, tp = run(
        place_records, "place", [], [routed], [((8, 3, 4, 64), BF16), ((8, 6), BF16)]
    )
    g1, b1, g2, b2, gs, gf, bf, gt, bt = run(
        finish, "finish", [], [total],
        [
            ((27, 1, 16), F32), ((1, 16), F32), ((432, 32), F32), ((1, 32), F32),
            ((16, 32), F32), ((3, 32), F32), ((1, 3), F32), ((6, 32), F32), ((1, 6), F32),
        ],
        [((ROWS, 128), F32), ((BLOCK, 32), F32)],
    )
    return (
        fp[:, :, None],
        tp,
        jnp.transpose(g1.reshape(3, 3, 3, 1, 16), (4, 3, 0, 1, 2)),
        b1.reshape(16),
        jnp.transpose(g2.reshape(3, 3, 3, 16, 32), (4, 3, 0, 1, 2)),
        b2.reshape(32),
        jnp.transpose(gs),
        gf,
        bf.reshape(3),
        gt,
        bt.reshape(6),
    )


def solution(mesh):
    breadth = 4
    grid = mesh.devices.reshape(-1, breadth, mesh.shape["slab"])
    mesh = jax.sharding.Mesh(grid, ("z", "y", "slab"))
    groups = ("z", "y")
    cells = P(groups, "slab", None, None)
    fields = P(groups, None, "slab", None, None)
    return jax.shard_map(
        on_device,
        mesh=mesh,
        in_specs=(cells, fields, P(groups, None), P(groups)) + (P(),) * 9,
        out_specs=(fields, P(groups, None)) + (P(),) * 9,
        check_vma=False,
    )
```

time: 67.6 us -> 60.4 us (0.89)
  blocking collectives: 34.2 us -> 28.6 us
  local copies, waits for them, and re-layouts: 2.86 us -> 0.69 us
  waiting for transfers between devices: 7.75 us -> 9.86 us
  starting transfers between devices: 13.2 us -> 12.3 us
    all_to_all x2, blocking collectives: 34.2 us -> 28.6 us  [exchange(): return lax.all_to_all(block, axis, 0, 0, tiled=True)]
    unnamed x26 -> x22, local copies, waits for them, and re-layouts: 2.86 us -> 0.69 us
    all_to_all x2, waiting for transfers between devices: 7.75 us -> 9.86 us  [exchange(): return lax.all_to_all(block, axis, 0, 0, tiled=True)]
    all_to_all x2, starting transfers between devices: 13.2 us -> 12.3 us  [exchange(): return lax.all_to_all(block, axis, 0, 0, tiled=True)]
  transfers between devices with their start and end apart: 2 -> 2, of which waited for: 2 -> 2; matrix products, arithmetic and copies ran while one was open for 0% -> 0% of each run, Pallas kernels for 2% -> 3%
where the time goes in v2:
time: 60.4 us; the launch traced here: 60 us
  blocking collectives  28.6 us (47%)
  starting transfers between devices  12.3 us (20%)
  waiting for transfers between devices  9.86 us (16%)
  Pallas kernels  7.74 us (13%)
  between operations  0.82 us (1%)
  local copies, waits for them, and re-layouts  0.69 us (1%)
    all_to_all x2, blocking collectives, exchange(): return lax.all_to_all(block, axis, 0, 0, tiled=True)  28.6 us
    all_to_all x2, starting transfers between devices, exchange(): return lax.all_to_all(block, axis, 0, 0, tiled=True)  12.3 us
    all_to_all x2, waiting for transfers between devices, exchange(): return lax.all_to_all(block, axis, 0, 0, tiled=True)  9.86 us
    pallas_call x7, Pallas kernels, run(): pl.pallas_call(kernel, out_shape=tuple((jax.ShapeDtypeStruct(*o[0:2]) for...  7.74 us
  transfers between devices with their start and end apart: 2, of which 2 were waited for; matrix products, arithmetic and copies ran while one was open for 0% of the time, Pallas kernels for 3%

profile of v2, /device:TPU:1, one launch (start us, length us, event | category | flops | bytes accessed | tf_op | source)
XLA Modules:
  0.0 60.0 jit_solution(12994192990731590106)
XLA Ops:
  0.6 1.5 %pack.1 = bf16[8,40,128]{2,1,0:T(8,128)(2,1)} custom-call(s32[1]{0:T(128)} %bitcast.place_ref, bf16[8,2,8,128]{3,2,1,0:T(8,128)(2,1)} %vol_hbm.1, bf16[8,3,4,64]{3,2,1,0:T(4,128)(2,1)} %bitcast.32), custom_call_target="tpu_custom_call" | custom-call | tf_op jit(solution)/shard_map/pack/pallas_call | solution.py:456
  2.2 0.0 copy-start
  2.2 0.0 copy-start.2
  2.2 0.0 copy-start.4
  2.2 0.0 copy-start.5
  2.2 0.0 copy-start.6
  2.2 0.0 copy-start.7
  2.2 0.0 copy-start.8
  2.2 0.0 copy-start.9
  2.3 0.0 copy-start.10
  2.3 6.6 %all-to-all-start = ((bf16[8,40,128]{2,1,0:T(8,128)(2,1)}), bf16[8,40,128]{2,1,0:T(8,128)(2,1)S(1)}, u32[]{:S(2)}, u32[]{:S(2)}) async-start(bf16[8,40,128]{2,1,0:T(8,128)(2,1)} %pack.1), calls=%async_computation | async-start | bytes 163840 | tf_op jit(solution)/shard_map/all_to_all | solution.py:468
  8.9 0.0 copy-done
  8.9 0.0 copy-done.2
  8.9 0.0 copy-done.4
  8.9 0.0 copy-done.5
  8.9 0.0 copy-done.6
  9.0 0.0 copy-done.7
  9.0 0.0 copy-done.8
  9.0 0.0 copy-done.9
  9.0 0.6 %copy-done.1 = bf16[16,1,3,3,3]{0,4,3,2,1:T(4,128)(2,1)S(1)} copy-done((bf16[16,1,3,3,3]{0,4,3,2,1:T(4,128)(2,1)S(1)}, bf16[16,1,3,3,3]{0,4,3,2,1:T(4,128)(2,1)}, u32[]{:S(2)}) %copy-start.1) | copy-done | bytes 888
  9.6 0.0 copy-done.3
  9.6 1.0 %prepare.1 = (bf16[512,128]{1,0:T(8,128)(2,1)S(1)}, bf16[32,512]{1,0:T(8,128)(2,1)S(1)}, bf16[128,256]{1,0:T(8,128)(2,1)S(1)}, bf16[16,128]{1,0:T(8,128)(2,1)S(1...) custom-call(s32[1]{0:T(128)} %bitcast.place_ref, ...), custom_call_target="tpu_custom_call" | custom-call | tf_op jit(solution)/shard_map/prepare/pallas_call | solution.py:456
  10.7 3.2 %all-to-all-done.got_ref = bf16[8,40,128]{2,1,0:T(8,128)(2,1)S(1)} async-done(((bf16[8,40,128]{2,1,0:T(8,128)(2,1)}), bf16[8,40,128]{2,1,0:T(8,128)(2,1)S(1)}, u32[]{:S(2)}, u32[]{:S(2)}) %all-to-all-start) | async-done | bytes 81952 | tf_op jit(solution)/shard_map/all_to_all | solution.py:468
  13.8 2.6 %step.1 = bf16[32,16,128]{2,1,0:T(8,128)(2,1)S(1)} custom-call(bf16[8,40,128]{2,1,0:T(8,128)(2,1)S(1)} %all-to-all-done.got_ref, bf16[512,128]{1,0:T(8,128)(2,1)S(1)} %get-tuple-element.31.t1_ref, bf16[32,512]{1,0:T(8,128)(2,1)S(1)} %get-tuple-element.32.w2a_ref, bf16[128,256]{1,0:T(8,128)(2,1)S(1)} %get-tuple-element.33.wb_ref, ...), custom_call_target="tpu_custom_call" | custom-call | tf_op jit(solution)/shard_map/step/pallas_call | solution.py:456
  16.4 12.7 %all_to_all.20.got_ref = bf16[32,16,128]{2,1,0:T(8,128)(2,1)S(1)} all-to-all(bf16[32,16,128]{2,1,0:T(8,128)(2,1)S(1)} %step.1), channel_id=1, replica_groups=mesh['z'=8,'y'=4,'slab'=8] {'y','slab'}, dimensions={0} | all-to-all | bytes 262144 | tf_op jit(solution)/shard_map/all_to_all | solution.py:468
  29.2 0.3 route.1
  29.5 15.8 %all_to_all.21.got_ref = bf16[8,64,128]{2,1,0:T(8,128)(2,1)S(1)} all-to-all(bf16[8,64,128]{2,1,0:T(8,128)(2,1)S(1)} %route.1), channel_id=1, replica_groups=mesh['z'=8,'y'=4,'slab'=8] {'z'}, dimensions={0} | all-to-all | bytes 262144 | tf_op jit(solution)/shard_map/all_to_all | solution.py:468
  45.3 0.6 %spread.1 = f32[32,4,128]{2,1,0:T(4,128)} custom-call(bf16[8,64,128]{2,1,0:T(8,128)(2,1)S(1)} %all_to_all.21.got_ref), custom_call_target="tpu_custom_call" | custom-call | tf_op jit(solution)/shard_map/spread/pallas_call | solution.py:456
  46.0 5.7 %all-to-all-start.3 = ((f32[32,4,128]{2,1,0:T(4,128)}), f32[32,4,128]{2,1,0:T(4,128)S(1)}, u32[]{:S(2)}, u32[]{:S(2)}) async-start(f32[32,4,128]{2,1,0:T(4,128)} %spread.1), calls=%async_computation.3 | async-start | bytes 131072 | tf_op jit(solution)/shard_map/all_to_all | solution.py:468
  51.7 0.7 %place.1 = (bf16[8,3,4,64]{3,2,1,0:T(4,128)(2,1)}, bf16[8,6]{1,0:T(8,128)(2,1)}) custom-call(bf16[8,64,128]{2,1,0:T(8,128)(2,1)S(1)} %all_to_all.21.got_ref), custom_call_target="tpu_custom_call" | custom-call | tf_op jit(solution)/shard_map/place/pallas_call | solution.py:456
  52.4 6.7 %all-to-all-done.3.got_ref = f32[32,4,128]{2,1,0:T(4,128)S(1)} async-done(((f32[32,4,128]{2,1,0:T(4,128)}), f32[32,4,128]{2,1,0:T(4,128)S(1)}, u32[]{:S(2)}, u32[]{:S(2)}) %all-to-all-start.3) | async-done | bytes 65568 | tf_op jit(solution)/shard_map/all_to_all | solution.py:468
  59.1 0.9 %finish.1 = (f32[27,1,16]{2,1,0:T(1,128)}, f32[1,16]{1,0:T(1,128)}, f32[432,32]{1,0:T(8,128)}, f32[1,32]{1,0:T(1,128)}, f32[16,32]{1,0:T(8,128)}, /*index=5*/f32...) custom-call(f32[32,4,128]{2,1,0:T(4,128)S(1)} %all-to-all-done.3.got_ref), custom_call_target="tpu_custom_call" | custom-call | tf_op jit(solution)/shard_map/finish/pallas_call | solution.py:456
  (3 shorter events, 0.0 us)
Async XLA Ops:
  2.2 6.8 %copy-start = (bf16[32,16,3,3,3]{0,1,4,3,2:T(8,128)(2,1)S(1)}, bf16[32,16,3,3,3]{0,1,4,3,2:T(8,128)(2,1)}, u32[]{:S(2)}) copy-start(bf16[32,16,3,3,3]{0,1,4,3,2:T(8,128)(2,1)} %param.19) | copy-start | bytes 82948
  2.2 6.8 %copy-start.2 = (bf16[32,16]{0,1:T(8,128)(2,1)S(1)}, bf16[32,16]{0,1:T(8,128)(2,1)}, u32[]{:S(2)}) copy-start(bf16[32,16]{0,1:T(8,128)(2,1)} %param.21) | copy-start | bytes 3076
  2.2 6.7 %copy-start.4 = (bf16[8,6]{1,0:T(8,128)(2,1)S(1)}, bf16[8,6]{1,0:T(8,128)(2,1)}, u32[]{:S(2)}) copy-start(bf16[8,6]{1,0:T(8,128)(2,1)} %kt_ref.1) | copy-start | bytes 292
  2.2 6.7 %copy-start.5 = (bf16[3,32]{1,0:T(4,128)(2,1)S(1)}, bf16[3,32]{1,0:T(4,128)(2,1)}, u32[]{:S(2)}) copy-start(bf16[3,32]{1,0:T(4,128)(2,1)} %wf_ref.1) | copy-start | bytes 580
  2.2 6.7 %copy-start.6 = (s32[8]{0:T(128)S(1)}, s32[8]{0:T(128)}, u32[]{:S(2)}) copy-start(s32[8]{0:T(128)} %dest_ref.1) | copy-start | bytes 100
  2.2 6.7 %copy-start.7 = (f32[3]{0:T(128)S(1)}, f32[3]{0:T(128)}, u32[]{:S(2)}) copy-start(f32[3]{0:T(128)} %bf_ref.1) | copy-start | bytes 40
  2.2 6.7 %copy-start.8 = (f32[16]{0:T(128)S(1)}, f32[16]{0:T(128)}, u32[]{:S(2)}) copy-start(f32[16]{0:T(128)} %param.18) | copy-start | bytes 196
  2.2 6.7 %copy-start.9 = (f32[32]{0:T(128)S(1)}, f32[32]{0:T(128)}, u32[]{:S(2)}) copy-start(f32[32]{0:T(128)} %param.20) | copy-start | bytes 388
  2.3 6.7 %copy-start.10 = (f32[6]{0:T(128)S(1)}, f32[6]{0:T(128)}, u32[]{:S(2)}) copy-start(f32[6]{0:T(128)} %param.25) | copy-start | bytes 76
  2.3 11.6 %all-to-all-start = ((bf16[8,40,128]{2,1,0:T(8,128)(2,1)}), bf16[8,40,128]{2,1,0:T(8,128)(2,1)S(1)}, u32[]{:S(2)}, u32[]{:S(2)}) async-start(bf16[8,40,128]{2,1,0:T(8,128)(2,1)} %pack.1), calls=%async_computation | async-start | bytes 163840 | tf_op jit(solution)/shard_map/all_to_all | solution.py:468
  8.9 0.7 %copy-start.1 = (bf16[16,1,3,3,3]{0,4,3,2,1:T(4,128)(2,1)S(1)}, bf16[16,1,3,3,3]{0,4,3,2,1:T(4,128)(2,1)}, u32[]{:S(2)}) copy-start(bf16[16,1,3,3,3]{0,4,3,2,1:T(4,128)(2,1)} %param.17) | copy-start | bytes 2596
  8.9 0.7 %copy-start.3 = (bf16[6,32]{1,0:T(8,128)(2,1)S(1)}, bf16[6,32]{1,0:T(8,128)(2,1)}, u32[]{:S(2)}) copy-start(bf16[6,32]{1,0:T(8,128)(2,1)} %wt_ref.1) | copy-start | bytes 1156
  46.0 13.1 %all-to-all-start.3 = ((f32[32,4,128]{2,1,0:T(4,128)}), f32[32,4,128]{2,1,0:T(4,128)S(1)}, u32[]{:S(2)}, u32[]{:S(2)}) async-start(f32[32,4,128]{2,1,0:T(4,128)} %spread.1), calls=%async_computation.3 | async-start | bytes 131072 | tf_op jit(solution)/shard_map/all_to_all | solution.py:468

commit v3 on v2

--- a/solution.py
+++ b/solution.py
@@ -17,7 +17,8 @@
 CELLS = 512
 TAPS = 144
 ROWS = 128
-LAYERS = 64
+SENT = 24
+ROUTED = 40
 
 
 def mxu(a, b, dims=NN):
@@ -32,25 +33,26 @@
     return lax.broadcasted_iota(jnp.int32, shape, len(shape) - 2)
 
 
-def pack(place_ref, vol_hbm, ft_hbm, out_ref, vol_ref, ft_ref, done):
-    copies = [
-        pltpu.make_async_copy(vol_hbm, vol_ref, done.at[0]),
-        pltpu.make_async_copy(ft_hbm, ft_ref, done.at[1]),
-    ]
-    for copy in copies:
-        copy.start()
+def side_of(y):
+    return ((y + 1) // 2) % 2
+
+
+def pack(place_ref, vol_hbm, ft_hbm, out_ref, ft_ref, done):
+    planes = pltpu.make_async_copy(vol_hbm, out_ref.at[:, 0:2], done.at[0])
+    goals = pltpu.make_async_copy(ft_hbm, ft_ref, done.at[1])
+    goals.start()
+    planes.start()
     odd = place_ref[0] % 2 == 1
-    copies[0].wait()
-    for z in range(2):
-        out_ref[:, z * 8 : z * 8 + 8, :] = vol_ref[:, z]
-    copies[1].wait()
+    goals.wait()
     goal = ft_ref[...].astype(F32)
     none = jnp.zeros_like(goal)
     low = jnp.concatenate([goal, none], axis=3)
     high = jnp.concatenate([none, goal], axis=3)
     both = jnp.where(odd, high, low)
-    both = jnp.concatenate([both, jnp.zeros_like(both)], axis=2)
-    out_ref[:, 16:40, :] = both.reshape(8, 24, 128).astype(BF16)
+    out_ref[:, 2] = jnp.concatenate([both[:, 0], both[:, 1]], axis=1).astype(BF16)
+    rest = jnp.zeros((8, 4, 128), F32)
+    out_ref[:, 3] = jnp.concatenate([both[:, 2], rest], axis=1).astype(BF16)
+    planes.wait()
 
 
 def prepare(
@@ -58,7 +60,6 @@
     w1_ref, w2_ref, ws_ref, wf_ref, wt_ref, b1_ref, b2_ref, bt_ref, kt_ref,
     t1_ref, w2a_ref, wb_ref, wsb_ref, fw_ref, fwt_ref, cols_ref, wtt_ref, pick_ref,
     base, order,
-    *, breadth,
 ):
     r, c = rows((256, CELLS)), lanes((256, CELLS))
     x = 2 * (c % 64) - 1 + c // 128
@@ -141,16 +142,24 @@
     base[16:24, 0:6] = kt_ref[...].astype(F32)
     wtt_ref[32:40] = jnp.zeros((8, 128), F32)
     wtt_ref[32:33, 0:6] = bt_ref[...]
-    mine = rows((8, 128)) == place_ref[0]
+    place = place_ref[0]
+    mine = rows((8, 128)) == place
     wtt_ref[33:34] = jnp.sum(jnp.where(mine, base[16:24], 0.0), axis=0, keepdims=True)
-    dest = dest_ref[place_ref[0]]
+    dest = dest_ref[place]
+    group = jnp.maximum(dest, 0) // 8
     live = jnp.where(dest >= 0, 1.0, 0.0)
     wtt_ref[34:35] = jnp.broadcast_to(live, (1, 128))
     wtt_ref[35:36] = jnp.broadcast_to(dest.astype(F32), (1, 128))
-    across = (jnp.maximum(dest, 0) // 8) % breadth
-    for y in range(breadth):
-        here = jnp.where((dest >= 0) & (across == y), 1.0, 0.0)
-        wtt_ref[36 + y : 37 + y] = jnp.broadcast_to(here, (1, 128))
+    for t in range(2):
+        leads = side_of(lax.axis_index("yh") * 2 + t) == side_of(group % 4)
+        here = jnp.where((dest >= 0) & leads, 1.0, 0.0)
+        wtt_ref[36 + t : 37 + t] = jnp.broadcast_to(here, (1, 128))
+    rank = jnp.float32(0)
+    for e in range(8):
+        other = dest_ref[e]
+        twin = (other >= 0) & (jnp.maximum(other, 0) // 8 == group) & (e < place)
+        rank = jnp.where(twin, 1.0, rank)
+    wtt_ref[38:39] = jnp.broadcast_to(rank, (1, 128))
     row = rows((128, 1))
     bias = jnp.where(row < 8, bf_ref[0], jnp.where(row < 16, bf_ref[1], bf_ref[2]))
     cols_ref[:, 2:3] = bias
@@ -161,8 +170,7 @@
     got_ref,
     t1_ref, w2a_ref, wb_ref, wsb_ref, fw_ref, fwt_ref, cols_ref, wtt_ref, pick_ref,
     out_ref,
-    a_ref, a2_ref, d_ref, dz1_ref, total, sent,
-    *, breadth,
+    a_ref, a2_ref, d_ref, dz1_ref, total, extra, sent,
 ):
     live = wtt_ref[34:35, 0:1]
     empty = jnp.zeros((8, 128), F32)
@@ -170,8 +178,7 @@
     def plane(z):
         if z < 0 or z > 15:
             return empty
-        at = (z % 2) * 8
-        return got_ref[z // 2, at : at + 8, :].astype(F32)
+        return got_ref[z // 2, z % 2].astype(F32)
 
     low = jnp.concatenate([plane(4 * q - 1 + zi) for zi in range(4) for q in range(4)], axis=0)
     high = jnp.concatenate([plane(4 * q + 1 + zi) for zi in range(4) for q in range(4)], axis=0)
@@ -192,22 +199,22 @@
     lines.append(jnp.where(rows((16, CELLS)) == 0, 1.0, 0.0))
     xcol = jnp.concatenate(lines, axis=0).astype(BF16)
     b1 = jnp.concatenate([cols_ref[0:16, 0:1]] * 4, axis=0)
+    zero = jnp.zeros((), BF16)
     first_z = lanes((16, CELLS)) < 64
     first_x = lanes((48, CELLS)) % 64 == 0
     a_ref[0:BLOCK] = jnp.zeros((BLOCK, CELLS), BF16)
+    z1_all = mxu(t1_ref[...], xcol[0:128])
     for y in range(8):
-        z1 = mxu(t1_ref[y * 64 : y * 64 + 64], xcol[0:128]) + b1
+        z1 = z1_all[y * 64 : y * 64 + 64] + b1
         act = jnp.maximum(z1, 0.0).astype(BF16)
-        wide = act.astype(F32)
         at = (y + 1) * BLOCK
         for px in range(2):
-            moved = pltpu.roll(wide[px * 32 + 16 : px * 32 + 32], 64, 1)
-            moved = jnp.where(first_z, 0.0, moved)
+            moved = pltpu.roll(act[px * 32 + 16 : px * 32 + 32], 64, 1)
+            moved = jnp.where(first_z, zero, moved)
             a_ref[at + px * 48 : at + px * 48 + 32] = act[px * 32 : px * 32 + 32]
-            a_ref[at + px * 48 + 32 : at + px * 48 + 48] = moved.astype(BF16)
-        late = jnp.concatenate([wide[32:64], moved], axis=0)
-        late = jnp.where(first_x, 0.0, pltpu.roll(late, 1, 1))
-        a_ref[at + 96 : at + BLOCK] = late.astype(BF16)
+            a_ref[at + px * 48 + 32 : at + px * 48 + 48] = moved
+        late = jnp.concatenate([act[32:64], moved], axis=0)
+        a_ref[at + 96 : at + BLOCK] = jnp.where(first_x, zero, pltpu.roll(late, 1, 1))
     b2 = cols_ref[0:32, 1:2]
     pooled = jnp.zeros((32, 1), F32)
     for y in range(4):
@@ -226,13 +233,17 @@
     spread = jnp.sum(head * dt, axis=1, keepdims=True) / cell_count
     row = rows((24, 1))
     full = mxu(fw_ref[0:24], a2) + cols_ref[0:24, 2:3]
-    wanted = jnp.concatenate(
-        [
-            got_ref[2 * q, 16:40, :].astype(F32) + got_ref[2 * q + 1, 16:40, :].astype(F32)
-            for q in range(4)
-        ],
-        axis=1,
-    )
+    goals = [
+        jnp.concatenate(
+            [
+                got_ref[2 * q, 2 + h].astype(F32) + got_ref[2 * q + 1, 2 + h].astype(F32)
+                for q in range(4)
+            ],
+            axis=1,
+        )
+        for h in range(2)
+    ]
+    wanted = jnp.concatenate([goals[0], pltpu.roll(goals[0], 4, 0), goals[1]], axis=0)
     diff = flux_scale * (full - wanted) * live
     df = jnp.where(row % 8 < 4, diff, 0.0)
     df = jnp.concatenate([df, jnp.zeros((8, CELLS), F32)], axis=0).astype(BF16)
@@ -244,16 +255,22 @@
             line = (line[:, 0:128] + line[:, 128:256]) + (line[:, 256:384] + line[:, 384:512])
             shares.append(line + pltpu.roll(line, 64, 1))
     left = lanes((8, 128)) < 64
-    marked = lanes((8, 128)) == 6
-    for y in range(breadth):
-        here = wtt_ref[36 + y : 37 + y] > 0
+    lane8 = lanes((8, 128))
+    dest = wtt_ref[35:36]
+    slot = dest - 8.0 * jnp.floor(dest / 8.0) + 1.0
+    last = jnp.where(lane8 < 6, jnp.broadcast_to(tensor, (8, 128)), 0.0)
+    last = jnp.where(lane8 == 6, dest, last)
+    last = jnp.where(lane8 == 7, wtt_ref[38:39], last)
+    last = jnp.where(lane8 == 8, slot, last)
+    for t in range(2):
+        here = wtt_ref[36 + t : 37 + t] > 0
         for k in range(6):
             both = jnp.where(left, shares[2 * k], shares[2 * k + 1])
-            sent[y * 8 : y * 8 + 8, 8 + k, :] = jnp.where(here, both, 0.0)
-        last = jnp.where(marked, wtt_ref[35:36], jnp.broadcast_to(tensor, (8, 128)))
-        none = jnp.where(marked, -1.0, 0.0)
-        sent[y * 8 : y * 8 + 8, 14, :] = jnp.where(here, last, none)
-        sent[y * 8 : y * 8 + 8, 15, :] = jnp.zeros((8, 128), F32)
+            sent[t * 8 : t * 8 + 8, 16 + k, :] = jnp.where(here, both, 0.0)
+        sent[t * 8 : t * 8 + 8, 22, :] = jnp.where(
+            here, last, jnp.where(lane8 == 6, -1.0, 0.0)
+        )
+        sent[t * 8 : t * 8 + 8, 23, :] = jnp.zeros((8, 128), F32)
     last_x = lanes((32, CELLS)) % 64 == 63
     last_z = lanes((32, CELLS)) >= 448
     bias2 = jnp.zeros((32, 1), F32)
@@ -263,13 +280,13 @@
         d = jnp.where(a2_ref[y * 32 : y * 32 + 32] > 0, da2, 0.0).astype(BF16)
         wide = d.astype(F32)
         bias2 = bias2 + jnp.sum(wide, axis=1, keepdims=True)
-        next_x = jnp.where(last_x, 0.0, pltpu.roll(wide, CELLS - 1, 1))
-        next_z = jnp.where(last_z, 0.0, pltpu.roll(wide, CELLS - 64, 1))
-        both = jnp.where(last_z, 0.0, pltpu.roll(next_x, CELLS - 64, 1))
+        next_x = jnp.where(last_x, zero, pltpu.roll(d, CELLS - 1, 1))
+        next_z = jnp.where(last_z, zero, pltpu.roll(d, CELLS - 64, 1))
+        both = jnp.where(last_z, zero, pltpu.roll(next_x, CELLS - 64, 1))
         d_ref[y * 128 : y * 128 + 32] = d
-        d_ref[y * 128 + 32 : y * 128 + 64] = next_x.astype(BF16)
-        d_ref[y * 128 + 64 : y * 128 + 96] = next_z.astype(BF16)
-        d_ref[y * 128 + 96 : y * 128 + 128] = both.astype(BF16)
+        d_ref[y * 128 + 32 : y * 128 + 64] = next_x
+        d_ref[y * 128 + 64 : y * 128 + 96] = next_z
+        d_ref[y * 128 + 96 : y * 128 + 128] = both
         dz2.append(d)
     d_ref[512:640] = jnp.zeros((128, CELLS), BF16)
     none = jnp.zeros((32, CELLS), BF16)
@@ -329,109 +346,134 @@
     cross = cross + pltpu.roll(cross, 64, 1)
     cross = cross + pltpu.roll(cross, 32, 1)
     flux_sum = jnp.sum(df.astype(F32), axis=1, keepdims=True)
-    total[0:108] = second[0:108]
     for ky in range(3):
-        total[ky * 36 : ky * 36 + 36, 96:128] = second[108:144, ky * 32 : ky * 32 + 32]
-    low = lanes((8, 128)) < 16
-    small = jnp.zeros((8, 128), F32)
-    for g in range(8):
-        at = (g // 3) * 32 + (g % 3) * 8
-        part = jnp.where(low, upright[at : at + 8], 0.0)
-        small = small + (pltpu.roll(part, 16 * g, 1) if g else part)
-    total[108:111] = small[0:3]
-    lines = jnp.concatenate(
-        [
-            jnp.sum(cross[f * 8 : f * 8 + 8], axis=0, keepdims=True) for f in range(3)
-        ]
-        + [jnp.zeros((5, 128), F32)],
-        axis=0,
-    )
-    lane8, row8 = lanes((8, 128)), rows((8, 128))
-    last = jnp.where(low, upright[80:88], 0.0)
-    last = jnp.where((lane8 >= 32) & (lane8 < 64), lines, last)
-    first_bias = pltpu.roll(jnp.where(lane < 16, upright[127:128], 0.0), 64, 1)
-    second_bias = pltpu.roll(jnp.where((lane >= 32) & (lane < 64), upright[0:1], 0.0), 32, 1)
+        tail_block = pltpu.roll(second[128:144], (96 - ky * 32) % 128, 1)
+        extra[ky * 16 : ky * 16 + 16] = tail_block
+    lane8 = lanes((8, 128))
+    for i in range(5):
+        pair = jnp.zeros((8, 128), F32)
+        for h in range(2 if i < 4 else 1):
+            g = 2 * i + h
+            at = (g // 3) * 32 + (g % 3) * 8
+            part = jnp.where(lane8 < 16, upright[at : at + 8], 0.0)
+            pair = pair + pltpu.roll(part, 96 + 16 * h, 1)
+        extra[48 + 3 * i : 51 + 3 * i] = pair[0:3]
     bias_row = jnp.zeros((1, 128), F32)
     for f in range(3):
+        extra[63 + f : 64 + f] = jnp.sum(cross[f * 8 : f * 8 + 8], axis=0, keepdims=True)
         sums = jnp.sum(flux_sum[f * 8 : f * 8 + 8], axis=0, keepdims=True)
-        bias_row = jnp.where(lane == 96 + f, sums, bias_row)
-    tensor_bias = pltpu.roll(jnp.where(lane < 32, dt, 0.0), 64, 1)
-    last = last + jnp.where(row8 == 0, second_bias + bias_row, 0.0)
-    last = last + jnp.where(row8 == 1, first_bias, 0.0)
-    last = last + jnp.where(row8 == 2, tensor_bias, 0.0)
-    total[111:114] = last[0:3]
-    total[114:120] = upright[1:7]
-    total[120:128] = jnp.zeros((8, 128), F32)
-    upper = rows((8, 128)) < 4
-    for t in range(0, ROWS, 8):
-        block = total[t : t + 8]
+        bias_row = jnp.where(lane == 112 + f, sums, bias_row)
+    extra[66:67] = pltpu.roll(upright[0:1], 64, 1)
+    first_row = pltpu.roll(jnp.where(lane < 16, upright[127:128], 0.0), 96, 1)
+    tensor_row = pltpu.roll(jnp.where(lane < 6, dt, 0.0), 116, 1)
+    extra[67:68] = first_row + bias_row + tensor_row
+    extra[68:74] = pltpu.roll(upright[0:8], 64, 1)[1:7]
+    extra[74:112] = jnp.zeros((38, 128), F32)
+    rest = lane8 >= 96
+    swap = lax.axis_index("yh") * 8
+    for t in range(16):
+        block = second[t * 8 : t * 8 + 8]
+        total[t * 8 : t * 8 + 8] = jnp.where(rest, 0.0, block)
+        total[t * 8 : t * 8 + 7] = jnp.where(
+            rest[0:7], extra[t * 7 : t * 7 + 7], block[0:7]
+        )
+        block = total[t * 8 : t * 8 + 8]
         high = block.astype(BF16).astype(F32)
-        low = block - high
-        sent[t // 4, 0:8, :] = jnp.where(upper, high, pltpu.roll(low, 4, 0))
-        sent[t // 4 + 1, 0:8, :] = jnp.where(upper, pltpu.roll(high, 4, 0), low)
+        to = lax.rem(t + swap, 16)
+        sent[to, 0:8, :] = high
+        sent[to, 8:16, :] = block - high
     out_ref[...] = sent[...].astype(BF16)
 
 
-def route(got_ref, out_ref, recs, *, breadth):
+def route(got_ref, out_ref, recs):
     recs[...] = got_ref[...].astype(F32)
     count = got_ref.shape[0]
-    depth = out_ref.shape[0]
-    parts = recs[0, 0:8, :]
+    full = recs[0, 0:8, :] + recs[0, 8:16, :]
     for p in range(1, count):
-        parts = parts + recs[p, 0:8, :]
-    upper = rows((8, 128)) < 4
-    full = parts + pltpu.roll(parts, 4, 0)
+        full = full + (recs[p, 0:8, :] + recs[p, 8:16, :])
     high = full.astype(BF16).astype(F32)
-    share = jnp.where(upper, high, full - high)
+    low = full - high
+    peers = out_ref.shape[0]
     lane = lanes((count, 128))
-    last = recs[:, 14, :]
-    dest = jnp.sum(jnp.where(lane == 6, last, 0.0), axis=1, keepdims=True)
-    mine = lax.axis_index("y")
-    slot = (lane // 8 * breadth + mine) * 8 + lane % 8
-    hit = jnp.where((dest == slot.astype(F32)) & (lane < 8 * depth), 1.0, 0.0)
-    if count < 128:
-        hit = jnp.concatenate([hit, jnp.zeros((128 - count, 128), F32)], axis=0)
-    choose = jnp.transpose(hit)[0 : 8 * depth, 0:count].astype(BF16)
-    layers = [mxu(choose, recs[:, 8 + k, :].astype(BF16)) for k in range(7)]
-    for z in range(depth):
-        tall = [share] + [layer[z * 8 : z * 8 + 8] for layer in layers]
-        out_ref[z] = jnp.concatenate(tall, axis=0).astype(BF16)
+    last = recs[:, 22, :]
+    dest = jnp.sum(jnp.where(lane == 6, last, 0.0), axis=1, keepdims=True).astype(jnp.int32)
+    rank = jnp.sum(jnp.where(lane == 7, last, 0.0), axis=1, keepdims=True).astype(jnp.int32)
+    side = side_of(lax.axis_index("yh") * 2 + lax.axis_index("yl"))
+    peer = lane // 4
+    group = (peer // 2) * 4 + jnp.where(peer % 2 == 0, side, 3 - side)
+    seat = (rows((count, 128)) // 8) * 2 + rank
+    right = (dest >= group * 8) & (dest < group * 8 + 8) & (seat == lane % 4)
+    hit = jnp.where(right & (peer < peers), 1.0, 0.0)
+    hit = jnp.concatenate([hit, jnp.zeros((128 - count, 128), F32)], axis=0)
+    choose = jnp.transpose(hit)[0 : 4 * peers, 0:count].astype(BF16)
+    layers = [mxu(choose, recs[:, 16 + k, :].astype(BF16)) for k in range(6)]
+    marks = mxu(choose, last.astype(BF16))
+    marks = jnp.where(lanes((4 * peers, 128)) < 16, marks, 0.0)
+    marks = [pltpu.roll(marks, 96, 1), pltpu.roll(marks, 112, 1)]
+    row8, lane8 = rows((8, 128)), lanes((8, 128))
+    upper, spare = row8 < 4, (row8 == 7) & (lane8 >= 96)
+    for i in range(peers):
+        tall = []
+        for h, part in enumerate((high, low)):
+            at = 4 * i + 2 * h
+            seats = marks[0][at : at + 1] + marks[1][at + 1 : at + 2]
+            tall.append(jnp.where(spare, seats, part))
+        at = (i // 2) * 8
+        for m in range(3):
+            even, odd = layers[2 * m][at : at + 8], layers[2 * m + 1][at : at + 8]
+            if i % 2 == 0:
+                tall.append(jnp.where(upper, even, pltpu.roll(odd, 4, 0)))
+            else:
+                tall.append(jnp.where(upper, pltpu.roll(even, 4, 0), odd))
+        out_ref[i] = jnp.concatenate(tall, axis=0).astype(BF16)
 
 
 def spread(got_ref, out_ref):
-    parts = jnp.sum(got_ref[...].astype(F32)[:, 0:8, :], axis=0)
-    share = parts[0:4] + parts[4:8]
+    parts = jnp.sum(got_ref[:, 0:16, :].astype(F32), axis=0)
+    share = parts[0:8] + parts[8:16]
     out_ref[...] = jnp.broadcast_to(share[None], out_ref.shape)
 
 
-def place_records(got_ref, fp_ref, tp_ref):
-    layers = got_ref[0].astype(F32)
-    for z in range(1, got_ref.shape[0]):
-        layers = layers + got_ref[z].astype(F32)
+def place_records(got_ref, fp_ref, tp_ref, recs):
+    recs[...] = got_ref[...].astype(F32)
+    count = got_ref.shape[0]
+    marks = [
+        pltpu.roll(recs[:, 7 + 8 * (j // 2), :], 32 - 16 * (j % 2), 1) for j in range(4)
+    ]
+    marks = jnp.concatenate(marks, axis=0)
+    lane = lanes((4 * count, 128))
+    slot = jnp.sum(jnp.where(lane == 8, marks, 0.0), axis=1, keepdims=True) - 1.0
+    hit = jnp.where((slot == lane.astype(F32)) & (lane < 8), 1.0, 0.0)
+    hit = jnp.concatenate([hit, jnp.zeros((128 - 4 * count, 128), F32)], axis=0)
+    choose = jnp.transpose(hit)[0:8, 0 : 4 * count].astype(BF16)
     for k in range(6):
-        got = layers[8 + 8 * k : 16 + 8 * k].astype(BF16)
+        held = jnp.concatenate([recs[:, 16 + 4 * k + j, :] for j in range(4)], axis=0)
+        got = mxu(choose, held.astype(BF16)).astype(BF16)
         f, y = (2 * k) // 4, (2 * k) % 4
         fp_ref[:, f, y, :] = got[:, 0:64]
         fp_ref[:, f, y + 1, :] = got[:, 64:128]
-    tp_ref[...] = layers[56:64, 0:6].astype(BF16)
+    tp_ref[...] = mxu(choose, marks.astype(BF16))[:, 0:6].astype(BF16)
 
 
 def finish(
     got_ref,
     g1_ref, b1_ref, g2_ref, b2_ref, gs_ref, gf_ref, bf_ref, gt_ref, bt_ref,
-    total, second,
+    total, extra, second,
 ):
-    for p in range(got_ref.shape[0]):
-        total[p * 4 : p * 4 + 4] = got_ref[p]
+    swap = lax.axis_index("yh") * 8
+    for p in range(16):
+        block = got_ref[lax.rem(p + swap, 16)]
+        total[p * 8 : p * 8 + 8] = block
+        extra[p * 7 : p * 7 + 7] = block[0:7, 96:128]
     for kz in range(3):
         for ky in range(3):
             for kx in range(3):
                 g = kz * 3 + kx
-                at, to = (108 + ky, 16 * g) if g < 8 else (111 + ky, 0)
-                g1_ref[(kz * 3 + ky) * 3 + kx] = total[at : at + 1, to : to + 16]
+                at, to = 48 + 3 * (g // 2) + ky, 16 * (g % 2)
+                g1_ref[(kz * 3 + ky) * 3 + kx] = extra[at : at + 1, to : to + 16]
     for ky in range(3):
-        second[0:108] = total[0:108, ky * 32 : ky * 32 + 32]
-        second[108:144] = total[ky * 36 : ky * 36 + 36, 96:128]
+        second[0:128] = total[0:128, ky * 32 : ky * 32 + 32]
+        second[128:144] = extra[ky * 16 : ky * 16 + 16]
         for s, kx in enumerate((1, 2, 0)):
             for zo, kz in enumerate((1, 2, 0)):
                 to = ((kz * 3 + ky) * 3 + kx) * 16
@@ -439,12 +481,12 @@
                 g2_ref[to : to + 16] = part
                 if ky == 1 and kx == 1 and kz == 1:
                     gs_ref[...] = part
-    gf_ref[...] = total[111:114, 32:64]
-    b2_ref[...] = total[111:112, 64:96]
-    bf_ref[...] = total[111:112, 96:99]
-    b1_ref[...] = total[112:113, 64:80]
-    bt_ref[...] = total[113:114, 64:70]
-    gt_ref[...] = total[114:120, 32:64]
+    gf_ref[...] = extra[63:66]
+    b2_ref[...] = extra[66:67]
+    b1_ref[...] = extra[67:68, 0:16]
+    bf_ref[...] = extra[67:68, 16:19]
+    bt_ref[...] = extra[67:68, 20:26]
+    gt_ref[...] = extra[68:74]
 
 
 SMEM = pl.BlockSpec(memory_space=pltpu.SMEM)
@@ -464,8 +506,8 @@
     )(*scalars, *arrays)
 
 
-def exchange(block, axis):
-    return lax.all_to_all(block, axis, 0, 0, tiled=True)
+def exchange(block, axis, groups=None):
+    return lax.all_to_all(block, axis, 0, 0, tiled=True, axis_index_groups=groups)
 
 
 def on_device(
@@ -473,21 +515,22 @@
     first_weight, first_bias, second_weight, second_bias, short_weight,
     flux_weight, flux_bias, tensor_weight, tensor_bias,
 ):
-    depth, breadth, slabs = (lax.axis_size(a) for a in ("z", "y", "slab"))
-    count = breadth * slabs
-    records = 8 * depth * breadth
+    depth, slabs = lax.axis_size("z"), lax.axis_size("slab")
+    near, far = 2 * slabs, 2 * depth
+    lines = [[z * 4 + y for z in range(depth) for y in pair] for pair in ((0, 3), (1, 2))]
+    records = 8 * depth * 4
     flux_count = records * 3 * slabs * 4 * 64
     tensor_count = records * 6
     cell_count = slabs * 4 * 64
     place = lax.axis_index("slab").astype(jnp.int32).reshape(1)
     (mine,) = run(
-        pack, "pack", [place], [volume, flux_target[:, :, 0]], [((8, 40, 128), BF16)],
-        [((8, 2, 8, 128), BF16), ((8, 3, 4, 64), BF16), pltpu.SemaphoreType.DMA((2,))],
+        pack, "pack", [place], [volume, flux_target[:, :, 0]], [((8, 4, 8, 128), BF16)],
+        [((8, 3, 4, 64), BF16), pltpu.SemaphoreType.DMA((2,))],
         pl.BlockSpec(memory_space=pl.ANY), 60,
     )
     record = exchange(mine, "slab")
     weights = run(
-        functools.partial(prepare, breadth=breadth), "prepare", [place, dest, flux_bias],
+        prepare, "prepare", [place, dest, flux_bias],
         [
             jnp.transpose(first_weight[:, 0], (1, 2, 3, 0)),
             jnp.transpose(second_weight, (2, 3, 4, 1, 0)).reshape(432, 32),
@@ -504,26 +547,25 @@
         [((96, 128), F32), ((512, 128), F32)],
     )
     (terms,) = run(
-        functools.partial(
-            step, 2.0 / flux_count, 2.0 / tensor_count, float(cell_count), breadth=breadth
-        ),
-        "step", [], [record, *weights],
-        [((count, 16, 128), BF16)],
+        functools.partial(step, 2.0 / flux_count, 2.0 / tensor_count, float(cell_count)),
+        "step", [], [record, *weights], [((near, SENT, 128), BF16)],
         [
             ((9 * BLOCK, CELLS), BF16), ((128, CELLS), BF16), ((640, CELLS), BF16),
-            ((CELLS, CELLS), BF16), ((ROWS, 128), F32), ((count, 16, 128), F32),
+            ((CELLS, CELLS), BF16), ((ROWS, 128), F32), ((112, 128), F32),
+            ((near, SENT, 128), F32),
         ],
     )
-    terms = exchange(terms, ("y", "slab"))
+    terms = exchange(terms, ("yl", "slab"))
     (routed,) = run(
-        functools.partial(route, breadth=breadth), "route", [], [terms],
-        [((depth, LAYERS, 128), BF16)], [((count, 16, 128), F32)],
-    )
-    routed = exchange(routed, "z")
-    (share,) = run(spread, "spread", [], [routed], [((count, 4, 128), F32)])
-    total = exchange(share, ("y", "slab"))
+        route, "route", [], [terms], [((far, ROUTED, 128), BF16)],
+        [((near, SENT, 128), F32)],
+    )
+    routed = exchange(routed, ("z", "yh", "yl"), lines)
+    (share,) = run(spread, "spread", [], [routed], [((near, 8, 128), F32)])
+    total = exchange(share, ("yl", "slab"))
     fp, tp = run(
-        place_records, "place", [], [routed], [((8, 3, 4, 64), BF16), ((8, 6), BF16)]
+        place_records, "place", [], [routed], [((8, 3, 4, 64), BF16), ((8, 6), BF16)],
+        [((far, ROUTED, 128), F32)],
     )
     g1, b1, g2, b2, gs, gf, bf, gt, bt = run(
         finish, "finish", [], [total],
@@ -531,7 +573,7 @@
             ((27, 1, 16), F32), ((1, 16), F32), ((432, 32), F32), ((1, 32), F32),
             ((16, 32), F32), ((3, 32), F32), ((1, 3), F32), ((6, 32), F32), ((1, 6), F32),
         ],
-        [((ROWS, 128), F32), ((BLOCK, 32), F32)],
+        [((ROWS, 128), F32), ((112, 32), F32), ((BLOCK, 32), F32)],
     )
     return (
         fp[:, :, None],
@@ -549,10 +591,9 @@
 
 
 def solution(mesh):
-    breadth = 4
-    grid = mesh.devices.reshape(-1, breadth, mesh.shape["slab"])
-    mesh = jax.sharding.Mesh(grid, ("z", "y", "slab"))
-    groups = ("z", "y")
+    grid = mesh.devices.reshape(-1, 2, 2, mesh.shape["slab"])
+    mesh = jax.sharding.Mesh(grid, ("z", "yh", "yl", "slab"))
+    groups = ("z", "yh", "yl")
     cells = P(groups, "slab", None, None)
     fields = P(groups, None, "slab", None, None)
     return jax.shard_map(

time: 60.4 us -> 59.1 us (0.978)
  waiting for transfers between devices: 9.86 us -> 7.86 us
    all_to_all x2, waiting for transfers between devices: 9.86 us -> 7.86 us  [exchange(): lax.all_to_all(block, axis, 0, 0, tiled=True, axis_index_groups=groups)]
  transfers between devices with their start and end apart: 2 -> 2, of which waited for: 2 -> 2; matrix products, arithmetic and copies ran while one was open for 0% -> 0% of each run, Pallas kernels for 3% -> 4%
where the time goes in v3:
time: 59.1 us; the launch traced here: 58.7 us
  blocking collectives  29.2 us (49%)
  starting transfers between devices  12 us (20%)
  Pallas kernels  8.11 us (14%)
  waiting for transfers between devices  7.86 us (13%)
  between operations  0.82 us (1%)
  local copies, waits for them, and re-layouts  0.69 us (1%)
    all_to_all x2, blocking collectives, exchange(): lax.all_to_all(block, axis, 0, 0, tiled=True, axis_index_groups=groups)  29.2 us
    all_to_all x2, starting transfers between devices, exchange(): lax.all_to_all(block, axis, 0, 0, tiled=True, axis_index_groups=groups)  12 us
    pallas_call x7, Pallas kernels, run(): pl.pallas_call(kernel, out_shape=tuple((jax.ShapeDtypeStruct(*o[0:2]) for...  8.11 us
    all_to_all x2, waiting for transfers between devices, exchange(): lax.all_to_all(block, axis, 0, 0, tiled=True, axis_index_groups=groups)  7.86 us
  transfers between devices with their start and end apart: 2, of which 2 were waited for; matrix products, arithmetic and copies ran while one was open for 0% of the time, Pallas kernels for 4%

profile of v3, /device:TPU:1, one launch (start us, length us, event | category | flops | bytes accessed | tf_op | source)
XLA Modules:
  0.0 58.7 jit_solution(7905488464029016214)
XLA Ops:
  0.6 0.0 copy-start
  0.7 1.5 %pack.1 = bf16[8,4,8,128]{3,2,1,0:T(8,128)(2,1)} custom-call(s32[1]{0:T(128)} %bitcast.place_ref, bf16[8,2,8,128]{3,2,1,0:T(8,128)(2,1)} %vol_hbm.1, bf16[8,3,4,64]{3,2,1,0:T(4,128)(2,1)} %bitcast.32), custom_call_target="tpu_custom_call" | custom-call | tf_op jit(solution)/shard_map/pack/pallas_call | solution.py:498
  2.2 0.0 copy-start.2
  2.2 0.0 copy-start.4
  2.2 0.0 copy-start.5
  2.2 0.0 copy-start.6
  2.2 0.0 copy-start.7
  2.2 0.0 copy-start.8
  2.2 0.0 copy-start.9
  2.3 0.0 copy-start.10
  2.3 6.6 %all-to-all-start = ((bf16[8,4,8,128]{3,2,1,0:T(8,128)(2,1)}), bf16[8,4,8,128]{3,2,1,0:T(8,128)(2,1)S(1)}, u32[]{:S(2)}, u32[]{:S(2)}) async-start(bf16[8,4,8,128]{3,2,1,0:T(8,128)(2,1)} %pack.1), calls=%async_computation | async-start | bytes 131072 | tf_op jit(solution)/shard_map/all_to_all | solution.py:510
  8.9 0.0 copy-done
  8.9 0.0 copy-done.2
  8.9 0.0 copy-done.4
  8.9 0.0 copy-done.5
  8.9 0.0 copy-done.6
  9.0 0.0 copy-done.7
  9.0 0.0 copy-done.8
  9.0 0.0 copy-done.9
  9.0 0.6 %copy-done.1 = bf16[16,1,3,3,3]{0,4,3,2,1:T(4,128)(2,1)S(1)} copy-done((bf16[16,1,3,3,3]{0,4,3,2,1:T(4,128)(2,1)S(1)}, bf16[16,1,3,3,3]{0,4,3,2,1:T(4,128)(2,1)}, u32[]{:S(2)}) %copy-start.1) | copy-done | bytes 888
  9.6 0.0 copy-done.3
  9.6 1.1 %prepare.1 = (bf16[512,128]{1,0:T(8,128)(2,1)S(1)}, bf16[32,512]{1,0:T(8,128)(2,1)S(1)}, bf16[128,256]{1,0:T(8,128)(2,1)S(1)}, bf16[16,128]{1,0:T(8,128)(2,1)S(1...) custom-call(s32[1]{0:T(128)} %bitcast.place_ref, ...), custom_call_target="tpu_custom_call" | custom-call | tf_op jit(solution)/shard_map/prepare/pallas_call | solution.py:498
  10.7 3.1 %all-to-all-done.got_ref = bf16[8,4,8,128]{3,2,1,0:T(8,128)(2,1)S(1)} async-done(((bf16[8,4,8,128]{3,2,1,0:T(8,128)(2,1)}), bf16[8,4,8,128]{3,2,1,0:T(8,128)(2,1)S(1)}, u32[]{:S(2)}, u32[]{:S(2)}) %all-to-all-start) | async-done | bytes 65568 | tf_op jit(solution)/shard_map/all_to_all | solution.py:510
  13.8 2.5 %step.1 = bf16[16,24,128]{2,1,0:T(8,128)(2,1)S(1)} custom-call(bf16[8,4,8,128]{3,2,1,0:T(8,128)(2,1)S(1)} %all-to-all-done.got_ref, bf16[512,128]{1,0:T(8,128)(2,1)S(1)} %get-tuple-element.31.t1_ref, bf16[32,512]{1,0:T(8,128)(2,1)S(1)} %get-tuple-element.32.w2a_ref, bf16[128,256]{1,0:T(8,128)(2,1)S(1)} %get-tuple-element.33.wb_ref, ...), custom_call_target="tpu_custom_call" | custom-call | tf_op jit(solution)/shard_map/step/pallas_call | solution.py:498
  16.3 9.2 %all_to_all.20.got_ref = bf16[16,24,128]{2,1,0:T(8,128)(2,1)S(1)} all-to-all(bf16[16,24,128]{2,1,0:T(8,128)(2,1)S(1)} %step.1), channel_id=1, replica_groups=mesh['z'=8,'yh'=2,'yl'=2,'slab'=8] {'yl','slab'}, dimensions={0} | all-to-all | bytes 196608 | tf_op jit(solution)/shard_map/all_to_all | solution.py:510
  25.5 0.4 route.1
  25.9 20.0 %all_to_all.21.got_ref = bf16[16,40,128]{2,1,0:T(8,128)(2,1)S(1)} all-to-all(bf16[16,40,128]{2,1,0:T(8,128)(2,1)S(1)} %route.1), channel_id=1, replica_groups={{0,24,32,56,64,88,96,120,128,152,160,184,192,216,224,248},{8,16,40,48,7..., dimensions={0} | all-to-all | bytes 327680 | tf_op jit(solution)/shard_map/all_to_all | solution.py:510
  45.9 0.7 %spread.1 = f32[16,8,128]{2,1,0:T(8,128)} custom-call(bf16[16,40,128]{2,1,0:T(8,128)(2,1)S(1)} %all_to_all.21.got_ref), custom_call_target="tpu_custom_call" | custom-call | tf_op jit(solution)/shard_map/spread/pallas_call | solution.py:498
  46.5 5.4 %all-to-all-start.3 = ((f32[16,8,128]{2,1,0:T(8,128)}), f32[16,8,128]{2,1,0:T(8,128)S(1)}, u32[]{:S(2)}, u32[]{:S(2)}) async-start(f32[16,8,128]{2,1,0:T(8,128)} %spread.1), calls=%async_computation.3 | async-start | bytes 131072 | tf_op jit(solution)/shard_map/all_to_all | solution.py:510
  51.9 1.1 %place.1 = (bf16[8,3,4,64]{3,2,1,0:T(4,128)(2,1)}, bf16[8,6]{1,0:T(8,128)(2,1)}) custom-call(bf16[16,40,128]{2,1,0:T(8,128)(2,1)S(1)} %all_to_all.21.got_ref), custom_call_target="tpu_custom_call" | custom-call | tf_op jit(solution)/shard_map/place/pallas_call | solution.py:498
  53.0 4.8 %all-to-all-done.3.got_ref = f32[16,8,128]{2,1,0:T(8,128)S(1)} async-done(((f32[16,8,128]{2,1,0:T(8,128)}), f32[16,8,128]{2,1,0:T(8,128)S(1)}, u32[]{:S(2)}, u32[]{:S(2)}) %all-to-all-start.3) | async-done | bytes 65568 | tf_op jit(solution)/shard_map/all_to_all | solution.py:510
  57.8 0.9 %finish.1 = (f32[27,1,16]{2,1,0:T(1,128)}, f32[1,16]{1,0:T(1,128)}, f32[432,32]{1,0:T(8,128)}, f32[1,32]{1,0:T(1,128)}, f32[16,32]{1,0:T(8,128)}, /*index=5*/f32...) custom-call(f32[16,8,128]{2,1,0:T(8,128)S(1)} %all-to-all-done.3.got_ref), custom_call_target="tpu_custom_call" | custom-call | tf_op jit(solution)/shard_map/finish/pallas_call | solution.py:498
  (3 shorter events, 0.0 us)
Async XLA Ops:
  0.6 8.3 %copy-start = (bf16[32,16,3,3,3]{0,1,4,3,2:T(8,128)(2,1)S(1)}, bf16[32,16,3,3,3]{0,1,4,3,2:T(8,128)(2,1)}, u32[]{:S(2)}) copy-start(bf16[32,16,3,3,3]{0,1,4,3,2:T(8,128)(2,1)} %param.19) | copy-start | bytes 82948
  2.2 6.7 %copy-start.2 = (bf16[32,16]{0,1:T(8,128)(2,1)S(1)}, bf16[32,16]{0,1:T(8,128)(2,1)}, u32[]{:S(2)}) copy-start(bf16[32,16]{0,1:T(8,128)(2,1)} %param.21) | copy-start | bytes 3076
  2.2 6.7 %copy-start.4 = (bf16[8,6]{1,0:T(8,128)(2,1)S(1)}, bf16[8,6]{1,0:T(8,128)(2,1)}, u32[]{:S(2)}) copy-start(bf16[8,6]{1,0:T(8,128)(2,1)} %kt_ref.1) | copy-start | bytes 292
  2.2 6.7 %copy-start.5 = (bf16[3,32]{1,0:T(4,128)(2,1)S(1)}, bf16[3,32]{1,0:T(4,128)(2,1)}, u32[]{:S(2)}) copy-start(bf16[3,32]{1,0:T(4,128)(2,1)} %wf_ref.1) | copy-start | bytes 580
  2.2 6.7 %copy-start.6 = (s32[8]{0:T(128)S(1)}, s32[8]{0:T(128)}, u32[]{:S(2)}) copy-start(s32[8]{0:T(128)} %dest_ref.1) | copy-start | bytes 100
  2.2 6.7 %copy-start.7 = (f32[3]{0:T(128)S(1)}, f32[3]{0:T(128)}, u32[]{:S(2)}) copy-start(f32[3]{0:T(128)} %bf_ref.1) | copy-start | bytes 40
  2.2 6.7 %copy-start.8 = (f32[16]{0:T(128)S(1)}, f32[16]{0:T(128)}, u32[]{:S(2)}) copy-start(f32[16]{0:T(128)} %param.18) | copy-start | bytes 196
  2.2 6.7 %copy-start.9 = (f32[32]{0:T(128)S(1)}, f32[32]{0:T(128)}, u32[]{:S(2)}) copy-start(f32[32]{0:T(128)} %param.20) | copy-start | bytes 388
  2.3 6.7 %copy-start.10 = (f32[6]{0:T(128)S(1)}, f32[6]{0:T(128)}, u32[]{:S(2)}) copy-start(f32[6]{0:T(128)} %param.25) | copy-start | bytes 76
  2.3 11.5 %all-to-all-start = ((bf16[8,4,8,128]{3,2,1,0:T(8,128)(2,1)}), bf16[8,4,8,128]{3,2,1,0:T(8,128)(2,1)S(1)}, u32[]{:S(2)}, u32[]{:S(2)}) async-start(bf16[8,4,8,128]{3,2,1,0:T(8,128)(2,1)} %pack.1), calls=%async_computation | async-start | bytes 131072 | tf_op jit(solution)/shard_map/all_to_all | solution.py:510
  8.9 0.7 %copy-start.1 = (bf16[16,1,3,3,3]{0,4,3,2,1:T(4,128)(2,1)S(1)}, bf16[16,1,3,3,3]{0,4,3,2,1:T(4,128)(2,1)}, u32[]{:S(2)}) copy-start(bf16[16,1,3,3,3]{0,4,3,2,1:T(4,128)(2,1)} %param.17) | copy-start | bytes 2596
  8.9 0.7 %copy-start.3 = (bf16[6,32]{1,0:T(8,128)(2,1)S(1)}, bf16[6,32]{1,0:T(8,128)(2,1)}, u32[]{:S(2)}) copy-start(bf16[6,32]{1,0:T(8,128)(2,1)} %wt_ref.1) | copy-start | bytes 1156
  46.5 11.3 %all-to-all-start.3 = ((f32[16,8,128]{2,1,0:T(8,128)}), f32[16,8,128]{2,1,0:T(8,128)S(1)}, u32[]{:S(2)}, u32[]{:S(2)}) async-start(f32[16,8,128]{2,1,0:T(8,128)} %spread.1), calls=%async_computation.3 | async-start | bytes 131072 | tf_op jit(solution)/shard_map/all_to_all | solution.py:510

commit v4 on v3

--- a/solution.py
+++ b/solution.py
@@ -35,24 +35,6 @@
 
 def side_of(y):
     return ((y + 1) // 2) % 2
-
-
-def pack(place_ref, vol_hbm, ft_hbm, out_ref, ft_ref, done):
-    planes = pltpu.make_async_copy(vol_hbm, out_ref.at[:, 0:2], done.at[0])
-    goals = pltpu.make_async_copy(ft_hbm, ft_ref, done.at[1])
-    goals.start()
-    planes.start()
-    odd = place_ref[0] % 2 == 1
-    goals.wait()
-    goal = ft_ref[...].astype(F32)
-    none = jnp.zeros_like(goal)
-    low = jnp.concatenate([goal, none], axis=3)
-    high = jnp.concatenate([none, goal], axis=3)
-    both = jnp.where(odd, high, low)
-    out_ref[:, 2] = jnp.concatenate([both[:, 0], both[:, 1]], axis=1).astype(BF16)
-    rest = jnp.zeros((8, 4, 128), F32)
-    out_ref[:, 3] = jnp.concatenate([both[:, 2], rest], axis=1).astype(BF16)
-    planes.wait()
 
 
 def prepare(
@@ -236,7 +218,8 @@
     goals = [
         jnp.concatenate(
             [
-                got_ref[2 * q, 2 + h].astype(F32) + got_ref[2 * q + 1, 2 + h].astype(F32)
+                got_ref[2 * q, 2 + h].astype(F32)
+                + pltpu.roll(got_ref[2 * q + 1, 2 + h].astype(F32), 64, 1)
                 for q in range(4)
             ],
             axis=1,
@@ -456,10 +439,11 @@
 
 
 def finish(
-    got_ref,
-    g1_ref, b1_ref, g2_ref, b2_ref, gs_ref, gf_ref, bf_ref, gt_ref, bt_ref,
-    total, extra, second,
+    got_ref, routed_ref,
+    fp_ref, tp_ref, g1_ref, b1_ref, g2_ref, b2_ref, gs_ref, gf_ref, bf_ref, gt_ref, bt_ref,
+    total, extra, second, recs,
 ):
+    place_records(routed_ref, fp_ref, tp_ref, recs)
     swap = lax.axis_index("yh") * 8
     for p in range(16):
         block = got_ref[lax.rem(p + swap, 16)]
@@ -523,11 +507,8 @@
     tensor_count = records * 6
     cell_count = slabs * 4 * 64
     place = lax.axis_index("slab").astype(jnp.int32).reshape(1)
-    (mine,) = run(
-        pack, "pack", [place], [volume, flux_target[:, :, 0]], [((8, 4, 8, 128), BF16)],
-        [((8, 3, 4, 64), BF16), pltpu.SemaphoreType.DMA((2,))],
-        pl.BlockSpec(memory_space=pl.ANY), 60,
-    )
+    goal = jnp.pad(flux_target[:, :, 0], ((0, 0), (0, 1), (0, 0), (0, 64)))
+    mine = jnp.concatenate([volume, goal.reshape(8, 2, 8, 128)], axis=1)
     record = exchange(mine, "slab")
     weights = run(
         prepare, "prepare", [place, dest, flux_bias],
@@ -563,17 +544,17 @@
     routed = exchange(routed, ("z", "yh", "yl"), lines)
     (share,) = run(spread, "spread", [], [routed], [((near, 8, 128), F32)])
     total = exchange(share, ("yl", "slab"))
-    fp, tp = run(
-        place_records, "place", [], [routed], [((8, 3, 4, 64), BF16), ((8, 6), BF16)],
-        [((far, ROUTED, 128), F32)],
-    )
-    g1, b1, g2, b2, gs, gf, bf, gt, bt = run(
-        finish, "finish", [], [total],
+    fp, tp, g1, b1, g2, b2, gs, gf, bf, gt, bt = run(
+        finish, "finish", [], [total, routed],
         [
+            ((8, 3, 4, 64), BF16), ((8, 6), BF16),
             ((27, 1, 16), F32), ((1, 16), F32), ((432, 32), F32), ((1, 32), F32),
             ((16, 32), F32), ((3, 32), F32), ((1, 3), F32), ((6, 32), F32), ((1, 6), F32),
         ],
-        [((ROWS, 128), F32), ((112, 32), F32), ((BLOCK, 32), F32)],
+        [
+            ((ROWS, 128), F32), ((112, 32), F32), ((BLOCK, 32), F32),
+            ((far, ROUTED, 128), F32),
+        ],
     )
     return (
         fp[:, :, None],

time: 59.1 us -> 57.6 us (0.975)
  blocking collectives: 29.2 us -> 39.6 us
  starting transfers between devices: 12 us -> 6.64 us
  waiting for transfers between devices: 7.86 us -> 3.03 us
  Pallas kernels: 8.11 us -> 5.15 us
  local copies, waits for them, and re-layouts: 0.69 us -> 1.46 us
  other arithmetic: 0 us -> 0.64 us
    all_to_all x2 -> x3, blocking collectives: 29.2 us -> 39.6 us  [exchange(): lax.all_to_all(block, axis, 0, 0, tiled=True, axis_index_groups=groups)]
    all_to_all x2 -> x1, starting transfers between devices: 12 us -> 6.64 us  [exchange(): lax.all_to_all(block, axis, 0, 0, tiled=True, axis_index_groups=groups)]
    all_to_all x2 -> x1, waiting for transfers between devices: 7.86 us -> 3.03 us  [exchange(): lax.all_to_all(block, axis, 0, 0, tiled=True, axis_index_groups=groups)]
    pallas_call x7 -> x5, Pallas kernels: 8.11 us -> 5.15 us  [run(): pl.pallas_call(kernel, out_shape=tuple((jax.ShapeDtypeStruct(*o[0:2]) for...]
    pad x0 -> x1, local copies, waits for them, and re-layouts: none -> 0.76 us  [on_device(): goal = jnp.pad(flux_target[:, :, 0], ((0, 0), (0, 1), (0, 0), (0, 64)))]
    concatenate x0 -> x1, other arithmetic: none -> 0.64 us  [on_device(): mine = jnp.concatenate([volume, goal.reshape(8, 2, 8, 128)], axis=1)]
  transfers between devices with their start and end apart: 2 -> 1, of which waited for: 2 -> 1; matrix products, arithmetic and copies ran while one was open for 0% -> 0% of each run, Pallas kernels for 4% -> 2%
where the time goes in v4:
time: 57.6 us; the launch traced here: 57.2 us
  blocking collectives  39.6 us (69%)
  starting transfers between devices  6.64 us (12%)
  Pallas kernels  5.15 us (9%)
  waiting for transfers between devices  3.03 us (5%)
  local copies, waits for them, and re-layouts  1.46 us (3%)
  between operations  0.77 us (1%)
  other arithmetic  0.64 us (1%)
    all_to_all x3, blocking collectives, exchange(): lax.all_to_all(block, axis, 0, 0, tiled=True, axis_index_groups=groups)  39.6 us
    all_to_all x1, starting transfers between devices, exchange(): lax.all_to_all(block, axis, 0, 0, tiled=True, axis_index_groups=groups)  6.64 us
    pallas_call x5, Pallas kernels, run(): pl.pallas_call(kernel, out_shape=tuple((jax.ShapeDtypeStruct(*o[0:2]) for...  5.15 us
    all_to_all x1, waiting for transfers between devices, exchange(): lax.all_to_all(block, axis, 0, 0, tiled=True, axis_index_groups=groups)  3.03 us
  transfers between devices with their start and end apart: 1, of which 1 were waited for; matrix products, arithmetic and copies ran while one was open for 0% of the time, Pallas kernels for 2%

profile of v4, /device:TPU:1, one launch (start us, length us, event | category | flops | bytes accessed | tf_op | source)
XLA Modules:
  0.0 57.2 jit_solution(10627038254084894940)
XLA Ops:
  0.6 0.0 copy-start.11
  0.7 0.8 %pad.4 = bf16[8,4,4,128]{3,2,1,0:T(4,128)(2,1)S(1)} pad(bf16[8,3,4,64]{3,2,1,0:T(4,128)(2,1)} %bitcast.34, bf16[]{:T(256)} %constant.2.clone.1), padding=0_0x0_1x0_0x0_64 | pad | bytes 45058 | tf_op jit(solution)/shard_map/jit(_pad)/pad | solution.py:510
  1.4 0.0 copy-done.11
  1.4 0.0 copy-start
  1.4 0.6 %pad_maximum_fusion = bf16[8,4,8,128]{3,2,1,0:T(8,128)(2,1)} fusion(bf16[8,2,8,128]{3,2,1,0:T(8,128)(2,1)S(1)} %bitcast.33, bf16[8,2,8,128]{3,2,1,0:T(8,128)(2,1)S(1)} %copy-done.11), kind=kLoop, calls=%fused_computation | loop fusion | flops 32768 | bytes 131072 | tf_op jit(solution)/shard_map/concatenate | solution.py:511
  2.1 0.0 copy-start.7
  2.1 0.0 copy-start.8
  2.1 0.0 copy-start.9
  2.1 0.0 copy-start.10
  2.1 6.6 %all-to-all-start = ((bf16[8,4,8,128]{3,2,1,0:T(8,128)(2,1)}), bf16[8,4,8,128]{3,2,1,0:T(8,128)(2,1)S(1)}, u32[]{:S(2)}, u32[]{:S(2)}) async-start(bf16[8,4,8,128]{3,2,1,0:T(8,128)(2,1)} %pad_maximum_fusion), calls=%async_computation | async-start | bytes 131072 | tf_op jit(solution)/shard_map/all_to_all | solution.py:494
  8.7 0.0 copy-start.2
  8.7 0.0 copy-start.3
  8.8 0.0 copy-start.5
  8.8 0.0 copy-done
  8.8 0.0 copy-done.7
  8.8 0.0 copy-done.8
  8.8 0.0 copy-done.9
  8.8 0.0 copy-done.10
  8.8 0.6 %copy-done.1 = bf16[16,1,3,3,3]{0,4,3,2,1:T(4,128)(2,1)S(1)} copy-done((bf16[16,1,3,3,3]{0,4,3,2,1:T(4,128)(2,1)S(1)}, bf16[16,1,3,3,3]{0,4,3,2,1:T(4,128)(2,1)}, u32[]{:S(2)}) %copy-start.1) | copy-done | bytes 888
  9.4 0.0 copy-done.6
  9.4 0.0 copy-done.4
  9.4 0.0 copy-done.2
  9.5 0.0 copy-done.3
  9.5 0.0 copy-done.5
  9.5 1.1 %prepare.1 = (bf16[512,128]{1,0:T(8,128)(2,1)S(1)}, bf16[32,512]{1,0:T(8,128)(2,1)S(1)}, bf16[128,256]{1,0:T(8,128)(2,1)S(1)}, bf16[16,128]{1,0:T(8,128)(2,1)S(1...) custom-call(s32[1]{0:T(128)} %bitcast.2.place_ref, ...), custom_call_target="tpu_custom_call" | custom-call | tf_op jit(solution)/shard_map/prepare/pallas_call | solution.py:482
  10.6 3.0 %all-to-all-done.got_ref = bf16[8,4,8,128]{3,2,1,0:T(8,128)(2,1)S(1)} async-done(((bf16[8,4,8,128]{3,2,1,0:T(8,128)(2,1)}), bf16[8,4,8,128]{3,2,1,0:T(8,128)(2,1)S(1)}, u32[]{:S(2)}, u32[]{:S(2)}) %all-to-all-start) | async-done | bytes 65568 | tf_op jit(solution)/shard_map/all_to_all | solution.py:494
  13.6 2.5 %step.1 = bf16[16,24,128]{2,1,0:T(8,128)(2,1)S(1)} custom-call(bf16[8,4,8,128]{3,2,1,0:T(8,128)(2,1)S(1)} %all-to-all-done.got_ref, bf16[512,128]{1,0:T(8,128)(2,1)S(1)} %get-tuple-element.31.t1_ref, bf16[32,512]{1,0:T(8,128)(2,1)S(1)} %get-tuple-element.32.w2a_ref, bf16[128,256]{1,0:T(8,128)(2,1)S(1)} %get-tuple-element.33.wb_ref, ...), custom_call_target="tpu_custom_call" | custom-call | tf_op jit(solution)/shard_map/step/pallas_call | solution.py:482
  16.1 9.2 %all_to_all.20.got_ref = bf16[16,24,128]{2,1,0:T(8,128)(2,1)S(1)} all-to-all(bf16[16,24,128]{2,1,0:T(8,128)(2,1)S(1)} %step.1), channel_id=1, replica_groups=mesh['z'=8,'yh'=2,'yl'=2,'slab'=8] {'yl','slab'}, dimensions={0} | all-to-all | bytes 196608 | tf_op jit(solution)/shard_map/all_to_all | solution.py:494
  25.3 0.4 route.1
  25.7 20.0 %all_to_all.21.got_ref.routed_ref = bf16[16,40,128]{2,1,0:T(8,128)(2,1)S(1)} all-to-all(bf16[16,40,128]{2,1,0:T(8,128)(2,1)S(1)} %route.1), channel_id=1, replica_groups={{0,24,32,56,64,88,96,120,128,152,160,184,192,216,224,248},{8,16,40,48,7..., dimensions={0} | all-to-all | bytes 327680 | tf_op jit(solution)/shard_map/all_to_all | solution.py:494
  45.7 10.4 %all_to_all.22.got_ref = f32[16,8,128]{2,1,0:T(8,128)S(1)} all-to-all(f32[16,8,128]{2,1,0:T(8,128)S(1)} %spread.1), channel_id=1, replica_groups=mesh['z'=8,'yh'=2,'yl'=2,'slab'=8] {'yl','slab'}, dimensions={0} | all-to-all | bytes 131072 | tf_op jit(solution)/shard_map/all_to_all | solution.py:494
  56.1 1.1 %finish.1 = (bf16[8,3,4,64]{3,2,1,0:T(4,128)(2,1)}, bf16[8,6]{1,0:T(8,128)(2,1)}, f32[27,1,16]{2,1,0:T(1,128)}, f32[1,16]{1,0:T(1,128)}, f32[432,32]{1,0:T(8,128...) custom-call(f32[16,8,128]{2,1,0:T(8,128)S(1)} %all_to_all.22.got_ref, ...), custom_call_target="tpu_custom_call" | custom-call | tf_op jit(solution)/shard_map/finish/pallas_call | solution.py:482
  (4 shorter events, 0.0 us)
Async XLA Ops:
  0.6 0.8 %copy-start.11 = (bf16[8,2,8,128]{3,2,1,0:T(8,128)(2,1)S(1)}, bf16[8,2,8,128]{3,2,1,0:T(8,128)(2,1)}, u32[]{:S(2)}) copy-start(bf16[8,2,8,128]{3,2,1,0:T(8,128)(2,1)} %param.13) | copy-start | bytes 98308
  1.4 7.3 %copy-start = (bf16[32,16,3,3,3]{0,1,4,3,2:T(8,128)(2,1)S(1)}, bf16[32,16,3,3,3]{0,1,4,3,2:T(8,128)(2,1)}, u32[]{:S(2)}) copy-start(bf16[32,16,3,3,3]{0,1,4,3,2:T(8,128)(2,1)} %param.19) | copy-start | bytes 82948
  2.1 6.7 %copy-start.7 = (f32[3]{0:T(128)S(1)}, f32[3]{0:T(128)}, u32[]{:S(2)}) copy-start(f32[3]{0:T(128)} %bf_ref.1) | copy-start | bytes 40
  2.1 6.7 %copy-start.8 = (f32[16]{0:T(128)S(1)}, f32[16]{0:T(128)}, u32[]{:S(2)}) copy-start(f32[16]{0:T(128)} %param.18) | copy-start | bytes 196
  2.1 6.7 %copy-start.9 = (f32[32]{0:T(128)S(1)}, f32[32]{0:T(128)}, u32[]{:S(2)}) copy-start(f32[32]{0:T(128)} %param.20) | copy-start | bytes 388
  2.1 6.7 %copy-start.10 = (f32[6]{0:T(128)S(1)}, f32[6]{0:T(128)}, u32[]{:S(2)}) copy-start(f32[6]{0:T(128)} %param.25) | copy-start | bytes 76
  2.1 11.5 %all-to-all-start = ((bf16[8,4,8,128]{3,2,1,0:T(8,128)(2,1)}), bf16[8,4,8,128]{3,2,1,0:T(8,128)(2,1)S(1)}, u32[]{:S(2)}, u32[]{:S(2)}) async-start(bf16[8,4,8,128]{3,2,1,0:T(8,128)(2,1)} %pad_maximum_fusion), calls=%async_computation | async-start | bytes 131072 | tf_op jit(solution)/shard_map/all_to_all | solution.py:494
  8.7 0.7 %copy-start.1 = (bf16[16,1,3,3,3]{0,4,3,2,1:T(4,128)(2,1)S(1)}, bf16[16,1,3,3,3]{0,4,3,2,1:T(4,128)(2,1)}, u32[]{:S(2)}) copy-start(bf16[16,1,3,3,3]{0,4,3,2,1:T(4,128)(2,1)} %param.17) | copy-start | bytes 2596
  8.7 0.7 %copy-start.6 = (s32[8]{0:T(128)S(1)}, s32[8]{0:T(128)}, u32[]{:S(2)}) copy-start(s32[8]{0:T(128)} %dest_ref.1) | copy-start | bytes 100
  8.7 0.7 %copy-start.4 = (bf16[8,6]{1,0:T(8,128)(2,1)S(1)}, bf16[8,6]{1,0:T(8,128)(2,1)}, u32[]{:S(2)}) copy-start(bf16[8,6]{1,0:T(8,128)(2,1)} %kt_ref.1) | copy-start | bytes 292
  8.7 0.7 %copy-start.2 = (bf16[32,16]{0,1:T(8,128)(2,1)S(1)}, bf16[32,16]{0,1:T(8,128)(2,1)}, u32[]{:S(2)}) copy-start(bf16[32,16]{0,1:T(8,128)(2,1)} %param.21) | copy-start | bytes 3076
  8.7 0.7 %copy-start.3 = (bf16[6,32]{1,0:T(8,128)(2,1)S(1)}, bf16[6,32]{1,0:T(8,128)(2,1)}, u32[]{:S(2)}) copy-start(bf16[6,32]{1,0:T(8,128)(2,1)} %wt_ref.1) | copy-start | bytes 1156
  8.8 0.7 %copy-start.5 = (bf16[3,32]{1,0:T(4,128)(2,1)S(1)}, bf16[3,32]{1,0:T(4,128)(2,1)}, u32[]{:S(2)}) copy-start(bf16[3,32]{1,0:T(4,128)(2,1)} %wf_ref.1) | copy-start | bytes 580

commit v5 on v4

--- a/solution.py
+++ b/solution.py
@@ -18,7 +18,7 @@
 TAPS = 144
 ROWS = 128
 SENT = 24
-ROUTED = 40
+ROUTED = 32
 
 
 def mxu(a, b, dims=NN):
@@ -265,7 +265,7 @@
         bias2 = bias2 + jnp.sum(wide, axis=1, keepdims=True)
         next_x = jnp.where(last_x, zero, pltpu.roll(d, CELLS - 1, 1))
         next_z = jnp.where(last_z, zero, pltpu.roll(d, CELLS - 64, 1))
-        both = jnp.where(last_z, zero, pltpu.roll(next_x, CELLS - 64, 1))
+        both = jnp.where(last_x | last_z, zero, pltpu.roll(d, CELLS - 65, 1))
         d_ref[y * 128 : y * 128 + 32] = d
         d_ref[y * 128 + 32 : y * 128 + 64] = next_x
         d_ref[y * 128 + 64 : y * 128 + 96] = next_z
@@ -351,15 +351,16 @@
     tensor_row = pltpu.roll(jnp.where(lane < 6, dt, 0.0), 116, 1)
     extra[67:68] = first_row + bias_row + tensor_row
     extra[68:74] = pltpu.roll(upright[0:8], 64, 1)[1:7]
-    extra[74:112] = jnp.zeros((38, 128), F32)
+    extra[74:80] = jnp.zeros((6, 128), F32)
     rest = lane8 >= 96
     swap = lax.axis_index("yh") * 8
     for t in range(16):
         block = second[t * 8 : t * 8 + 8]
         total[t * 8 : t * 8 + 8] = jnp.where(rest, 0.0, block)
-        total[t * 8 : t * 8 + 7] = jnp.where(
-            rest[0:7], extra[t * 7 : t * 7 + 7], block[0:7]
-        )
+        tail_rows = extra[t * 3 : t * 3 + 3]
+        other_rows = extra[48 + t * 2 : 50 + t * 2]
+        total[t * 8 : t * 8 + 3] = jnp.where(rest[0:3], tail_rows, block[0:3])
+        total[t * 8 + 3 : t * 8 + 5] = jnp.where(rest[0:2], other_rows, block[3:5])
         block = total[t * 8 : t * 8 + 8]
         high = block.astype(BF16).astype(F32)
         to = lax.rem(t + swap, 16)
@@ -391,16 +392,18 @@
     choose = jnp.transpose(hit)[0 : 4 * peers, 0:count].astype(BF16)
     layers = [mxu(choose, recs[:, 16 + k, :].astype(BF16)) for k in range(6)]
     marks = mxu(choose, last.astype(BF16))
-    marks = jnp.where(lanes((4 * peers, 128)) < 16, marks, 0.0)
-    marks = [pltpu.roll(marks, 96, 1), pltpu.roll(marks, 112, 1)]
+    lane = lanes((4 * peers, 128))
+    marks = jnp.where(lane == 6, pltpu.roll(marks, 126, 1), jnp.where(lane < 6, marks, 0.0))
+    marks = [pltpu.roll(marks, 96 + 8 * j, 1) for j in range(4)]
     row8, lane8 = rows((8, 128)), lanes((8, 128))
     upper, spare = row8 < 4, (row8 == 7) & (lane8 >= 96)
+    remainder = ((row8 == 5) | (row8 == 6)) & (lane8 >= 96)
+    share = jnp.where(remainder, pltpu.roll(low, 2, 0), high)
     for i in range(peers):
-        tall = []
-        for h, part in enumerate((high, low)):
-            at = 4 * i + 2 * h
-            seats = marks[0][at : at + 1] + marks[1][at + 1 : at + 2]
-            tall.append(jnp.where(spare, seats, part))
+        seats = marks[0][4 * i : 4 * i + 1]
+        for j in range(1, 4):
+            seats = seats + marks[j][4 * i + j : 4 * i + j + 1]
+        tall = [jnp.where(spare, seats, share)]
         at = (i // 2) * 8
         for m in range(3):
             even, odd = layers[2 * m][at : at + 8], layers[2 * m + 1][at : at + 8]
@@ -412,30 +415,28 @@
 
 
 def spread(got_ref, out_ref):
-    parts = jnp.sum(got_ref[:, 0:16, :].astype(F32), axis=0)
-    share = parts[0:8] + parts[8:16]
+    parts = jnp.sum(got_ref[:, 0:8, :].astype(F32), axis=0)
+    row8 = rows((8, 128))
+    split = ((row8 == 3) | (row8 == 4)) & (lanes((8, 128)) >= 96)
+    share = parts + jnp.where(split, pltpu.roll(parts, 6, 0), 0.0)
     out_ref[...] = jnp.broadcast_to(share[None], out_ref.shape)
 
 
-def place_records(got_ref, fp_ref, tp_ref, recs):
+def pick_records(got_ref, recs):
     recs[...] = got_ref[...].astype(F32)
     count = got_ref.shape[0]
-    marks = [
-        pltpu.roll(recs[:, 7 + 8 * (j // 2), :], 32 - 16 * (j % 2), 1) for j in range(4)
-    ]
+    marks = [pltpu.roll(recs[:, 7, :], 32 - 8 * j, 1) for j in range(4)]
     marks = jnp.concatenate(marks, axis=0)
     lane = lanes((4 * count, 128))
-    slot = jnp.sum(jnp.where(lane == 8, marks, 0.0), axis=1, keepdims=True) - 1.0
+    slot = jnp.sum(jnp.where(lane == 6, marks, 0.0), axis=1, keepdims=True) - 1.0
     hit = jnp.where((slot == lane.astype(F32)) & (lane < 8), 1.0, 0.0)
-    hit = jnp.concatenate([hit, jnp.zeros((128 - 4 * count, 128), F32)], axis=0)
-    choose = jnp.transpose(hit)[0:8, 0 : 4 * count].astype(BF16)
-    for k in range(6):
-        held = jnp.concatenate([recs[:, 16 + 4 * k + j, :] for j in range(4)], axis=0)
-        got = mxu(choose, held.astype(BF16)).astype(BF16)
-        f, y = (2 * k) // 4, (2 * k) % 4
-        fp_ref[:, f, y, :] = got[:, 0:64]
-        fp_ref[:, f, y + 1, :] = got[:, 64:128]
-    tp_ref[...] = mxu(choose, marks.astype(BF16))[:, 0:6].astype(BF16)
+    hit = hit.astype(BF16)
+    held = [
+        jnp.concatenate([recs[:, 8 + 4 * k + j, :] for j in range(4)], axis=0)
+        for k in range(6)
+    ]
+    every = mxu(hit, jnp.concatenate(held + [marks], axis=1).astype(BF16), TN)[0:8]
+    return every
 
 
 def finish(
@@ -443,12 +444,13 @@
     fp_ref, tp_ref, g1_ref, b1_ref, g2_ref, b2_ref, gs_ref, gf_ref, bf_ref, gt_ref, bt_ref,
     total, extra, second, recs,
 ):
-    place_records(routed_ref, fp_ref, tp_ref, recs)
+    every = pick_records(routed_ref, recs)
     swap = lax.axis_index("yh") * 8
     for p in range(16):
         block = got_ref[lax.rem(p + swap, 16)]
         total[p * 8 : p * 8 + 8] = block
-        extra[p * 7 : p * 7 + 7] = block[0:7, 96:128]
+        extra[p * 3 : p * 3 + 3] = block[0:3, 96:128]
+        extra[48 + p * 2 : 50 + p * 2] = block[3:5, 96:128]
     for kz in range(3):
         for ky in range(3):
             for kx in range(3):
@@ -471,6 +473,12 @@
     bf_ref[...] = extra[67:68, 16:19]
     bt_ref[...] = extra[67:68, 20:26]
     gt_ref[...] = extra[68:74]
+    for k in range(6):
+        got = every[:, k * 128 : k * 128 + 128].astype(BF16)
+        f, y = (2 * k) // 4, (2 * k) % 4
+        fp_ref[:, f, y, :] = got[:, 0:64]
+        fp_ref[:, f, y + 1, :] = got[:, 64:128]
+    tp_ref[...] = every[:, 768:774].astype(BF16)
 
 
 SMEM = pl.BlockSpec(memory_space=pltpu.SMEM)

time: 57.6 us -> 57 us (0.990)
  blocking collectives: 39.6 us -> 38.9 us
    all_to_all x3, blocking collectives: 39.6 us -> 38.9 us  [exchange(): lax.all_to_all(block, axis, 0, 0, tiled=True, axis_index_groups=groups)]
where the time goes in v5:
time: 57 us; the launch traced here: 56.6 us
  blocking collectives  38.9 us (68%)
  starting transfers between devices  6.64 us (12%)
  Pallas kernels  5.15 us (9%)
  waiting for transfers between devices  3.03 us (5%)
  local copies, waits for them, and re-layouts  1.46 us (3%)
  between operations  0.77 us (1%)
  other arithmetic  0.64 us (1%)
    all_to_all x3, blocking collectives, exchange(): lax.all_to_all(block, axis, 0, 0, tiled=True, axis_index_groups=groups)  38.9 us
    all_to_all x1, starting transfers between devices, exchange(): lax.all_to_all(block, axis, 0, 0, tiled=True, axis_index_groups=groups)  6.64 us
    pallas_call x5, Pallas kernels, run(): pl.pallas_call(kernel, out_shape=tuple((jax.ShapeDtypeStruct(*o[0:2]) for...  5.15 us
    all_to_all x1, waiting for transfers between devices, exchange(): lax.all_to_all(block, axis, 0, 0, tiled=True, axis_index_groups=groups)  3.03 us
  transfers between devices with their start and end apart: 1, of which 1 were waited for; matrix products, arithmetic and copies ran while one was open for 0% of the time, Pallas kernels for 2%

profile of v5, /device:TPU:1, one launch (start us, length us, event | category | flops | bytes accessed | tf_op | source)
XLA Modules:
  0.0 56.6 jit_solution(8381633672569341601)
XLA Ops:
  0.6 0.0 copy-start.11
  0.7 0.8 %pad.4 = bf16[8,4,4,128]{3,2,1,0:T(4,128)(2,1)S(1)} pad(bf16[8,3,4,64]{3,2,1,0:T(4,128)(2,1)} %bitcast.34, bf16[]{:T(256)} %constant.2.clone.1), padding=0_0x0_1x0_0x0_64 | pad | bytes 45058 | tf_op jit(solution)/shard_map/jit(_pad)/pad | solution.py:518
  1.4 0.0 copy-done.11
  1.4 0.0 copy-start
  1.4 0.6 %pad_maximum_fusion = bf16[8,4,8,128]{3,2,1,0:T(8,128)(2,1)} fusion(bf16[8,2,8,128]{3,2,1,0:T(8,128)(2,1)S(1)} %bitcast.33, bf16[8,2,8,128]{3,2,1,0:T(8,128)(2,1)S(1)} %copy-done.11), kind=kLoop, calls=%fused_computation | loop fusion | flops 32768 | bytes 131072 | tf_op jit(solution)/shard_map/concatenate | solution.py:519
  2.1 0.0 copy-start.7
  2.1 0.0 copy-start.8
  2.1 0.0 copy-start.9
  2.1 0.0 copy-start.10
  2.1 6.6 %all-to-all-start = ((bf16[8,4,8,128]{3,2,1,0:T(8,128)(2,1)}), bf16[8,4,8,128]{3,2,1,0:T(8,128)(2,1)S(1)}, u32[]{:S(2)}, u32[]{:S(2)}) async-start(bf16[8,4,8,128]{3,2,1,0:T(8,128)(2,1)} %pad_maximum_fusion), calls=%async_computation | async-start | bytes 131072 | tf_op jit(solution)/shard_map/all_to_all | solution.py:502
  8.7 0.0 copy-start.2
  8.7 0.0 copy-start.3
  8.8 0.0 copy-start.5
  8.8 0.0 copy-done
  8.8 0.0 copy-done.7
  8.8 0.0 copy-done.8
  8.8 0.0 copy-done.9
  8.8 0.0 copy-done.10
  8.8 0.6 %copy-done.1 = bf16[16,1,3,3,3]{0,4,3,2,1:T(4,128)(2,1)S(1)} copy-done((bf16[16,1,3,3,3]{0,4,3,2,1:T(4,128)(2,1)S(1)}, bf16[16,1,3,3,3]{0,4,3,2,1:T(4,128)(2,1)}, u32[]{:S(2)}) %copy-start.1) | copy-done | bytes 888
  9.4 0.0 copy-done.6
  9.4 0.0 copy-done.4
  9.4 0.0 copy-done.2
  9.5 0.0 copy-done.3
  9.5 0.0 copy-done.5
  9.5 1.1 %prepare.1 = (bf16[512,128]{1,0:T(8,128)(2,1)S(1)}, bf16[32,512]{1,0:T(8,128)(2,1)S(1)}, bf16[128,256]{1,0:T(8,128)(2,1)S(1)}, bf16[16,128]{1,0:T(8,128)(2,1)S(1...) custom-call(s32[1]{0:T(128)} %bitcast.2.place_ref, ...), custom_call_target="tpu_custom_call" | custom-call | tf_op jit(solution)/shard_map/prepare/pallas_call | solution.py:490
  10.6 3.0 %all-to-all-done.got_ref = bf16[8,4,8,128]{3,2,1,0:T(8,128)(2,1)S(1)} async-done(((bf16[8,4,8,128]{3,2,1,0:T(8,128)(2,1)}), bf16[8,4,8,128]{3,2,1,0:T(8,128)(2,1)S(1)}, u32[]{:S(2)}, u32[]{:S(2)}) %all-to-all-start) | async-done | bytes 65568 | tf_op jit(solution)/shard_map/all_to_all | solution.py:502
  13.6 2.4 %step.1 = bf16[16,24,128]{2,1,0:T(8,128)(2,1)S(1)} custom-call(bf16[8,4,8,128]{3,2,1,0:T(8,128)(2,1)S(1)} %all-to-all-done.got_ref, bf16[512,128]{1,0:T(8,128)(2,1)S(1)} %get-tuple-element.31.t1_ref, bf16[32,512]{1,0:T(8,128)(2,1)S(1)} %get-tuple-element.32.w2a_ref, bf16[128,256]{1,0:T(8,128)(2,1)S(1)} %get-tuple-element.33.wb_ref, ...), custom_call_target="tpu_custom_call" | custom-call | tf_op jit(solution)/shard_map/step/pallas_call | solution.py:490
  16.0 9.2 %all_to_all.20.got_ref = bf16[16,24,128]{2,1,0:T(8,128)(2,1)S(1)} all-to-all(bf16[16,24,128]{2,1,0:T(8,128)(2,1)S(1)} %step.1), channel_id=1, replica_groups=mesh['z'=8,'yh'=2,'yl'=2,'slab'=8] {'yl','slab'}, dimensions={0} | all-to-all | bytes 196608 | tf_op jit(solution)/shard_map/all_to_all | solution.py:502
  25.2 0.5 route.1
  25.7 19.4 %all_to_all.21.got_ref.routed_ref = bf16[16,32,128]{2,1,0:T(8,128)(2,1)S(1)} all-to-all(bf16[16,32,128]{2,1,0:T(8,128)(2,1)S(1)} %route.1), channel_id=1, replica_groups={{0,24,32,56,64,88,96,120,128,152,160,184,192,216,224,248},{8,16,40,48,7..., dimensions={0} | all-to-all | bytes 262144 | tf_op jit(solution)/shard_map/all_to_all | solution.py:502
  45.1 10.4 %all_to_all.22.got_ref = f32[16,8,128]{2,1,0:T(8,128)S(1)} all-to-all(f32[16,8,128]{2,1,0:T(8,128)S(1)} %spread.1), channel_id=1, replica_groups=mesh['z'=8,'yh'=2,'yl'=2,'slab'=8] {'yl','slab'}, dimensions={0} | all-to-all | bytes 131072 | tf_op jit(solution)/shard_map/all_to_all | solution.py:502
  55.5 1.1 %finish.1 = (bf16[8,3,4,64]{3,2,1,0:T(4,128)(2,1)}, bf16[8,6]{1,0:T(8,128)(2,1)}, f32[27,1,16]{2,1,0:T(1,128)}, f32[1,16]{1,0:T(1,128)}, f32[432,32]{1,0:T(8,128...) custom-call(f32[16,8,128]{2,1,0:T(8,128)S(1)} %all_to_all.22.got_ref, ...), custom_call_target="tpu_custom_call" | custom-call | tf_op jit(solution)/shard_map/finish/pallas_call | solution.py:490
  (4 shorter events, 0.0 us)
Async XLA Ops:
  0.6 0.8 %copy-start.11 = (bf16[8,2,8,128]{3,2,1,0:T(8,128)(2,1)S(1)}, bf16[8,2,8,128]{3,2,1,0:T(8,128)(2,1)}, u32[]{:S(2)}) copy-start(bf16[8,2,8,128]{3,2,1,0:T(8,128)(2,1)} %param.13) | copy-start | bytes 98308
  1.4 7.3 %copy-start = (bf16[32,16,3,3,3]{0,1,4,3,2:T(8,128)(2,1)S(1)}, bf16[32,16,3,3,3]{0,1,4,3,2:T(8,128)(2,1)}, u32[]{:S(2)}) copy-start(bf16[32,16,3,3,3]{0,1,4,3,2:T(8,128)(2,1)} %param.19) | copy-start | bytes 82948
  2.1 6.7 %copy-start.7 = (f32[3]{0:T(128)S(1)}, f32[3]{0:T(128)}, u32[]{:S(2)}) copy-start(f32[3]{0:T(128)} %bf_ref.1) | copy-start | bytes 40
  2.1 6.7 %copy-start.8 = (f32[16]{0:T(128)S(1)}, f32[16]{0:T(128)}, u32[]{:S(2)}) copy-start(f32[16]{0:T(128)} %param.18) | copy-start | bytes 196
  2.1 6.7 %copy-start.9 = (f32[32]{0:T(128)S(1)}, f32[32]{0:T(128)}, u32[]{:S(2)}) copy-start(f32[32]{0:T(128)} %param.20) | copy-start | bytes 388
  2.1 6.7 %copy-start.10 = (f32[6]{0:T(128)S(1)}, f32[6]{0:T(128)}, u32[]{:S(2)}) copy-start(f32[6]{0:T(128)} %param.25) | copy-start | bytes 76
  2.1 11.5 %all-to-all-start = ((bf16[8,4,8,128]{3,2,1,0:T(8,128)(2,1)}), bf16[8,4,8,128]{3,2,1,0:T(8,128)(2,1)S(1)}, u32[]{:S(2)}, u32[]{:S(2)}) async-start(bf16[8,4,8,128]{3,2,1,0:T(8,128)(2,1)} %pad_maximum_fusion), calls=%async_computation | async-start | bytes 131072 | tf_op jit(solution)/shard_map/all_to_all | solution.py:502
  8.7 0.7 %copy-start.1 = (bf16[16,1,3,3,3]{0,4,3,2,1:T(4,128)(2,1)S(1)}, bf16[16,1,3,3,3]{0,4,3,2,1:T(4,128)(2,1)}, u32[]{:S(2)}) copy-start(bf16[16,1,3,3,3]{0,4,3,2,1:T(4,128)(2,1)} %param.17) | copy-start | bytes 2596
  8.7 0.7 %copy-start.6 = (s32[8]{0:T(128)S(1)}, s32[8]{0:T(128)}, u32[]{:S(2)}) copy-start(s32[8]{0:T(128)} %dest_ref.1) | copy-start | bytes 100
  8.7 0.7 %copy-start.4 = (bf16[8,6]{1,0:T(8,128)(2,1)S(1)}, bf16[8,6]{1,0:T(8,128)(2,1)}, u32[]{:S(2)}) copy-start(bf16[8,6]{1,0:T(8,128)(2,1)} %kt_ref.1) | copy-start | bytes 292
  8.7 0.7 %copy-start.2 = (bf16[32,16]{0,1:T(8,128)(2,1)S(1)}, bf16[32,16]{0,1:T(8,128)(2,1)}, u32[]{:S(2)}) copy-start(bf16[32,16]{0,1:T(8,128)(2,1)} %param.21) | copy-start | bytes 3076
  8.7 0.7 %copy-start.3 = (bf16[6,32]{1,0:T(8,128)(2,1)S(1)}, bf16[6,32]{1,0:T(8,128)(2,1)}, u32[]{:S(2)}) copy-start(bf16[6,32]{1,0:T(8,128)(2,1)} %wt_ref.1) | copy-start | bytes 1156
  8.8 0.7 %copy-start.5 = (bf16[3,32]{1,0:T(4,128)(2,1)S(1)}, bf16[3,32]{1,0:T(4,128)(2,1)}, u32[]{:S(2)}) copy-start(bf16[3,32]{1,0:T(4,128)(2,1)} %wf_ref.1) | copy-start | bytes 580

commit v6 on v5

--- a/solution.py
+++ b/solution.py
@@ -14,10 +14,11 @@
 TN = (((0,), (0,)), ((), ()))
 
 BLOCK = 144
+TALL = 160
 CELLS = 512
 TAPS = 144
 ROWS = 128
-SENT = 24
+SENT = 16
 ROUTED = 32
 
 
@@ -80,12 +81,12 @@
     for ky in range(3):
         for s, kx in enumerate((1, 2, 0)):
             for zo, kz in enumerate((1, 2, 0)):
-                to, at = ky * 144 + s * 48 + zo * 16, ((kz * 3 + ky) * 3 + kx) * 16
+                to, at = ky * TALL + s * 48 + zo * 16, ((kz * 3 + ky) * 3 + kx) * 16
                 order[to : to + 16, 0:32] = w2[at : at + 16]
-    order[432:448, 0:32] = ws_ref[...].astype(F32)
+    order[304:320, 0:32] = ws_ref[...].astype(F32)
     w2t = order[...]
     w2a_ref[...] = jnp.transpose(w2t)[0:32].astype(BF16)
-    wsb_ref[...] = w2t[432:448].astype(BF16)
+    wsb_ref[...] = w2t[304:320].astype(BF16)
     own, near = ((1, 0),), ((2, 0), (0, 1))
     for sub in range(2):
         for px in range(2):
@@ -94,7 +95,7 @@
                 for ky, sy in near if sub else own:
                     for kx, sx in near if px else own:
                         for kz, sz in near if z else own:
-                            at = ky * 144 + (1, 2, 0).index(kx) * 48 + (1, 2, 0).index(kz) * 16
+                            at = ky * TALL + (1, 2, 0).index(kx) * 48 + (1, 2, 0).index(kz) * 16
                             to = sz * 64 + sx * 32
                             part = w2t[at : at + 16]
                             sides[sy] = sides[sy] + (pltpu.roll(part, to, 1) if to else part)
@@ -184,26 +185,25 @@
     zero = jnp.zeros((), BF16)
     first_z = lanes((16, CELLS)) < 64
     first_x = lanes((48, CELLS)) % 64 == 0
-    a_ref[0:BLOCK] = jnp.zeros((BLOCK, CELLS), BF16)
+    a_ref[0:TALL] = jnp.zeros((TALL, CELLS), BF16)
     z1_all = mxu(t1_ref[...], xcol[0:128])
     for y in range(8):
         z1 = z1_all[y * 64 : y * 64 + 64] + b1
         act = jnp.maximum(z1, 0.0).astype(BF16)
-        at = (y + 1) * BLOCK
+        at = (y + 1) * TALL
         for px in range(2):
             moved = pltpu.roll(act[px * 32 + 16 : px * 32 + 32], 64, 1)
             moved = jnp.where(first_z, zero, moved)
             a_ref[at + px * 48 : at + px * 48 + 32] = act[px * 32 : px * 32 + 32]
             a_ref[at + px * 48 + 32 : at + px * 48 + 48] = moved
+        a_ref[at + BLOCK : at + TALL] = act[0:16]
         late = jnp.concatenate([act[32:64], moved], axis=0)
         a_ref[at + 96 : at + BLOCK] = jnp.where(first_x, zero, pltpu.roll(late, 1, 1))
     b2 = cols_ref[0:32, 1:2]
     pooled = jnp.zeros((32, 1), F32)
     for y in range(4):
-        at = 2 * y * BLOCK
-        z2 = mxu(w2a_ref[:, 0:432], a_ref[at : at + 432])
-        short = mxu(w2a_ref[:, 432:448], a_ref[at + BLOCK : at + BLOCK + 16])
-        z2 = (z2 + b2) + short
+        at = 2 * y * TALL
+        z2 = mxu(w2a_ref[:, 0:480], a_ref[at : at + 480]) + b2
         act = jnp.maximum(z2, 0.0).astype(BF16)
         a2_ref[y * 32 : y * 32 + 32] = act
         pooled = pooled + jnp.sum(act.astype(F32), axis=1, keepdims=True)
@@ -249,11 +249,11 @@
         here = wtt_ref[36 + t : 37 + t] > 0
         for k in range(6):
             both = jnp.where(left, shares[2 * k], shares[2 * k + 1])
-            sent[t * 8 : t * 8 + 8, 16 + k, :] = jnp.where(here, both, 0.0)
-        sent[t * 8 : t * 8 + 8, 22, :] = jnp.where(
+            sent[t * 8 : t * 8 + 8, 8 + k, :] = jnp.where(here, both, 0.0)
+        sent[t * 8 : t * 8 + 8, 14, :] = jnp.where(
             here, last, jnp.where(lane8 == 6, -1.0, 0.0)
         )
-        sent[t * 8 : t * 8 + 8, 23, :] = jnp.zeros((8, 128), F32)
+        sent[t * 8 : t * 8 + 8, 15, :] = jnp.zeros((8, 128), F32)
     last_x = lanes((32, CELLS)) % 64 == 63
     last_z = lanes((32, CELLS)) >= 448
     bias2 = jnp.zeros((32, 1), F32)
@@ -275,12 +275,12 @@
     none = jnp.zeros((32, CELLS), BF16)
     second = jnp.zeros((BLOCK, 128), F32)
     for y in range(4):
-        at = (2 * y + 1) * BLOCK
+        at = (2 * y + 1) * TALL
         da1 = mxu(wb_ref[...], d_ref[y * 128 : y * 128 + 256])
         short = mxu(wsb_ref[:, 0:32], dz2[y])
         da1 = jnp.concatenate([da1[0:16] + short, da1[16:128]], axis=0)
         for sub in range(2):
-            act = a_ref[at + sub * BLOCK : at + sub * BLOCK + BLOCK]
+            act = a_ref[at + sub * TALL : at + sub * TALL + BLOCK]
             if sub == 0:
                 sides = [none, dz2[y], none, none]
             else:
@@ -332,7 +332,7 @@
     for ky in range(3):
         tail_block = pltpu.roll(second[128:144], (96 - ky * 32) % 128, 1)
         extra[ky * 16 : ky * 16 + 16] = tail_block
-    lane8 = lanes((8, 128))
+    lane8, row8 = lanes((8, 128)), rows((8, 128))
     for i in range(5):
         pair = jnp.zeros((8, 128), F32)
         for h in range(2 if i < 4 else 1):
@@ -353,6 +353,7 @@
     extra[68:74] = pltpu.roll(upright[0:8], 64, 1)[1:7]
     extra[74:80] = jnp.zeros((6, 128), F32)
     rest = lane8 >= 96
+    remainder = ((row8 == 5) | (row8 == 6)) & rest
     swap = lax.axis_index("yh") * 8
     for t in range(16):
         block = second[t * 8 : t * 8 + 8]
@@ -364,22 +365,24 @@
         block = total[t * 8 : t * 8 + 8]
         high = block.astype(BF16).astype(F32)
         to = lax.rem(t + swap, 16)
-        sent[to, 0:8, :] = high
-        sent[to, 8:16, :] = block - high
+        sent[to, 0:8, :] = jnp.where(remainder, pltpu.roll(block - high, 2, 0), high)
     out_ref[...] = sent[...].astype(BF16)
 
 
 def route(got_ref, out_ref, recs):
     recs[...] = got_ref[...].astype(F32)
     count = got_ref.shape[0]
-    full = recs[0, 0:8, :] + recs[0, 8:16, :]
+    full = recs[0, 0:8, :]
     for p in range(1, count):
-        full = full + (recs[p, 0:8, :] + recs[p, 8:16, :])
+        full = full + recs[p, 0:8, :]
+    row8, lane8 = rows((8, 128)), lanes((8, 128))
+    split = ((row8 == 3) | (row8 == 4)) & (lane8 >= 96)
+    full = full + jnp.where(split, pltpu.roll(full, 6, 0), 0.0)
     high = full.astype(BF16).astype(F32)
     low = full - high
     peers = out_ref.shape[0]
     lane = lanes((count, 128))
-    last = recs[:, 22, :]
+    last = recs[:, 14, :]
     dest = jnp.sum(jnp.where(lane == 6, last, 0.0), axis=1, keepdims=True).astype(jnp.int32)
     rank = jnp.sum(jnp.where(lane == 7, last, 0.0), axis=1, keepdims=True).astype(jnp.int32)
     side = side_of(lax.axis_index("yh") * 2 + lax.axis_index("yl"))
@@ -390,7 +393,7 @@
     hit = jnp.where(right & (peer < peers), 1.0, 0.0)
     hit = jnp.concatenate([hit, jnp.zeros((128 - count, 128), F32)], axis=0)
     choose = jnp.transpose(hit)[0 : 4 * peers, 0:count].astype(BF16)
-    layers = [mxu(choose, recs[:, 16 + k, :].astype(BF16)) for k in range(6)]
+    layers = [mxu(choose, recs[:, 8 + k, :].astype(BF16)) for k in range(6)]
     marks = mxu(choose, last.astype(BF16))
     lane = lanes((4 * peers, 128))
     marks = jnp.where(lane == 6, pltpu.roll(marks, 126, 1), jnp.where(lane < 6, marks, 0.0))
@@ -539,7 +542,7 @@
         functools.partial(step, 2.0 / flux_count, 2.0 / tensor_count, float(cell_count)),
         "step", [], [record, *weights], [((near, SENT, 128), BF16)],
         [
-            ((9 * BLOCK, CELLS), BF16), ((128, CELLS), BF16), ((640, CELLS), BF16),
+            ((9 * TALL, CELLS), BF16), ((128, CELLS), BF16), ((640, CELLS), BF16),
             ((CELLS, CELLS), BF16), ((ROWS, 128), F32), ((112, 128), F32),
             ((near, SENT, 128), F32),
         ],

time: 57 us -> 56.9 us (level)
  no operation moved by 1% of the time
where the time goes in v6:
time: 56.9 us; the launch traced here: 56.5 us
  blocking collectives  38.8 us (68%)
  starting transfers between devices  6.64 us (12%)
  Pallas kernels  5.15 us (9%)
  waiting for transfers between devices  3.03 us (5%)
  local copies, waits for them, and re-layouts  1.46 us (3%)
  between operations  0.77 us (1%)
  other arithmetic  0.64 us (1%)
    all_to_all x3, blocking collectives, exchange(): lax.all_to_all(block, axis, 0, 0, tiled=True, axis_index_groups=groups)  38.8 us
    all_to_all x1, starting transfers between devices, exchange(): lax.all_to_all(block, axis, 0, 0, tiled=True, axis_index_groups=groups)  6.64 us
    pallas_call x5, Pallas kernels, run(): pl.pallas_call(kernel, out_shape=tuple((jax.ShapeDtypeStruct(*o[0:2]) for...  5.15 us
    all_to_all x1, waiting for transfers between devices, exchange(): lax.all_to_all(block, axis, 0, 0, tiled=True, axis_index_groups=groups)  3.03 us
  transfers between devices with their start and end apart: 1, of which 1 were waited for; matrix products, arithmetic and copies ran while one was open for 0% of the time, Pallas kernels for 2%

profile of v6, /device:TPU:1, one launch (start us, length us, event | category | flops | bytes accessed | tf_op | source)
XLA Modules:
  0.0 56.5 jit_solution(148167394302384670)
XLA Ops:
  0.6 0.0 copy-start.11
  0.7 0.8 %pad.4 = bf16[8,4,4,128]{3,2,1,0:T(4,128)(2,1)S(1)} pad(bf16[8,3,4,64]{3,2,1,0:T(4,128)(2,1)} %bitcast.34, bf16[]{:T(256)} %constant.2.clone.1), padding=0_0x0_1x0_0x0_64 | pad | bytes 45058 | tf_op jit(solution)/shard_map/jit(_pad)/pad | solution.py:521
  1.4 0.0 copy-done.11
  1.4 0.0 copy-start
  1.4 0.6 %pad_maximum_fusion = bf16[8,4,8,128]{3,2,1,0:T(8,128)(2,1)} fusion(bf16[8,2,8,128]{3,2,1,0:T(8,128)(2,1)S(1)} %bitcast.33, bf16[8,2,8,128]{3,2,1,0:T(8,128)(2,1)S(1)} %copy-done.11), kind=kLoop, calls=%fused_computation | loop fusion | flops 32768 | bytes 131072 | tf_op jit(solution)/shard_map/concatenate | solution.py:522
  2.1 0.0 copy-start.7
  2.1 0.0 copy-start.8
  2.1 0.0 copy-start.9
  2.1 0.0 copy-start.10
  2.1 6.6 %all-to-all-start = ((bf16[8,4,8,128]{3,2,1,0:T(8,128)(2,1)}), bf16[8,4,8,128]{3,2,1,0:T(8,128)(2,1)S(1)}, u32[]{:S(2)}, u32[]{:S(2)}) async-start(bf16[8,4,8,128]{3,2,1,0:T(8,128)(2,1)} %pad_maximum_fusion), calls=%async_computation | async-start | bytes 131072 | tf_op jit(solution)/shard_map/all_to_all | solution.py:505
  8.7 0.0 copy-start.2
  8.7 0.0 copy-start.3
  8.8 0.0 copy-start.5
  8.8 0.0 copy-done
  8.8 0.0 copy-done.7
  8.8 0.0 copy-done.8
  8.8 0.0 copy-done.9
  8.8 0.0 copy-done.10
  8.8 0.6 %copy-done.1 = bf16[16,1,3,3,3]{0,4,3,2,1:T(4,128)(2,1)S(1)} copy-done((bf16[16,1,3,3,3]{0,4,3,2,1:T(4,128)(2,1)S(1)}, bf16[16,1,3,3,3]{0,4,3,2,1:T(4,128)(2,1)}, u32[]{:S(2)}) %copy-start.1) | copy-done | bytes 888
  9.4 0.0 copy-done.6
  9.4 0.0 copy-done.4
  9.4 0.0 copy-done.2
  9.5 0.0 copy-done.3
  9.5 0.0 copy-done.5
  9.5 1.1 %prepare.1 = (bf16[512,128]{1,0:T(8,128)(2,1)S(1)}, bf16[32,512]{1,0:T(8,128)(2,1)S(1)}, bf16[128,256]{1,0:T(8,128)(2,1)S(1)}, bf16[16,128]{1,0:T(8,128)(2,1)S(1...) custom-call(s32[1]{0:T(128)} %bitcast.2.place_ref, ...), custom_call_target="tpu_custom_call" | custom-call | tf_op jit(solution)/shard_map/prepare/pallas_call | solution.py:493
  10.6 3.0 %all-to-all-done.got_ref = bf16[8,4,8,128]{3,2,1,0:T(8,128)(2,1)S(1)} async-done(((bf16[8,4,8,128]{3,2,1,0:T(8,128)(2,1)}), bf16[8,4,8,128]{3,2,1,0:T(8,128)(2,1)S(1)}, u32[]{:S(2)}, u32[]{:S(2)}) %all-to-all-start) | async-done | bytes 65568 | tf_op jit(solution)/shard_map/all_to_all | solution.py:505
  13.6 2.4 %step.1 = bf16[16,16,128]{2,1,0:T(8,128)(2,1)S(1)} custom-call(bf16[8,4,8,128]{3,2,1,0:T(8,128)(2,1)S(1)} %all-to-all-done.got_ref, bf16[512,128]{1,0:T(8,128)(2,1)S(1)} %get-tuple-element.31.t1_ref, bf16[32,512]{1,0:T(8,128)(2,1)S(1)} %get-tuple-element.32.w2a_ref, bf16[128,256]{1,0:T(8,128)(2,1)S(1)} %get-tuple-element.33.wb_ref, ...), custom_call_target="tpu_custom_call" | custom-call | tf_op jit(solution)/shard_map/step/pallas_call | solution.py:493
  16.0 9.1 %all_to_all.20.got_ref = bf16[16,16,128]{2,1,0:T(8,128)(2,1)S(1)} all-to-all(bf16[16,16,128]{2,1,0:T(8,128)(2,1)S(1)} %step.1), channel_id=1, replica_groups=mesh['z'=8,'yh'=2,'yl'=2,'slab'=8] {'yl','slab'}, dimensions={0} | all-to-all | bytes 131072 | tf_op jit(solution)/shard_map/all_to_all | solution.py:505
  25.2 0.5 route.1
  25.7 19.3 %all_to_all.21.got_ref.routed_ref = bf16[16,32,128]{2,1,0:T(8,128)(2,1)S(1)} all-to-all(bf16[16,32,128]{2,1,0:T(8,128)(2,1)S(1)} %route.1), channel_id=1, replica_groups={{0,24,32,56,64,88,96,120,128,152,160,184,192,216,224,248},{8,16,40,48,7..., dimensions={0} | all-to-all | bytes 262144 | tf_op jit(solution)/shard_map/all_to_all | solution.py:505
  45.0 10.4 %all_to_all.22.got_ref = f32[16,8,128]{2,1,0:T(8,128)S(1)} all-to-all(f32[16,8,128]{2,1,0:T(8,128)S(1)} %spread.1), channel_id=1, replica_groups=mesh['z'=8,'yh'=2,'yl'=2,'slab'=8] {'yl','slab'}, dimensions={0} | all-to-all | bytes 131072 | tf_op jit(solution)/shard_map/all_to_all | solution.py:505
  55.4 1.1 %finish.1 = (bf16[8,3,4,64]{3,2,1,0:T(4,128)(2,1)}, bf16[8,6]{1,0:T(8,128)(2,1)}, f32[27,1,16]{2,1,0:T(1,128)}, f32[1,16]{1,0:T(1,128)}, f32[432,32]{1,0:T(8,128...) custom-call(f32[16,8,128]{2,1,0:T(8,128)S(1)} %all_to_all.22.got_ref, ...), custom_call_target="tpu_custom_call" | custom-call | tf_op jit(solution)/shard_map/finish/pallas_call | solution.py:493
  (4 shorter events, 0.0 us)
Async XLA Ops:
  0.6 0.8 %copy-start.11 = (bf16[8,2,8,128]{3,2,1,0:T(8,128)(2,1)S(1)}, bf16[8,2,8,128]{3,2,1,0:T(8,128)(2,1)}, u32[]{:S(2)}) copy-start(bf16[8,2,8,128]{3,2,1,0:T(8,128)(2,1)} %param.13) | copy-start | bytes 98308
  1.4 7.3 %copy-start = (bf16[32,16,3,3,3]{0,1,4,3,2:T(8,128)(2,1)S(1)}, bf16[32,16,3,3,3]{0,1,4,3,2:T(8,128)(2,1)}, u32[]{:S(2)}) copy-start(bf16[32,16,3,3,3]{0,1,4,3,2:T(8,128)(2,1)} %param.19) | copy-start | bytes 82948
  2.1 6.7 %copy-start.7 = (f32[3]{0:T(128)S(1)}, f32[3]{0:T(128)}, u32[]{:S(2)}) copy-start(f32[3]{0:T(128)} %bf_ref.1) | copy-start | bytes 40
  2.1 6.7 %copy-start.8 = (f32[16]{0:T(128)S(1)}, f32[16]{0:T(128)}, u32[]{:S(2)}) copy-start(f32[16]{0:T(128)} %param.18) | copy-start | bytes 196
  2.1 6.7 %copy-start.9 = (f32[32]{0:T(128)S(1)}, f32[32]{0:T(128)}, u32[]{:S(2)}) copy-start(f32[32]{0:T(128)} %param.20) | copy-start | bytes 388
  2.1 6.7 %copy-start.10 = (f32[6]{0:T(128)S(1)}, f32[6]{0:T(128)}, u32[]{:S(2)}) copy-start(f32[6]{0:T(128)} %param.25) | copy-start | bytes 76
  2.1 11.5 %all-to-all-start = ((bf16[8,4,8,128]{3,2,1,0:T(8,128)(2,1)}), bf16[8,4,8,128]{3,2,1,0:T(8,128)(2,1)S(1)}, u32[]{:S(2)}, u32[]{:S(2)}) async-start(bf16[8,4,8,128]{3,2,1,0:T(8,128)(2,1)} %pad_maximum_fusion), calls=%async_computation | async-start | bytes 131072 | tf_op jit(solution)/shard_map/all_to_all | solution.py:505
  8.7 0.7 %copy-start.1 = (bf16[16,1,3,3,3]{0,4,3,2,1:T(4,128)(2,1)S(1)}, bf16[16,1,3,3,3]{0,4,3,2,1:T(4,128)(2,1)}, u32[]{:S(2)}) copy-start(bf16[16,1,3,3,3]{0,4,3,2,1:T(4,128)(2,1)} %param.17) | copy-start | bytes 2596
  8.7 0.7 %copy-start.6 = (s32[8]{0:T(128)S(1)}, s32[8]{0:T(128)}, u32[]{:S(2)}) copy-start(s32[8]{0:T(128)} %dest_ref.1) | copy-start | bytes 100
  8.7 0.7 %copy-start.4 = (bf16[8,6]{1,0:T(8,128)(2,1)S(1)}, bf16[8,6]{1,0:T(8,128)(2,1)}, u32[]{:S(2)}) copy-start(bf16[8,6]{1,0:T(8,128)(2,1)} %kt_ref.1) | copy-start | bytes 292
  8.7 0.7 %copy-start.2 = (bf16[32,16]{0,1:T(8,128)(2,1)S(1)}, bf16[32,16]{0,1:T(8,128)(2,1)}, u32[]{:S(2)}) copy-start(bf16[32,16]{0,1:T(8,128)(2,1)} %param.21) | copy-start | bytes 3076
  8.7 0.7 %copy-start.3 = (bf16[6,32]{1,0:T(8,128)(2,1)S(1)}, bf16[6,32]{1,0:T(8,128)(2,1)}, u32[]{:S(2)}) copy-start(bf16[6,32]{1,0:T(8,128)(2,1)} %wt_ref.1) | copy-start | bytes 1156
  8.8 0.7 %copy-start.5 = (bf16[3,32]{1,0:T(4,128)(2,1)S(1)}, bf16[3,32]{1,0:T(4,128)(2,1)}, u32[]{:S(2)}) copy-start(bf16[3,32]{1,0:T(4,128)(2,1)} %wf_ref.1) | copy-start | bytes 580
